TPU v7x, 512 devices: a whole 4x4x16 slice. The times are simulated.
512 devices in a mesh: section: 8 (over y, z_hi), replica: 64 (over z_lo, x, core).
Axes of the slice: x: 4, y: 4, z: 16 (z_hi: 2, z_lo: 8; z = z_hi * 8 + z_lo), core: 2. Of those that a mesh axis runs over, the one named last changes fastest.
Arguments:
- embeds: bfloat16 [8192, 4096], P('replica'), may hold values from -16 to 16
- shared_basis: bfloat16 [4096, 256], replicated, as said below
- down_proj: bfloat16 [8, 4096, 64], P('section'), may hold values from -0.09375 to 0.09375
- up_proj: bfloat16 [8, 4096, 64], P('section'), may hold values from -0.75 to 0.75
- norm_gain: float32 [8, 4096], P('section'), may hold values from 0.1 to 1.9
- coef_grad: bfloat16 [8192, 256], P('replica'), may hold values from -0.15625 to 0.15625
Outputs:
- coefs: bfloat16 [8, 8192, 256], P('section', 'replica')
- weight_grads: float32 [8, 4096, 128], P('section', 'replica')
Inputs may be any that keep to these rules, and one draw needn't show every extreme that they name: The columns of shared_basis are orthonormal up to bfloat16 rounding.
All inputs are finite; a program needn't handle non-finite values.
Results may differ from a plain program's by a relative error of at most 0.014.
Values may be sent and summed in bfloat16 or wider, within the bound.
No kernel may reach another device: no remote copies, remote signals or barrier semaphores. Data moves between devices by JAX's collectives and lax.ppermute only.
A program may use at most 64 MiB of HBM per device.

v0:
```python
import jax
import jax.numpy as jnp
from jax import lax
from jax.sharding import PartitionSpec as P

MICRO = 4
ROWS = 32


eps_norm = 1e-05


def from_behind(value, axis, steps):
    count = lax.axis_size(axis)
    leading, last = (max(0, -steps), min(count, count - steps))
    return lax.ppermute(value, axis, [(source, source + steps) for source in range(leading, last)])


def section_forward(coef_in, embedded, basis, down_weight, up_weight, gain_row):
    expanded = jnp.einsum("nr,dr->nd", coef_in, basis, preferred_element_type=jnp.float32)
    hidden = embedded.astype(jnp.float32) + expanded
    inverse_rms = lax.rsqrt(jnp.mean(hidden * hidden, axis=-1, keepdims=True) + eps_norm)
    normed = (hidden * inverse_rms * gain_row).astype(jnp.bfloat16)
    preact = jnp.dot(normed, down_weight, preferred_element_type=jnp.float32)
    activation = jax.nn.silu(preact).astype(jnp.bfloat16)
    branch = jnp.einsum("nk,dk->nd", activation, up_weight, preferred_element_type=jnp.float32)
    delta_rows = (expanded + branch).astype(jnp.bfloat16)
    coef_out = jnp.dot(delta_rows, basis, preferred_element_type=jnp.float32).astype(jnp.bfloat16)
    return (coef_out, hidden, normed, preact, activation)


def section_backward(grad_out, hidden, preact, basis, down_weight, up_weight, gain_row):
    grad_delta = jnp.einsum(
        "nr,dr->nd", grad_out, basis, preferred_element_type=jnp.float32
    ).astype(jnp.bfloat16)
    grad_act = jnp.dot(grad_delta, up_weight, preferred_element_type=jnp.float32)
    sigmoid_pre = jax.nn.sigmoid(preact)
    grad_pre = (grad_act * sigmoid_pre * (1.0 + preact * (1.0 - sigmoid_pre))).astype(jnp.bfloat16)
    grad_normed = jnp.einsum("nk,dk->nd", grad_pre, down_weight, preferred_element_type=jnp.float32)
    inverse_rms = lax.rsqrt(jnp.mean(hidden * hidden, axis=-1, keepdims=True) + eps_norm)
    scaled_rows = hidden * inverse_rms
    grad_scaled = grad_normed * gain_row
    grad_hidden = inverse_rms * (
        grad_scaled - scaled_rows * jnp.mean(grad_scaled * scaled_rows, axis=-1, keepdims=True)
    )
    grad_base = (grad_delta.astype(jnp.float32) + grad_hidden).astype(jnp.bfloat16)
    grad_in = jnp.dot(grad_base, basis, preferred_element_type=jnp.float32).astype(jnp.bfloat16)
    return (grad_in, grad_delta, grad_pre)


def local(embeds, shared_basis, down_proj, up_proj, norm_gain, coef_grad):
    section_count = lax.axis_size("section")
    section_index = lax.axis_index("section")
    down_weight = down_proj[0]
    up_weight = up_proj[0]
    gain_row = norm_gain[0]
    width_r = shared_basis.shape[1]
    width_k = down_weight.shape[1]
    width_d = embeds.shape[1]
    token_rows = embeds.shape[0]
    tick_count = MICRO + section_count - 1
    store_rows = (MICRO + 1) * ROWS

    def forward_tick(state_tuple, tick_index):
        incoming, coef_store, hidden_store, normed_store, preact_store, activ_store = state_tuple
        micro_index = tick_index - section_index
        is_valid = (micro_index >= 0) & (micro_index < MICRO)
        place_row = jnp.where(is_valid, micro_index, MICRO) * ROWS
        first_row = jnp.clip(micro_index, 0, MICRO - 1) * ROWS
        embedded = lax.dynamic_slice_in_dim(embeds, first_row, ROWS, 0)
        coef_out, hidden, normed, preact, activation = section_forward(
            incoming, embedded, shared_basis, down_weight, up_weight, gain_row
        )
        coef_store = lax.dynamic_update_slice_in_dim(coef_store, coef_out, place_row, 0)
        hidden_store = lax.dynamic_update_slice_in_dim(hidden_store, hidden, place_row, 0)
        normed_store = lax.dynamic_update_slice_in_dim(normed_store, normed, place_row, 0)
        preact_store = lax.dynamic_update_slice_in_dim(preact_store, preact, place_row, 0)
        activ_store = lax.dynamic_update_slice_in_dim(activ_store, activation, place_row, 0)
        sent = from_behind(coef_out, "section", 1)
        return ((sent, coef_store, hidden_store, normed_store, preact_store, activ_store), None)

    forward_init = (
        jnp.zeros((ROWS, width_r), jnp.bfloat16),
        jnp.zeros((store_rows, width_r), jnp.bfloat16),
        jnp.zeros((store_rows, width_d), jnp.float32),
        jnp.zeros((store_rows, width_d), jnp.bfloat16),
        jnp.zeros((store_rows, width_k), jnp.float32),
        jnp.zeros((store_rows, width_k), jnp.bfloat16),
    )
    forward_state, _ = lax.scan(forward_tick, forward_init, jnp.arange(tick_count, dtype=jnp.int32))
    coef_store, hidden_store, normed_store, preact_store, activ_store = forward_state[1:]

    def backward_tick(state_tuple, tick_index):
        incoming, delta_store, gradpre_store = state_tuple
        micro_index = tick_index - (section_count - 1 - section_index)
        is_valid = (micro_index >= 0) & (micro_index < MICRO)
        place_row = jnp.where(is_valid, micro_index, MICRO) * ROWS
        first_row = jnp.clip(micro_index, 0, MICRO - 1) * ROWS
        cotangent_rows = lax.dynamic_slice_in_dim(coef_grad, first_row, ROWS, 0)
        grad_out = jnp.where(section_index == section_count - 1, cotangent_rows, incoming)
        hidden = lax.dynamic_slice_in_dim(hidden_store, first_row, ROWS, 0)
        preact = lax.dynamic_slice_in_dim(preact_store, first_row, ROWS, 0)
        grad_in, grad_delta, grad_pre = section_backward(
            grad_out, hidden, preact, shared_basis, down_weight, up_weight, gain_row
        )
        delta_store = lax.dynamic_update_slice_in_dim(delta_store, grad_delta, place_row, 0)
        gradpre_store = lax.dynamic_update_slice_in_dim(gradpre_store, grad_pre, place_row, 0)
        sent = from_behind(grad_in, "section", -1)
        return ((sent, delta_store, gradpre_store), None)

    backward_init = (
        jnp.zeros((ROWS, width_r), jnp.bfloat16),
        jnp.zeros((store_rows, width_d), jnp.bfloat16),
        jnp.zeros((store_rows, width_k), jnp.bfloat16),
    )
    backward_state, _ = lax.scan(
        backward_tick, backward_init, jnp.arange(tick_count, dtype=jnp.int32)
    )
    delta_all = backward_state[1][:token_rows]
    gradpre_all = backward_state[2][:token_rows]
    normed_all = normed_store[:token_rows]
    activ_all = activ_store[:token_rows]
    shard_rows = width_d // lax.axis_size("replica")
    summed_all = lax.psum(
        jnp.concatenate(
            [
                jnp.einsum(
                    "nd,nk->dk", normed_all, gradpre_all, preferred_element_type=jnp.float32
                ),
                jnp.einsum("nd,nk->dk", delta_all, activ_all, preferred_element_type=jnp.float32),
            ],
            axis=1,
        ),
        "replica",
    )
    grad_shard = lax.dynamic_slice_in_dim(
        summed_all, lax.axis_index("replica") * shard_rows, shard_rows, 0
    )
    return (coef_store[:token_rows].reshape(1, token_rows, width_r), grad_shard[None])


def solution(mesh):
    placed = (
        P("replica", None),
        P(),
        P("section", None, None),
        P("section", None, None),
        P("section", None),
        P("replica", None),
    )
    return jax.shard_map(
        local,
        mesh=mesh,
        in_specs=placed,
        out_specs=(P("section", "replica", None), P("section", "replica", None)),
        check_vma=False,
    )
```

profile of v0, /device:TPU:1, one launch (start us, length us, event | category | flops | bytes accessed | tf_op | source)
XLA Modules:
  0.0 1379.3 jit_solution(415344805559804332)
XLA Ops:
  8.7 2.4 copy.11
  14.2 247.2 %while.36 = (s32[]{:T(128)}, bf16[32,256]{1,0:T(8,128)(2,1)S(1)}, bf16[160,256]{1,0:T(8,128)(2,1)S(1)}, f32[160,4096]{1,0:T(8,128)}, bf16[160,4096]{1,0:T(8,128)...) while((s32[]{:T(128)}, bf16[32,256]{1,0:T(8,128)(2,1)S(1)}, ...), condition=%wide.region_2.3_spmd, body=%wide.region_0.2_spmd.sunk | while | flops 169242672 | bytes 11477963 | solution.py:90
  15.5 2.6 fusion.50
  23.1 16.3 %collective-permute-start = (bf16[32,256]{1,0:T(8,128)(2,1)S(1)}, bf16[32,256]{1,0:T(8,128)(2,1)S(1)}, u32[]{:S(2)}, u32[]{:S(2)}) collective-permute-start(bf16[32,256]{1,0:T(8,128)(2,1)S(1)} %get-tuple-element.486), channel_id=1, source_target_pairs={{0,64},{64,128},{128,192},{192,256},{256,320},{320,384},{384,448},... | collective-permute-start | bytes 49160 | tf_op jit(solution)/shard_map/while/body/eval_jaxpr/ppermute | solution.py:16
  41.5 2.6 fusion.50
  49.1 12.7 collective-permute-start
  64.0 2.6 fusion.50
  71.6 12.3 collective-permute-start
  86.1 2.6 fusion.50
  93.7 12.4 collective-permute-start
  108.2 2.6 fusion.50
  115.8 12.3 collective-permute-start
  130.3 2.6 fusion.50
  137.9 12.3 collective-permute-start
  152.4 2.6 fusion.50
  160.0 12.3 collective-permute-start
  174.5 2.6 fusion.50
  182.0 12.3 collective-permute-start
  196.5 2.6 fusion.50
  204.1 12.3 collective-permute-start
  218.6 2.6 fusion.50
  226.2 12.3 collective-permute-start
  240.7 2.6 fusion.50
  248.3 12.3 collective-permute-start
  262.7 245.0 %while.37 = (s32[]{:T(128)}, bf16[32,256]{1,0:T(8,128)(2,1)S(1)}, bf16[160,4096]{1,0:T(8,128)(2,1)}, bf16[160,64]{1,0:T(8,128)(2,1)S(1)}, pred[]{:T(512)}, /*ind...) while((s32[]{:T(128)}, bf16[32,256]{1,0:T(8,128)(2,1)S(1)}, ...), condition=%wide.region_6.7_spmd, body=%wide.region_3.6_spmd.sunk | while | flops 169642032 | bytes 11704420 | solution.py:116
  265.2 2.2 constant_dynamic-update-slice_fusion.16
  272.2 12.2 collective-permute-done.1
  286.8 2.2 constant_dynamic-update-slice_fusion.16
  293.8 12.8 collective-permute-done.1
  309.1 2.2 constant_dynamic-update-slice_fusion.16
  316.1 12.8 collective-permute-done.1
  331.3 2.2 constant_dynamic-update-slice_fusion.16
  338.3 12.8 collective-permute-done.1
  353.6 2.2 constant_dynamic-update-slice_fusion.16
  360.6 12.8 collective-permute-done.1
  375.9 2.2 constant_dynamic-update-slice_fusion.16
  382.9 12.8 collective-permute-done.1
  398.2 2.2 constant_dynamic-update-slice_fusion.16
  405.2 12.9 collective-permute-done.1
  420.6 2.2 constant_dynamic-update-slice_fusion.16
  427.6 12.8 collective-permute-done.1
  442.9 2.2 constant_dynamic-update-slice_fusion.16
  449.9 12.8 collective-permute-done.1
  465.2 2.2 constant_dynamic-update-slice_fusion.16
  472.2 12.9 collective-permute-done.1
  487.5 2.3 constant_dynamic-update-slice_fusion.16
  494.6 13.1 collective-permute-done.1
  511.9 858.9 %all-reduce.2.cloned.1.call-done = f32[4096,128]{0,1:T(8,128)} async-done(((f32[4096,128]{0,1:T(8,128)}), f32[4096,128]{0,1:T(8,128)}) %all-reduce.2.cloned.1.call-update) | async-done | bytes 2097168 | tf_op jit(solution)/shard_map/psum | solution.py:124
  (235 shorter events, 154.4 us)
Async XLA Ops:
  7.2 1363.6 %all-reduce.2.cloned.1.call-start = ((), (), s32[]{:S(2)}) async-start(), calls=%async_computation | async-start | bytes 4194304 | tf_op jit(solution)/shard_map/psum | solution.py:124
  11.1 3.1 copy-start
  11.1 3.1 copy-start.4
  18.1 0.8 copy-start.2
  23.1 17.1 %collective-permute-start = (bf16[32,256]{1,0:T(8,128)(2,1)S(1)}, bf16[32,256]{1,0:T(8,128)(2,1)S(1)}, u32[]{:S(2)}, u32[]{:S(2)}) collective-permute-start(bf16[32,256]{1,0:T(8,128)(2,1)S(1)} %get-tuple-element.486), channel_id=1, source_target_pairs={{0,64},{64,128},{128,192},{192,256},{256,320},{320,384},{384,448},... | collective-permute-start | bytes 49160 | tf_op jit(solution)/shard_map/while/body/eval_jaxpr/ppermute | solution.py:16
  44.1 0.8 copy-start.2
  49.1 13.6 collective-permute-start
  66.7 0.8 copy-start.2
  71.6 13.2 collective-permute-start
  88.7 0.8 copy-start.2
  93.7 13.2 collective-permute-start
  110.8 0.8 copy-start.2
  115.8 13.2 collective-permute-start
  132.9 0.8 copy-start.2
  137.9 13.2 collective-permute-start
  155.0 0.8 copy-start.2
  160.0 13.2 collective-permute-start
  177.1 0.8 copy-start.2
  182.0 13.2 collective-permute-start
  199.1 0.8 copy-start.2
  204.1 13.2 collective-permute-start
  221.2 0.8 copy-start.2
  226.2 13.2 collective-permute-start
  243.3 0.8 copy-start.2
  248.3 13.2 collective-permute-start
  265.1 2.2 copy-start.1
  270.9 13.5 collective-permute-start.1
  286.8 2.2 copy-start.1
  292.5 14.1 %collective-permute-start.1 = (bf16[32,256]{1,0:T(8,128)(2,1)S(1)}, bf16[32,256]{1,0:T(8,128)(2,1)S(1)}, u32[]{:S(2)}, u32[]{:S(2)}) collective-permute-start(bf16[32,256]{1,0:T(8,128)(2,1)S(1)} %convolution_convert_fusion.3), channel_id=1, source_target_pairs={{64,0},{128,64},{192,128},{256,192},{320,256},{384,320},{448,384},... | collective-permute-start | bytes 49160 | tf_op jit(solution)/shard_map/while/body/eval_jaxpr/ppermute | solution.py:16
  309.1 2.2 copy-start.1
  314.8 14.1 %collective-permute-start.1 = (bf16[32,256]{1,0:T(8,128)(2,1)S(1)}, bf16[32,256]{1,0:T(8,128)(2,1)S(1)}, u32[]{:S(2)}, u32[]{:S(2)}) collective-permute-start(bf16[32,256]{1,0:T(8,128)(2,1)S(1)} %convolution_convert_fusion.3), channel_id=1, source_target_pairs={{64,0},{128,64},{192,128},{256,192},{320,256},{384,320},{448,384},... | collective-permute-start | bytes 49160 | tf_op jit(solution)/shard_map/while/body/eval_jaxpr/ppermute | solution.py:16
  331.3 2.2 copy-start.1
  337.0 14.1 %collective-permute-start.1 = (bf16[32,256]{1,0:T(8,128)(2,1)S(1)}, bf16[32,256]{1,0:T(8,128)(2,1)S(1)}, u32[]{:S(2)}, u32[]{:S(2)}) collective-permute-start(bf16[32,256]{1,0:T(8,128)(2,1)S(1)} %convolution_convert_fusion.3), channel_id=1, source_target_pairs={{64,0},{128,64},{192,128},{256,192},{320,256},{384,320},{448,384},... | collective-permute-start | bytes 49160 | tf_op jit(solution)/shard_map/while/body/eval_jaxpr/ppermute | solution.py:16
  353.6 2.2 copy-start.1
  359.3 14.1 %collective-permute-start.1 = (bf16[32,256]{1,0:T(8,128)(2,1)S(1)}, bf16[32,256]{1,0:T(8,128)(2,1)S(1)}, u32[]{:S(2)}, u32[]{:S(2)}) collective-permute-start(bf16[32,256]{1,0:T(8,128)(2,1)S(1)} %convolution_convert_fusion.3), channel_id=1, source_target_pairs={{64,0},{128,64},{192,128},{256,192},{320,256},{384,320},{448,384},... | collective-permute-start | bytes 49160 | tf_op jit(solution)/shard_map/while/body/eval_jaxpr/ppermute | solution.py:16
  375.9 2.2 copy-start.1
  381.6 14.1 %collective-permute-start.1 = (bf16[32,256]{1,0:T(8,128)(2,1)S(1)}, bf16[32,256]{1,0:T(8,128)(2,1)S(1)}, u32[]{:S(2)}, u32[]{:S(2)}) collective-permute-start(bf16[32,256]{1,0:T(8,128)(2,1)S(1)} %convolution_convert_fusion.3), channel_id=1, source_target_pairs={{64,0},{128,64},{192,128},{256,192},{320,256},{384,320},{448,384},... | collective-permute-start | bytes 49160 | tf_op jit(solution)/shard_map/while/body/eval_jaxpr/ppermute | solution.py:16
  398.2 2.2 copy-start.1
  403.9 14.2 %collective-permute-start.1 = (bf16[32,256]{1,0:T(8,128)(2,1)S(1)}, bf16[32,256]{1,0:T(8,128)(2,1)S(1)}, u32[]{:S(2)}, u32[]{:S(2)}) collective-permute-start(bf16[32,256]{1,0:T(8,128)(2,1)S(1)} %convolution_convert_fusion.3), channel_id=1, source_target_pairs={{64,0},{128,64},{192,128},{256,192},{320,256},{384,320},{448,384},... | collective-permute-start | bytes 49160 | tf_op jit(solution)/shard_map/while/body/eval_jaxpr/ppermute | solution.py:16
  420.6 2.2 copy-start.1
  426.3 14.1 %collective-permute-start.1 = (bf16[32,256]{1,0:T(8,128)(2,1)S(1)}, bf16[32,256]{1,0:T(8,128)(2,1)S(1)}, u32[]{:S(2)}, u32[]{:S(2)}) collective-permute-start(bf16[32,256]{1,0:T(8,128)(2,1)S(1)} %convolution_convert_fusion.3), channel_id=1, source_target_pairs={{64,0},{128,64},{192,128},{256,192},{320,256},{384,320},{448,384},... | collective-permute-start | bytes 49160 | tf_op jit(solution)/shard_map/while/body/eval_jaxpr/ppermute | solution.py:16
  442.9 2.2 copy-start.1
  448.6 14.1 %collective-permute-start.1 = (bf16[32,256]{1,0:T(8,128)(2,1)S(1)}, bf16[32,256]{1,0:T(8,128)(2,1)S(1)}, u32[]{:S(2)}, u32[]{:S(2)}) collective-permute-start(bf16[32,256]{1,0:T(8,128)(2,1)S(1)} %convolution_convert_fusion.3), channel_id=1, source_target_pairs={{64,0},{128,64},{192,128},{256,192},{320,256},{384,320},{448,384},... | collective-permute-start | bytes 49160 | tf_op jit(solution)/shard_map/while/body/eval_jaxpr/ppermute | solution.py:16
  465.2 2.3 copy-start.1
  470.9 14.2 %collective-permute-start.1 = (bf16[32,256]{1,0:T(8,128)(2,1)S(1)}, bf16[32,256]{1,0:T(8,128)(2,1)S(1)}, u32[]{:S(2)}, u32[]{:S(2)}) collective-permute-start(bf16[32,256]{1,0:T(8,128)(2,1)S(1)} %convolution_convert_fusion.3), channel_id=1, source_target_pairs={{64,0},{128,64},{192,128},{256,192},{320,256},{384,320},{448,384},... | collective-permute-start | bytes 49160 | tf_op jit(solution)/shard_map/while/body/eval_jaxpr/ppermute | solution.py:16
  487.5 2.3 copy-start.1
  493.3 14.4 %collective-permute-start.1 = (bf16[32,256]{1,0:T(8,128)(2,1)S(1)}, bf16[32,256]{1,0:T(8,128)(2,1)S(1)}, u32[]{:S(2)}, u32[]{:S(2)}) collective-permute-start(bf16[32,256]{1,0:T(8,128)(2,1)S(1)} %convolution_convert_fusion.3), channel_id=1, source_target_pairs={{64,0},{128,64},{192,128},{256,192},{320,256},{384,320},{448,384},... | collective-permute-start | bytes 49160 | tf_op jit(solution)/shard_map/while/body/eval_jaxpr/ppermute | solution.py:16
  507.7 1.7 copy-start.3
Sparse Core Ops, SparseCore 0:
  511.3 859.4 all-reduce.1
where the time goes:
time: 1380 us
  waiting for transfers between devices  1010 us (73%)
  starting transfers between devices  154 us (11%)
  matrix products  120 us (9%)
  other arithmetic  34.4 us (2%)
  local copies, waits for them, and re-layouts  32.6 us (2%)
  loops' own time  15.6 us (1%)
  between operations  14.1 us (1%)
    psum x1, waiting for transfers between devices, local(): lax.psum(jnp.concatenate([jnp.einsum('nd,nk->dk', normed_all, gradpre_all...  859 us
    ppermute x22, starting transfers between devices, from_behind(): lax.ppermute(value, axis, [(source, source + steps) for source in range(l...  154 us
    ppermute x22, waiting for transfers between devices, from_behind(): lax.ppermute(value, axis, [(source, source + steps) for source in range(l...  150 us
    dot_general x11, matrix products, section_forward(): jnp.einsum('nr,dr->nd', coef_in, basis, preferred_element_type=jnp.float32)  28.5 us
  transfers between devices with their start and end apart: 23, of which 23 were waited for; matrix products, arithmetic and copies ran while one was open for 0% of the time, Pallas kernels for 0%

commit v1 on v0

v1 whole, which is shorter than its diff:
```python
import functools

import jax
import jax.numpy as jnp
from jax import lax
from jax.experimental import pallas as pl
from jax.experimental.pallas import tpu as pltpu
from jax.sharding import Mesh, PartitionSpec as P

F32 = jnp.float32
BF16 = jnp.bfloat16
EPS = 1e-05
SECTION = ("y", "z_hi")
REPLICA = ("z_lo", "x", "core")
AXES = SECTION + REPLICA
SIZES = (4, 2, 8, 4, 2)

NN = (((1,), (0,)), ((), ()))
NT = (((1,), (1,)), ((), ()))
TN = (((0,), (0,)), ((), ()))


def dot(a, b, dims=NN):
    return lax.dot_general(a, b, dims, preferred_element_type=F32)


def project_kernel(steps, emb, basis, down, up, gain, block, emb_basis, norm, acc, acc_pre):
    step = pl.program_id(0)
    e = emb[...]
    down_t = (down[...].astype(F32).T * gain[...]).astype(BF16)
    up_t = up[...].astype(F32).T.astype(BF16)
    stacked = jnp.concatenate([e, down_t, up_t], axis=0)
    part = dot(stacked, basis[...])
    pre = dot(e, down_t, NT)
    ef = e.astype(F32)
    sq = ef * ef
    width = sq.shape[1]
    square = sq[:, :128]
    for at in range(128, width, 128):
        square = square + sq[:, at : at + 128]

    @pl.when(step == 0)
    def _():
        acc[...] = part
        acc_pre[...] = pre
        norm[...] = square

    @pl.when(step > 0)
    def _():
        acc[...] += part
        acc_pre[...] += pre
        norm[...] += square

    @pl.when(step == steps - 1)
    def _():
        rows = emb_basis.shape[0]
        emb_basis[...] = acc[:rows, :]
        block[:, :256] = acc[rows:, :].astype(BF16)
        total = acc_pre[...]
        high = total.astype(BF16)
        block[:, 256:320] = high
        block[:, 320:384] = (total - high.astype(F32)).astype(BF16)
        norm[...] = jnp.broadcast_to(jnp.sum(norm[...], axis=1, keepdims=True), norm.shape)


def project(embeds, basis, down, up, gain):
    rows, width = embeds.shape
    rank = basis.shape[1]
    inner = down.shape[1]
    steps = 8
    chunk = width // steps
    return pl.pallas_call(
        functools.partial(project_kernel, steps),
        grid=(steps,),
        in_specs=[
            pl.BlockSpec((rows, chunk), lambda i: (0, i)),
            pl.BlockSpec((chunk, rank), lambda i: (i, 0)),
            pl.BlockSpec((chunk, inner), lambda i: (i, 0)),
            pl.BlockSpec((chunk, inner), lambda i: (i, 0)),
            pl.BlockSpec((1, chunk), lambda i: (0, i)),
        ],
        out_specs=[
            pl.BlockSpec((2 * inner, rank + 2 * inner), lambda i: (0, 0)),
            pl.BlockSpec((rows, rank), lambda i: (0, 0)),
            pl.BlockSpec((rows, 128), lambda i: (0, 0)),
        ],
        out_shape=[
            jax.ShapeDtypeStruct((2 * inner, rank + 2 * inner), BF16),
            jax.ShapeDtypeStruct((rows, rank), F32),
            jax.ShapeDtypeStruct((rows, 128), F32),
        ],
        scratch_shapes=[
            pltpu.VMEM((rows + 2 * inner, rank), F32),
            pltpu.VMEM((rows, inner), F32),
        ],
        compiler_params=pltpu.CompilerParams(vmem_limit_bytes=32 * 1024 * 1024),
        name="project",
    )(embeds, basis, down, up, gain)


def chain_kernel(
    count, place, blocks, emb_basis, norm, cotangent, emb, basis, gain,
    coefs, slots, c_kept, g_kept, p_kept, a_kept, pre_kept, slope_kept, inv_kept, wide,
):
    width = emb.shape[1]
    inner = 64
    eu = emb_basis[...]
    sq = norm[:, :1]
    c = jnp.zeros(eu.shape, BF16)
    c_kept[0] = c
    for s in range(count):
        cf = c.astype(F32)
        pre = blocks[s, :, 256:320].astype(F32) + blocks[s, :, 320:384].astype(F32)
        total = sq
        if s:
            pre = pre + dot(c, blocks[s, :inner, :256], NT)
            total = total + jnp.sum(cf * (2.0 * eu + cf), axis=1, keepdims=True)
        inv = lax.rsqrt(jnp.maximum(total, 0.0) * (1.0 / width) + EPS)
        pre = pre * inv
        sig = 1.0 / (1.0 + jnp.exp(-pre))
        act = (pre * sig).astype(BF16)
        pre_kept[s] = pre
        slope_kept[s] = sig * (1.0 + pre * (1.0 - sig))
        inv_kept[s] = jnp.broadcast_to(inv, inv_kept.shape[1:])
        a_kept[s] = act
        c = (cf + dot(act, blocks[s, inner:, :256])).astype(BF16)
        c_kept[s + 1] = c

    g = cotangent[...]
    for s in reversed(range(count)):
        g_kept[s] = g
        inv = inv_kept[s][:, :1]
        gp = (dot(g, blocks[s, inner:, :256], NT) * slope_kept[s]).astype(BF16)
        gpf = gp.astype(F32)
        p_kept[s] = gpf * inv
        if s:
            mean = jnp.sum(gpf * pre_kept[s], axis=1, keepdims=True) * (1.0 / width)
            back = dot(gp, blocks[s, :inner, :256])
            hid = eu + c_kept[s].astype(F32)
            g = (g.astype(F32) + inv * back - (inv * inv * mean) * hid).astype(BF16)

    me = place[0]
    coefs[...] = c_kept[me + 1]
    p_t = p_kept[me].T.astype(BF16)
    cp = dot(p_t, c_kept[me]).astype(BF16)
    act_t = a_kept[me].astype(F32).T.astype(BF16)
    s2 = dot(act_t, g_kept[me]).astype(BF16)
    for at in range(0, width, 1024):
        cols = slice(at, at + 1024)
        grad = dot(p_t, emb[:, cols]) + dot(cp, basis[cols, :], NT)
        wide[:, cols] = grad * gain[:, cols]
    low = lax.broadcasted_iota(jnp.int32, (inner, 128), 1) < 64
    for x in range(4):
        for q in range(4):
            first = wide[:, ((2 * q) * 4 + x) * 128 : ((2 * q) * 4 + x) * 128 + 128]
            second = wide[:, ((2 * q + 1) * 4 + x) * 128 : ((2 * q + 1) * 4 + x) * 128 + 128]
            lanes = slice(q * 128, q * 128 + 128)
            slots[2 * x, :, lanes] = jnp.where(low, first, pltpu.roll(second, 64, 1)).astype(BF16)
            slots[2 * x + 1, :, lanes] = jnp.where(low, pltpu.roll(first, 64, 1), second).astype(BF16)
    for j in range(8):
        slots[j, :, 512:768] = s2


def chain(place, blocks, emb_basis, norm, cotangent, embeds, basis, gain):
    count = blocks.shape[0]
    rows, rank = cotangent.shape
    inner = 64
    width = embeds.shape[1]
    vmem = pl.BlockSpec(memory_space=pltpu.VMEM)
    return pl.pallas_call(
        functools.partial(chain_kernel, count),
        in_specs=[pl.BlockSpec(memory_space=pltpu.SMEM)] + [vmem] * 7,
        out_specs=[vmem, vmem],
        out_shape=[
            jax.ShapeDtypeStruct((rows, rank), BF16),
            jax.ShapeDtypeStruct((8, inner, 768), BF16),
        ],
        scratch_shapes=[
            pltpu.VMEM((count + 1, rows, rank), BF16),
            pltpu.VMEM((count, rows, rank), BF16),
            pltpu.VMEM((count, rows, inner), F32),
            pltpu.VMEM((count, rows, inner), BF16),
            pltpu.VMEM((count, rows, inner), F32),
            pltpu.VMEM((count, rows, inner), F32),
            pltpu.VMEM((count, rows, 128), F32),
            pltpu.VMEM((inner, width), F32),
        ],
        compiler_params=pltpu.CompilerParams(vmem_limit_bytes=32 * 1024 * 1024),
        name="chain",
    )(place, blocks, emb_basis, norm, cotangent, embeds, basis, gain)


def middle_kernel(place, got, basis, out):
    total = got[0].astype(F32)
    for j in range(1, got.shape[0]):
        total = total + got[j].astype(F32)
    rows = basis[:, 0].reshape(512, 256)
    w2 = dot(total[:, 512:].astype(BF16), rows, NT)
    both = jnp.concatenate([total[:, :512], w2], axis=0)
    out[...] = both.T.astype(BF16).reshape(out.shape)


def middle(place, got, basis):
    view = basis.reshape(8, 8, 64, 256)
    return pl.pallas_call(
        middle_kernel,
        grid_spec=pltpu.PrefetchScalarGridSpec(
            num_scalar_prefetch=1,
            grid=(1,),
            in_specs=[
                pl.BlockSpec((8, 64, 768), lambda i, place: (0, 0, 0)),
                pl.BlockSpec((8, 1, 64, 256), lambda i, place: (0, place[0], 0, 0)),
            ],
            out_specs=pl.BlockSpec((8, 64, 128), lambda i, place: (0, 0, 0)),
        ),
        out_shape=jax.ShapeDtypeStruct((8, 64, 128), BF16),
        compiler_params=pltpu.CompilerParams(vmem_limit_bytes=32 * 1024 * 1024),
        name="middle",
    )(place, got, view)


def final_kernel(got, out):
    total = got[0].astype(F32)
    for j in range(1, got.shape[0]):
        total = total + got[j].astype(F32)
    out[...] = total


def final(got):
    return pl.pallas_call(
        final_kernel,
        out_shape=jax.ShapeDtypeStruct(got.shape[1:], F32),
        name="final",
    )(got)


def gather_sections(block):
    other = lax.ppermute(block, "z_hi", [(0, 1), (1, 0)])
    mine = lax.axis_index("z_hi")
    pair = jnp.where(mine == 0, jnp.stack([block, other]), jnp.stack([other, block]))
    every = lax.all_gather(pair, "y", tiled=False)
    return every.reshape((8,) + block.shape)


def local(embeds, shared_basis, down_proj, up_proj, norm_gain, coef_grad):
    place = lax.axis_index(SECTION).astype(jnp.int32).reshape(1)
    lane = lax.axis_index(("x", "core")).astype(jnp.int32).reshape(1)
    block, emb_basis, norm = project(embeds, shared_basis, down_proj[0], up_proj[0], norm_gain)
    blocks = gather_sections(block)
    coefs, slots = chain(place, blocks, emb_basis, norm, coef_grad, embeds, shared_basis, norm_gain)
    got = lax.all_to_all(slots, ("x", "core"), 0, 0, tiled=True)
    summed = middle(lane, got, shared_basis)
    got = lax.all_to_all(summed, "z_lo", 0, 0, tiled=True)
    return coefs[None], final(got)[None]


def solution(mesh):
    fine = Mesh(mesh.devices.reshape(SIZES), AXES)
    placed = (
        P(REPLICA, None),
        P(),
        P(SECTION, None, None),
        P(SECTION, None, None),
        P(SECTION, None),
        P(REPLICA, None),
    )
    return jax.shard_map(
        local,
        mesh=fine,
        in_specs=placed,
        out_specs=(P(SECTION, REPLICA, None), P(SECTION, REPLICA, None)),
        check_vma=False,
    )
```

time: 1380 us -> 97.3 us (0.07)
  the two profiles are of different devices: /device:TPU:1 before, /device:TPU:8 now
where the time goes in v1:
time: 97.3 us; the launch traced here: 96.9 us
  blocking collectives  39.2 us (40%)
  starting transfers between devices  20 us (21%)
  waiting for transfers between devices  16.3 us (17%)
  Pallas kernels  10.6 us (11%)
  local copies, waits for them, and re-layouts  8.97 us (9%)
  other arithmetic  1 us (1%)
    all_to_all x1, blocking collectives, local(): got = lax.all_to_all(summed, 'z_lo', 0, 0, tiled=True)  24.9 us
    ppermute x1, starting transfers between devices, gather_sections(): other = lax.ppermute(block, 'z_hi', [(0, 1), (1, 0)])  15.7 us
    all_gather x1, blocking collectives, gather_sections(): every = lax.all_gather(pair, 'y', tiled=False)  14.3 us
    all_to_all x1, waiting for transfers between devices, local(): got = lax.all_to_all(slots, ('x', 'core'), 0, 0, tiled=True)  13.2 us
    unnamed x18, local copies, waits for them, and re-layouts  8.97 us
    pallas_call x1, Pallas kernels, chain(): pl.pallas_call(functools.partial(chain_kernel, count), in_specs=[pl.Block...  5.87 us
    all_to_all x1, starting transfers between devices, local(): got = lax.all_to_all(slots, ('x', 'core'), 0, 0, tiled=True)  4.3 us
    ppermute x1, waiting for transfers between devices, gather_sections(): other = lax.ppermute(block, 'z_hi', [(0, 1), (1, 0)])  3.17 us
  transfers between devices with their start and end apart: 2, of which 2 were waited for; matrix products, arithmetic and copies ran while one was open for 0% of the time, Pallas kernels for 0%

profile of v1, /device:TPU:8, one launch (start us, length us, event | category | flops | bytes accessed | tf_op | source)
XLA Modules:
  0.0 96.9 jit_solution(15061778478009559195)
XLA Ops:
  0.6 0.0 copy-start
  0.6 0.0 copy-start.1
  0.6 2.5 %copy.10 = bf16[1,4096,64]{2,1,0:T(8,128)(2,1)} copy(bf16[1,4096,64]{1,2,0:T(8,128)(2,1)} %param.8) | data formatting | bytes 1048576 | tf_op args[2]
  3.2 2.4 %copy.11 = bf16[1,4096,64]{2,1,0:T(8,128)(2,1)} copy(bf16[1,4096,64]{1,2,0:T(8,128)(2,1)} %param.9) | data formatting | bytes 1048576 | tf_op args[3]
  5.6 0.0 copy-done
  5.6 0.0 copy-done.1
  5.6 0.0 copy-start.2
  5.6 1.2 %copy-done.2 = bf16[1,4096,64]{2,1,0:T(8,128)(2,1)S(1)} copy-done((bf16[1,4096,64]{2,1,0:T(8,128)(2,1)S(1)}, bf16[1,4096,64]{2,1,0:T(8,128)(2,1)}, u32[]{:S(2)}) %copy-start.2) | copy-done | bytes 524312
  6.8 0.0 copy-start.3
  6.8 1.2 %copy-done.3 = bf16[1,4096,64]{2,1,0:T(8,128)(2,1)S(1)} copy-done((bf16[1,4096,64]{2,1,0:T(8,128)(2,1)S(1)}, bf16[1,4096,64]{2,1,0:T(8,128)(2,1)}, u32[]{:S(2)}) %copy-start.3) | copy-done | bytes 524312
  8.0 0.0 copy-start.6
  8.0 0.7 copy-done.6
  8.7 0.0 copy-start.5
  8.7 0.0 copy-start.7
  8.7 2.9 %project.1 = (bf16[128,384]{1,0:T(8,128)(2,1)S(1)}, f32[128,256]{1,0:T(8,128)S(1)}, f32[128,128]{1,0:T(8,128)S(1)}) custom-call(bf16[128,4096]{1,0:T(8,128)(2,1)S(1)} %copy-done.1, bf16[4096,256]{1,0:T(8,128)(2,1)S(1)} %copy-done, bf16[4096,64]{1,0:T(8,128)(2,1)S(1)} %bitcast.11, bf16[4096,64]{1,0:T(8,128)(2,1)S(1)} %bitcast.12, f32[1,4096]{1,0:T(1,128)S(1)} %copy-done.6), custom_call_target="tpu_custom_call" | custom-call | tf_op jit(solution)/shard_map/project/pallas_call | solution.py:72
  11.7 15.7 %collective-permute-start = (bf16[128,384]{1,0:T(8,128)(2,1)S(1)}, bf16[128,384]{1,0:T(8,128)(2,1)}, u32[]{:S(2)}, u32[]{:S(2)}) collective-permute-start(bf16[128,384]{1,0:T(8,128)(2,1)S(1)} %get-tuple-element.7), channel_id=1, source_target_pairs={{0,64},{64,0},{1,65},{65,1},{2,66},{66,2},{3,67},{67,3},{4,68},{68... | collective-permute-start | bytes 294920 | tf_op jit(solution)/shard_map/ppermute | solution.py:238
  27.4 3.2 %collective-permute-done = bf16[128,384]{1,0:T(8,128)(2,1)} collective-permute-done((bf16[128,384]{1,0:T(8,128)(2,1)S(1)}, bf16[128,384]{1,0:T(8,128)(2,1)}, u32[]{:S(2)}, u32[]{:S(2)}) %collective-permute-start) | collective-permute-done | bytes 98336 | tf_op jit(solution)/shard_map/ppermute | solution.py:238
  30.6 1.0 %maximum_select_fusion = bf16[1,2,128,384]{3,2,1,0:T(8,128)(2,1)S(1)} fusion(bf16[1,1,128,384]{3,2,1,0:T(8,128)(2,1)} %bitcast.4, bf16[1,1,128,384]{3,2,1,0:T(8,128)(2,1)S(1)} %bitcast.14, pred[]{:T(512)S(6)} %eq.3), kind=kLoop, calls=%fused_computation | loop fusion | flops 294912 | bytes 393217 | tf_op jit(solution)/shard_map/jit(_where)/select_n | solution.py:240
  31.6 14.3 %all_gather.4 = bf16[4,2,128,384]{3,2,1,0:T(8,128)(2,1)S(1)} all-gather(bf16[1,2,128,384]{3,2,1,0:T(8,128)(2,1)S(1)} %maximum_select_fusion), channel_id=1, replica_groups=mesh['y'=4,'z_hi'=2,'z_lo'=8,'x'=4,'core'=2] {'y'}, dimensions={0}, use_global_device_ids=true | all-gather | bytes 983040 | tf_op jit(solution)/shard_map/all_gather | solution.py:241
  45.9 0.0 copy-done.5
  45.9 0.0 copy-done.7
  45.9 5.9 %chain.1 = (bf16[128,256]{1,0:T(8,128)(2,1)}, bf16[8,64,768]{2,1,0:T(8,128)(2,1)S(1)}) custom-call(s32[1]{0:T(128)} %bitcast.place, bf16[8,128,384]{2,1,0:T(8,128)(2,1)S(1)} %bitcast.13, f32[128,256]{1,0:T(8,128)S(1)} %get-tuple-element.8.emb_basis, f32[128,128]{1,0:T(8,128)S(1)} %get-tuple-element.9.norm, bf16[128,256]{1,0:T(8,128)(2,1)S(1)} %copy-done.5, ...), custom_call_target="tpu_custom_call" | custom-call | tf_op jit(solution)/shard_map/chain/pallas_call | solution.py:170
  51.8 0.0 copy-start.4
  51.8 0.9 copy-done.4
  52.6 4.3 %all-to-all-start = ((bf16[8,64,768]{2,1,0:T(8,128)(2,1)}), bf16[8,64,768]{2,1,0:T(8,128)(2,1)S(1)}, u32[]{:S(2)}, u32[]{:S(2)}) async-start(bf16[8,64,768]{2,1,0:T(8,128)(2,1)} %copy-done.4), calls=%async_computation | async-start | bytes 1572864 | tf_op jit(solution)/shard_map/all_to_all | solution.py:251
  56.9 13.2 %all-to-all-done.got = bf16[8,64,768]{2,1,0:T(8,128)(2,1)S(1)} async-done(((bf16[8,64,768]{2,1,0:T(8,128)(2,1)}), bf16[8,64,768]{2,1,0:T(8,128)(2,1)S(1)}, u32[]{:S(2)}, u32[]{:S(2)}) %all-to-all-start) | async-done | bytes 786464 | tf_op jit(solution)/shard_map/all_to_all | solution.py:251
  70.1 0.3 middle.1
  70.4 24.9 %all_to_all.10.got = bf16[8,64,128]{2,1,0:T(8,128)(2,1)} all-to-all(bf16[8,64,128]{2,1,0:T(8,128)(2,1)S(1)} %middle.1), channel_id=1, replica_groups=mesh['y'=4,'z_hi'=2,'z_lo'=8,'x'=4,'core'=2] {'z_lo'}, dimensions={0} | all-to-all | bytes 262144 | tf_op jit(solution)/shard_map/all_to_all | solution.py:253
  95.3 1.5 %final.1 = f32[64,128]{1,0:T(8,128)} custom-call(bf16[8,64,128]{2,1,0:T(8,128)(2,1)} %all_to_all.10.got), custom_call_target="tpu_custom_call" | custom-call | tf_op jit(solution)/shard_map/final/pallas_call | solution.py:230
Async XLA Ops:
  0.6 4.9 %copy-start = (bf16[4096,256]{1,0:T(8,128)(2,1)S(1)}, bf16[4096,256]{1,0:T(8,128)(2,1)}, u32[]{:S(2)}) copy-start(bf16[4096,256]{1,0:T(8,128)(2,1)} %basis.3) | copy-start | bytes 6291460
  0.6 4.9 %copy-start.1 = (bf16[128,4096]{1,0:T(8,128)(2,1)S(1)}, bf16[128,4096]{1,0:T(8,128)(2,1)}, u32[]{:S(2)}) copy-start(bf16[128,4096]{1,0:T(8,128)(2,1)} %emb.3) | copy-start | bytes 3145732
  5.6 1.2 %copy-start.2 = (bf16[1,4096,64]{2,1,0:T(8,128)(2,1)S(1)}, bf16[1,4096,64]{2,1,0:T(8,128)(2,1)}, u32[]{:S(2)}) copy-start(bf16[1,4096,64]{2,1,0:T(8,128)(2,1)} %copy.10) | copy-start | bytes 1572868
  6.8 1.2 %copy-start.3 = (bf16[1,4096,64]{2,1,0:T(8,128)(2,1)S(1)}, bf16[1,4096,64]{2,1,0:T(8,128)(2,1)}, u32[]{:S(2)}) copy-start(bf16[1,4096,64]{2,1,0:T(8,128)(2,1)} %copy.11) | copy-start | bytes 1572868
  8.0 0.7 copy-start.6
  8.7 37.2 %copy-start.5 = (bf16[128,256]{1,0:T(8,128)(2,1)S(1)}, bf16[128,256]{1,0:T(8,128)(2,1)}, u32[]{:S(2)}) copy-start(bf16[128,256]{1,0:T(8,128)(2,1)} %cotangent.1) | copy-start | bytes 196612
  8.7 37.2 %copy-start.7 = (f32[1,4096]{1,0:T(1,128)S(1)}, f32[1,4096]{1,0:T(1,128)}, u32[]{:S(2)}) copy-start(f32[1,4096]{1,0:T(1,128)} %gain.3) | copy-start | bytes 49156
  11.7 18.9 %collective-permute-start = (bf16[128,384]{1,0:T(8,128)(2,1)S(1)}, bf16[128,384]{1,0:T(8,128)(2,1)}, u32[]{:S(2)}, u32[]{:S(2)}) collective-permute-start(bf16[128,384]{1,0:T(8,128)(2,1)S(1)} %get-tuple-element.7), channel_id=1, source_target_pairs={{0,64},{64,0},{1,65},{65,1},{2,66},{66,2},{3,67},{67,3},{4,68},{68... | collective-permute-start | bytes 294920 | tf_op jit(solution)/shard_map/ppermute | solution.py:238
  51.8 0.9 copy-start.4
  52.6 17.5 %all-to-all-start = ((bf16[8,64,768]{2,1,0:T(8,128)(2,1)}), bf16[8,64,768]{2,1,0:T(8,128)(2,1)S(1)}, u32[]{:S(2)}, u32[]{:S(2)}) async-start(bf16[8,64,768]{2,1,0:T(8,128)(2,1)} %copy-done.4), calls=%async_computation | async-start | bytes 1572864 | tf_op jit(solution)/shard_map/all_to_all | solution.py:251

commit v2 on v1

--- a/solution.py
+++ b/solution.py
@@ -24,86 +24,94 @@
     return lax.dot_general(a, b, dims, preferred_element_type=F32)
 
 
-def project_kernel(steps, emb, basis, down, up, gain, block, emb_basis, norm, acc, acc_pre):
-    step = pl.program_id(0)
-    e = emb[...]
-    down_t = (down[...].astype(F32).T * gain[...]).astype(BF16)
-    up_t = up[...].astype(F32).T.astype(BF16)
-    stacked = jnp.concatenate([e, down_t, up_t], axis=0)
-    part = dot(stacked, basis[...])
-    pre = dot(e, down_t, NT)
-    ef = e.astype(F32)
-    sq = ef * ef
-    width = sq.shape[1]
-    square = sq[:, :128]
-    for at in range(128, width, 128):
-        square = square + sq[:, at : at + 128]
-
-    @pl.when(step == 0)
-    def _():
-        acc[...] = part
-        acc_pre[...] = pre
-        norm[...] = square
-
-    @pl.when(step > 0)
-    def _():
-        acc[...] += part
-        acc_pre[...] += pre
-        norm[...] += square
-
-    @pl.when(step == steps - 1)
-    def _():
-        rows = emb_basis.shape[0]
-        emb_basis[...] = acc[:rows, :]
-        block[:, :256] = acc[rows:, :].astype(BF16)
-        total = acc_pre[...]
-        high = total.astype(BF16)
-        block[:, 256:320] = high
-        block[:, 320:384] = (total - high.astype(F32)).astype(BF16)
-        norm[...] = jnp.broadcast_to(jnp.sum(norm[...], axis=1, keepdims=True), norm.shape)
-
-
-def project(embeds, basis, down, up, gain):
+def project_kernel(
+    chunk, emb_hbm, basis_hbm, down_hbm, up_hbm, gain_hbm,
+    block, repeated, emb_basis, norm, emb, basis, down, up, gain, sems,
+):
+    rows, width = emb.shape
+    steps = width // chunk
+    gain_copy = pltpu.make_async_copy(gain_hbm, gain, sems.at[4, 0])
+    gain_copy.start()
+    copies = []
+    for i in range(steps):
+        at = slice(i * chunk, (i + 1) * chunk)
+        group = [
+            pltpu.make_async_copy(down_hbm.at[:, at], down.at[:, at], sems.at[0, i]),
+            pltpu.make_async_copy(up_hbm.at[:, at], up.at[:, at], sems.at[1, i]),
+            pltpu.make_async_copy(emb_hbm.at[:, at], emb.at[:, at], sems.at[2, i]),
+            pltpu.make_async_copy(basis_hbm.at[at, :], basis.at[at, :], sems.at[3, i]),
+        ]
+        for copy in group:
+            copy.start()
+        copies.append(group)
+    gain_copy.wait()
+    acc = jnp.zeros((rows + 128, basis.shape[1]), F32)
+    acc_pre = jnp.zeros((rows, 64), F32)
+    square = jnp.zeros((rows, 128), F32)
+    for i in range(steps):
+        at = slice(i * chunk, (i + 1) * chunk)
+        for copy in copies[i]:
+            copy.wait()
+        e = emb[:, at]
+        scaled = (down[:, at].astype(F32) * gain[:, at]).astype(BF16)
+        stacked = jnp.concatenate([e, scaled, up[:, at]], axis=0)
+        acc = acc + dot(stacked, basis[at, :])
+        acc_pre = acc_pre + dot(e, scaled, NT)
+        ef = e.astype(F32)
+        sq = ef * ef
+        for k in range(0, chunk, 128):
+            square = square + sq[:, k : k + 128]
+    emb_basis[...] = acc[:rows, :]
+    high = acc_pre.astype(BF16)
+    low = (acc_pre - high.astype(F32)).astype(BF16)
+    weights = acc[rows:, :].astype(BF16)
+    for ref in (block, repeated.at[0], repeated.at[1], repeated.at[2], repeated.at[3]):
+        ref[:, :256] = weights
+        ref[:, 256:320] = high
+        ref[:, 320:384] = low
+    norm[...] = jnp.broadcast_to(jnp.sum(square, axis=1, keepdims=True), norm.shape)
+
+
+def project(embeds, basis, down_t, up_t, gain):
     rows, width = embeds.shape
     rank = basis.shape[1]
-    inner = down.shape[1]
-    steps = 8
-    chunk = width // steps
-    return pl.pallas_call(
-        functools.partial(project_kernel, steps),
-        grid=(steps,),
-        in_specs=[
-            pl.BlockSpec((rows, chunk), lambda i: (0, i)),
-            pl.BlockSpec((chunk, rank), lambda i: (i, 0)),
-            pl.BlockSpec((chunk, inner), lambda i: (i, 0)),
-            pl.BlockSpec((chunk, inner), lambda i: (i, 0)),
-            pl.BlockSpec((1, chunk), lambda i: (0, i)),
-        ],
-        out_specs=[
-            pl.BlockSpec((2 * inner, rank + 2 * inner), lambda i: (0, 0)),
-            pl.BlockSpec((rows, rank), lambda i: (0, 0)),
-            pl.BlockSpec((rows, 128), lambda i: (0, 0)),
-        ],
+    inner = down_t.shape[0]
+    chunk = 512
+    hbm = pl.BlockSpec(memory_space=pltpu.HBM)
+    vmem = pl.BlockSpec(memory_space=pltpu.VMEM)
+    return pl.pallas_call(
+        functools.partial(project_kernel, chunk),
+        in_specs=[hbm] * 5,
+        out_specs=[vmem] * 4,
         out_shape=[
             jax.ShapeDtypeStruct((2 * inner, rank + 2 * inner), BF16),
+            jax.ShapeDtypeStruct((4, 2 * inner, rank + 2 * inner), BF16),
             jax.ShapeDtypeStruct((rows, rank), F32),
             jax.ShapeDtypeStruct((rows, 128), F32),
         ],
         scratch_shapes=[
-            pltpu.VMEM((rows + 2 * inner, rank), F32),
-            pltpu.VMEM((rows, inner), F32),
-        ],
-        compiler_params=pltpu.CompilerParams(vmem_limit_bytes=32 * 1024 * 1024),
+            pltpu.VMEM((rows, width), BF16),
+            pltpu.VMEM((width, rank), BF16),
+            pltpu.VMEM((inner, width), BF16),
+            pltpu.VMEM((inner, width), BF16),
+            pltpu.VMEM((1, width), F32),
+            pltpu.SemaphoreType.DMA((5, width // chunk)),
+        ],
+        compiler_params=pltpu.CompilerParams(vmem_limit_bytes=60 * 1024 * 1024),
         name="project",
-    )(embeds, basis, down, up, gain)
+    )(embeds, basis, down_t, up_t, gain)
 
 
 def chain_kernel(
-    count, place, blocks, emb_basis, norm, cotangent, emb, basis, gain,
-    coefs, slots, c_kept, g_kept, p_kept, a_kept, pre_kept, slope_kept, inv_kept, wide,
+    count, place, own, other, emb_basis, norm, cotangent, emb, basis, gain,
+    coefs, slots_out, blocks, c_kept, g_kept, p_kept, a_kept, pre_kept, slope_kept, inv_kept, wide, slots, sems,
 ):
     width = emb.shape[1]
     inner = 64
+    half = place[1]
+    for y in range(count // 2):
+        blocks[2 * y + half] = own[y]
+        blocks[2 * y + 1 - half] = other[y]
     eu = emb_basis[...]
     sq = norm[:, :1]
     c = jnp.zeros(eu.shape, BF16)
@@ -150,6 +158,7 @@
         grad = dot(p_t, emb[:, cols]) + dot(cp, basis[cols, :], NT)
         wide[:, cols] = grad * gain[:, cols]
     low = lax.broadcasted_iota(jnp.int32, (inner, 128), 1) < 64
+    copies = [pltpu.make_async_copy(slots.at[j], slots_out.at[j], sems.at[j]) for j in range(8)]
     for x in range(4):
         for q in range(4):
             first = wide[:, ((2 * q) * 4 + x) * 128 : ((2 * q) * 4 + x) * 128 + 128]
@@ -157,25 +166,29 @@
             lanes = slice(q * 128, q * 128 + 128)
             slots[2 * x, :, lanes] = jnp.where(low, first, pltpu.roll(second, 64, 1)).astype(BF16)
             slots[2 * x + 1, :, lanes] = jnp.where(low, pltpu.roll(first, 64, 1), second).astype(BF16)
-    for j in range(8):
-        slots[j, :, 512:768] = s2
-
-
-def chain(place, blocks, emb_basis, norm, cotangent, embeds, basis, gain):
-    count = blocks.shape[0]
+        for j in (2 * x, 2 * x + 1):
+            slots[j, :, 512:768] = s2
+            copies[j].start()
+    for copy in copies:
+        copy.wait()
+
+
+def chain(place, own, other, emb_basis, norm, cotangent, embeds, basis, gain):
+    count = 2 * own.shape[0]
     rows, rank = cotangent.shape
     inner = 64
     width = embeds.shape[1]
     vmem = pl.BlockSpec(memory_space=pltpu.VMEM)
     return pl.pallas_call(
         functools.partial(chain_kernel, count),
-        in_specs=[pl.BlockSpec(memory_space=pltpu.SMEM)] + [vmem] * 7,
-        out_specs=[vmem, vmem],
+        in_specs=[pl.BlockSpec(memory_space=pltpu.SMEM)] + [vmem] * 8,
+        out_specs=[vmem, pl.BlockSpec(memory_space=pltpu.HBM)],
         out_shape=[
             jax.ShapeDtypeStruct((rows, rank), BF16),
             jax.ShapeDtypeStruct((8, inner, 768), BF16),
         ],
         scratch_shapes=[
+            pltpu.VMEM((count,) + own.shape[1:], BF16),
             pltpu.VMEM((count + 1, rows, rank), BF16),
             pltpu.VMEM((count, rows, rank), BF16),
             pltpu.VMEM((count, rows, inner), F32),
@@ -184,10 +197,12 @@
             pltpu.VMEM((count, rows, inner), F32),
             pltpu.VMEM((count, rows, 128), F32),
             pltpu.VMEM((inner, width), F32),
+            pltpu.VMEM((8, inner, 768), BF16),
+            pltpu.SemaphoreType.DMA((8,)),
         ],
         compiler_params=pltpu.CompilerParams(vmem_limit_bytes=32 * 1024 * 1024),
         name="chain",
-    )(place, blocks, emb_basis, norm, cotangent, embeds, basis, gain)
+    )(place, own, other, emb_basis, norm, cotangent, embeds, basis, gain)
 
 
 def middle_kernel(place, got, basis, out):
@@ -234,20 +249,18 @@
     )(got)
 
 
-def gather_sections(block):
-    other = lax.ppermute(block, "z_hi", [(0, 1), (1, 0)])
-    mine = lax.axis_index("z_hi")
-    pair = jnp.where(mine == 0, jnp.stack([block, other]), jnp.stack([other, block]))
-    every = lax.all_gather(pair, "y", tiled=False)
-    return every.reshape((8,) + block.shape)
-
-
 def local(embeds, shared_basis, down_proj, up_proj, norm_gain, coef_grad):
-    place = lax.axis_index(SECTION).astype(jnp.int32).reshape(1)
+    half = lax.axis_index("z_hi")
+    place = jnp.stack([2 * lax.axis_index("y") + half, half]).astype(jnp.int32)
     lane = lax.axis_index(("x", "core")).astype(jnp.int32).reshape(1)
-    block, emb_basis, norm = project(embeds, shared_basis, down_proj[0], up_proj[0], norm_gain)
-    blocks = gather_sections(block)
-    coefs, slots = chain(place, blocks, emb_basis, norm, coef_grad, embeds, shared_basis, norm_gain)
+    block, repeated, emb_basis, norm = project(
+        embeds, shared_basis, down_proj[0].T, up_proj[0].T, norm_gain
+    )
+    crossed = lax.ppermute(block, "z_hi", [(0, 1), (1, 0)])
+    own = lax.all_to_all(repeated, "y", 0, 0, tiled=True)
+    crossed = jnp.broadcast_to(crossed[None], repeated.shape)
+    other = lax.all_to_all(crossed, "y", 0, 0, tiled=True)
+    coefs, slots = chain(place, own, other, emb_basis, norm, coef_grad, embeds, shared_basis, norm_gain)
     got = lax.all_to_all(slots, ("x", "core"), 0, 0, tiled=True)
     summed = middle(lane, got, shared_basis)
     got = lax.all_to_all(summed, "z_lo", 0, 0, tiled=True)

time: 97.3 us -> 99.2 us (1.020)
  the two profiles are of different devices: /device:TPU:8 before, /device:TPU:32 now
where the time goes in v2:
time: 99.2 us; the launch traced here: 98.7 us
  starting transfers between devices  28.1 us (28%)
  waiting for transfers between devices  25.3 us (26%)
  blocking collectives  23.7 us (24%)
  Pallas kernels  14.5 us (15%)
  local copies, waits for them, and re-layouts  5.78 us (6%)
    all_to_all x1, blocking collectives, local(): got = lax.all_to_all(summed, 'z_lo', 0, 0, tiled=True)  23.7 us
    ppermute x1, starting transfers between devices, local(): crossed = lax.ppermute(block, 'z_hi', [(0, 1), (1, 0)])  14.8 us
    all_to_all x1, waiting for transfers between devices, local(): got = lax.all_to_all(slots, ('x', 'core'), 0, 0, tiled=True)  13.2 us
    pallas_call x1, Pallas kernels, chain(): pl.pallas_call(functools.partial(chain_kernel, count), in_specs=[pl.Block...  8.43 us
    all_to_all x1, waiting for transfers between devices, local(): other = lax.all_to_all(crossed, 'y', 0, 0, tiled=True)  6.89 us
    ppermute x1, waiting for transfers between devices, local(): crossed = lax.ppermute(block, 'z_hi', [(0, 1), (1, 0)])  5.22 us
    all_to_all x1, starting transfers between devices, local(): own = lax.all_to_all(repeated, 'y', 0, 0, tiled=True)  4.61 us
    all_to_all x1, starting transfers between devices, local(): other = lax.all_to_all(crossed, 'y', 0, 0, tiled=True)  4.41 us
  transfers between devices with their start and end apart: 4, of which 3 were waited for; matrix products, arithmetic and copies ran while one was open for 1% of the time, Pallas kernels for 0%

profile of v2, /device:TPU:32, one launch (start us, length us, event | category | flops | bytes accessed | tf_op | source)
XLA Modules:
  0.0 98.7 jit_solution(9823004092178432192)
XLA Ops:
  0.6 0.0 copy-start
  0.6 4.3 %project.1 = (bf16[128,384]{1,0:T(8,128)(2,1)}, bf16[4,128,384]{2,1,0:T(8,128)(2,1)}, f32[128,256]{1,0:T(8,128)}, f32[128,128]{1,0:T(8,128)}) custom-call(bf16[128,4096]{1,0:T(8,128)(2,1)} %emb.1, bf16[4096,256]{1,0:T(8,128)(2,1)} %basis.1, bf16[64,4096]{1,0:T(8,128)(2,1)} %bitcast.13, bf16[64,4096]{1,0:T(8,128)(2,1)} %bitcast.14, f32[1,4096]{1,0:T(1,128)} %gain.1), custom_call_target="tpu_custom_call" | custom-call | tf_op jit(solution)/shard_map/project/pallas_call | solution.py:82
  4.9 0.0 copy-start.1
  4.9 0.0 copy-start.6
  4.9 4.6 %all-to-all-start = ((bf16[4,128,384]{2,1,0:T(8,128)(2,1)}), bf16[4,128,384]{2,1,0:T(8,128)(2,1)S(1)}, u32[]{:S(2)}, u32[]{:S(2)}) async-start(bf16[4,128,384]{2,1,0:T(8,128)(2,1)} %get-tuple-element.8), calls=%async_computation | async-start | bytes 786432 | tf_op jit(solution)/shard_map/all_to_all | solution.py:260
  9.5 14.8 %collective-permute-start = (bf16[128,384]{1,0:T(8,128)(2,1)}, bf16[128,384]{1,0:T(8,128)(2,1)}, u32[]{:S(2)}, u32[]{:S(2)}) collective-permute-start(bf16[128,384]{1,0:T(8,128)(2,1)} %get-tuple-element.9), channel_id=1, source_target_pairs={{0,64},{64,0},{1,65},{65,1},{2,66},{66,2},{3,67},{67,3},{4,68},{68... | collective-permute-start | bytes 294920 | tf_op jit(solution)/shard_map/ppermute | solution.py:259
  24.4 5.2 %collective-permute-done = bf16[128,384]{1,0:T(8,128)(2,1)} collective-permute-done((bf16[128,384]{1,0:T(8,128)(2,1)}, bf16[128,384]{1,0:T(8,128)(2,1)}, u32[]{:S(2)}, u32[]{:S(2)}) %collective-permute-start) | collective-permute-done | bytes 98336 | tf_op jit(solution)/shard_map/ppermute | solution.py:259
  29.6 0.0 all-to-all-done.own
  29.6 1.7 %broadcast_in_dim.12 = bf16[4,128,384]{2,1,0:T(8,128)(2,1)} broadcast(bf16[128,384]{1,0:T(8,128)(2,1)} %collective-permute-done), dimensions={1,2} | broadcast | bytes 491520 | tf_op jit(solution)/shard_map/broadcast_in_dim | solution.py:261
  31.3 4.4 %all-to-all-start.1 = ((bf16[4,128,384]{2,1,0:T(8,128)(2,1)}), bf16[4,128,384]{2,1,0:T(8,128)(2,1)}, u32[]{:S(2)}, u32[]{:S(2)}) async-start(bf16[4,128,384]{2,1,0:T(8,128)(2,1)} %broadcast_in_dim.12), calls=%async_computation.1 | async-start | bytes 786432 | tf_op jit(solution)/shard_map/all_to_all | solution.py:262
  35.7 0.6 pad_add_fusion.place
  36.3 6.9 %all-to-all-done.1.other = bf16[4,128,384]{2,1,0:T(8,128)(2,1)} async-done(((bf16[4,128,384]{2,1,0:T(8,128)(2,1)}), bf16[4,128,384]{2,1,0:T(8,128)(2,1)}, u32[]{:S(2)}, u32[]{:S(2)}) %all-to-all-start.1) | async-done | bytes 393248 | tf_op jit(solution)/shard_map/all_to_all | solution.py:262
  43.2 0.0 copy-done
  43.2 0.0 copy-done.1
  43.2 0.0 copy-done.6
  43.2 0.0 copy-start.3
  43.2 0.9 copy-done.3
  44.1 0.0 copy-start.4
  44.1 0.8 copy-done.4
  44.9 0.0 copy-start.5
  44.9 0.8 copy-done.5
  45.8 0.0 copy-start.7
  45.8 0.6 copy-done.7
  46.4 8.4 %chain.1 = (bf16[128,256]{1,0:T(8,128)(2,1)}, bf16[8,64,768]{2,1,0:T(8,128)(2,1)S(1)}) custom-call(s32[2]{0:T(128)S(1)} %copy-done.7, bf16[4,128,384]{2,1,0:T(8,128)(2,1)S(1)} %all-to-all-done.own, bf16[4,128,384]{2,1,0:T(8,128)(2,1)} %all-to-all-done.1.other, f32[128,256]{1,0:T(8,128)S(1)} %copy-done.3, f32[128,128]{1,0:T(8,128)S(1)} %copy-done.5, ...), custom_call_target="tpu_custom_call" | custom-call | tf_op jit(solution)/shard_map/chain/pallas_call | solution.py:182
  54.8 0.0 copy-start.2
  54.8 0.9 copy-done.2
  55.7 4.3 %all-to-all-start.2 = ((bf16[8,64,768]{2,1,0:T(8,128)(2,1)}), bf16[8,64,768]{2,1,0:T(8,128)(2,1)S(1)}, u32[]{:S(2)}, u32[]{:S(2)}) async-start(bf16[8,64,768]{2,1,0:T(8,128)(2,1)} %copy-done.2), calls=%async_computation.2 | async-start | bytes 1572864 | tf_op jit(solution)/shard_map/all_to_all | solution.py:264
  60.0 13.2 %all-to-all-done.2.got = bf16[8,64,768]{2,1,0:T(8,128)(2,1)S(1)} async-done(((bf16[8,64,768]{2,1,0:T(8,128)(2,1)}), bf16[8,64,768]{2,1,0:T(8,128)(2,1)S(1)}, u32[]{:S(2)}, u32[]{:S(2)}) %all-to-all-start.2) | async-done | bytes 786464 | tf_op jit(solution)/shard_map/all_to_all | solution.py:264
  73.2 0.3 middle.1
  73.5 23.7 %all_to_all.20.got = bf16[8,64,128]{2,1,0:T(8,128)(2,1)} all-to-all(bf16[8,64,128]{2,1,0:T(8,128)(2,1)S(1)} %middle.1), channel_id=1, replica_groups=mesh['y'=4,'z_hi'=2,'z_lo'=8,'x'=4,'core'=2] {'z_lo'}, dimensions={0} | all-to-all | bytes 262144 | tf_op jit(solution)/shard_map/all_to_all | solution.py:266
  97.1 1.5 %final.1 = f32[64,128]{1,0:T(8,128)} custom-call(bf16[8,64,128]{2,1,0:T(8,128)(2,1)} %all_to_all.20.got), custom_call_target="tpu_custom_call" | custom-call | tf_op jit(solution)/shard_map/final/pallas_call | solution.py:245
Async XLA Ops:
  0.6 42.5 %copy-start = (bf16[4096,256]{1,0:T(8,128)(2,1)S(1)}, bf16[4096,256]{1,0:T(8,128)(2,1)}, u32[]{:S(2)}) copy-start(bf16[4096,256]{1,0:T(8,128)(2,1)} %basis.1) | copy-start | bytes 6291460
  4.9 38.3 %copy-start.1 = (bf16[128,4096]{1,0:T(8,128)(2,1)S(1)}, bf16[128,4096]{1,0:T(8,128)(2,1)}, u32[]{:S(2)}) copy-start(bf16[128,4096]{1,0:T(8,128)(2,1)} %emb.1) | copy-start | bytes 3145732
  4.9 38.3 %copy-start.6 = (f32[1,4096]{1,0:T(1,128)S(1)}, f32[1,4096]{1,0:T(1,128)}, u32[]{:S(2)}) copy-start(f32[1,4096]{1,0:T(1,128)} %gain.1) | copy-start | bytes 49156
  4.9 24.7 %all-to-all-start = ((bf16[4,128,384]{2,1,0:T(8,128)(2,1)}), bf16[4,128,384]{2,1,0:T(8,128)(2,1)S(1)}, u32[]{:S(2)}, u32[]{:S(2)}) async-start(bf16[4,128,384]{2,1,0:T(8,128)(2,1)} %get-tuple-element.8), calls=%async_computation | async-start | bytes 786432 | tf_op jit(solution)/shard_map/all_to_all | solution.py:260
  9.5 20.0 %collective-permute-start = (bf16[128,384]{1,0:T(8,128)(2,1)}, bf16[128,384]{1,0:T(8,128)(2,1)}, u32[]{:S(2)}, u32[]{:S(2)}) collective-permute-start(bf16[128,384]{1,0:T(8,128)(2,1)} %get-tuple-element.9), channel_id=1, source_target_pairs={{0,64},{64,0},{1,65},{65,1},{2,66},{66,2},{3,67},{67,3},{4,68},{68... | collective-permute-start | bytes 294920 | tf_op jit(solution)/shard_map/ppermute | solution.py:259
  31.3 11.9 %all-to-all-start.1 = ((bf16[4,128,384]{2,1,0:T(8,128)(2,1)}), bf16[4,128,384]{2,1,0:T(8,128)(2,1)}, u32[]{:S(2)}, u32[]{:S(2)}) async-start(bf16[4,128,384]{2,1,0:T(8,128)(2,1)} %broadcast_in_dim.12), calls=%async_computation.1 | async-start | bytes 786432 | tf_op jit(solution)/shard_map/all_to_all | solution.py:262
  43.2 0.9 copy-start.3
  44.1 0.8 copy-start.4
  44.9 0.8 copy-start.5
  45.8 0.6 copy-start.7
  54.8 0.9 copy-start.2
  55.7 17.5 %all-to-all-start.2 = ((bf16[8,64,768]{2,1,0:T(8,128)(2,1)}), bf16[8,64,768]{2,1,0:T(8,128)(2,1)S(1)}, u32[]{:S(2)}, u32[]{:S(2)}) async-start(bf16[8,64,768]{2,1,0:T(8,128)(2,1)} %copy-done.2), calls=%async_computation.2 | async-start | bytes 1572864 | tf_op jit(solution)/shard_map/all_to_all | solution.py:264

commit v3 on v2

--- a/solution.py
+++ b/solution.py
@@ -26,7 +26,7 @@
 
 def project_kernel(
     chunk, emb_hbm, basis_hbm, down_hbm, up_hbm, gain_hbm,
-    block, repeated, emb_basis, norm, emb, basis, down, up, gain, sems,
+    block, emb_basis, norm, emb, basis, down, up, gain, sems,
 ):
     rows, width = emb.shape
     steps = width // chunk
@@ -65,10 +65,9 @@
     high = acc_pre.astype(BF16)
     low = (acc_pre - high.astype(F32)).astype(BF16)
     weights = acc[rows:, :].astype(BF16)
-    for ref in (block, repeated.at[0], repeated.at[1], repeated.at[2], repeated.at[3]):
-        ref[:, :256] = weights
-        ref[:, 256:320] = high
-        ref[:, 320:384] = low
+    block[:, :256] = weights
+    block[:, 256:320] = high
+    block[:, 320:384] = low
     norm[...] = jnp.broadcast_to(jnp.sum(square, axis=1, keepdims=True), norm.shape)
 
 
@@ -79,13 +78,13 @@
     chunk = 512
     hbm = pl.BlockSpec(memory_space=pltpu.HBM)
     vmem = pl.BlockSpec(memory_space=pltpu.VMEM)
+    args = [pltpu.with_memory_space_constraint(a, pltpu.HBM) for a in (embeds, basis, down_t, up_t, gain)]
     return pl.pallas_call(
         functools.partial(project_kernel, chunk),
         in_specs=[hbm] * 5,
-        out_specs=[vmem] * 4,
+        out_specs=[vmem] * 3,
         out_shape=[
             jax.ShapeDtypeStruct((2 * inner, rank + 2 * inner), BF16),
-            jax.ShapeDtypeStruct((4, 2 * inner, rank + 2 * inner), BF16),
             jax.ShapeDtypeStruct((rows, rank), F32),
             jax.ShapeDtypeStruct((rows, 128), F32),
         ],
@@ -97,31 +96,38 @@
             pltpu.VMEM((1, width), F32),
             pltpu.SemaphoreType.DMA((5, width // chunk)),
         ],
-        compiler_params=pltpu.CompilerParams(vmem_limit_bytes=60 * 1024 * 1024),
+        compiler_params=pltpu.CompilerParams(vmem_limit_bytes=24 * 1024 * 1024),
         name="project",
-    )(embeds, basis, down_t, up_t, gain)
+    )(*args)
 
 
 def chain_kernel(
-    count, place, own, other, emb_basis, norm, cotangent, emb, basis, gain,
-    coefs, slots_out, blocks, c_kept, g_kept, p_kept, a_kept, pre_kept, slope_kept, inv_kept, wide, slots, sems,
+    own, other, norm, emb_basis, cotangent, emb, basis, gain,
+    coefs, slots_hbm,
+    blocks, c_kept, g_kept, p_kept, a_kept, pre_kept, slope_kept, inv_kept, wide, slots, out_sems,
 ):
+    count = blocks.shape[0] * blocks.shape[1]
     width = emb.shape[1]
     inner = 64
-    half = place[1]
-    for y in range(count // 2):
-        blocks[2 * y + half] = own[y]
-        blocks[2 * y + 1 - half] = other[y]
+    half = lax.axis_index("z_hi")
+    me = 2 * lax.axis_index("y") + half
+    blocks[half] = own[...]
+    blocks[1 - half] = other[...]
+
+    def block_of(s):
+        return blocks.at[s % 2, s // 2]
+
     eu = emb_basis[...]
     sq = norm[:, :1]
     c = jnp.zeros(eu.shape, BF16)
     c_kept[0] = c
     for s in range(count):
+        block = block_of(s)
         cf = c.astype(F32)
-        pre = blocks[s, :, 256:320].astype(F32) + blocks[s, :, 320:384].astype(F32)
+        pre = block[:, 256:320].astype(F32) + block[:, 320:384].astype(F32)
         total = sq
         if s:
-            pre = pre + dot(c, blocks[s, :inner, :256], NT)
+            pre = pre + dot(c, block[:inner, :256], NT)
             total = total + jnp.sum(cf * (2.0 * eu + cf), axis=1, keepdims=True)
         inv = lax.rsqrt(jnp.maximum(total, 0.0) * (1.0 / width) + EPS)
         pre = pre * inv
@@ -131,23 +137,23 @@
         slope_kept[s] = sig * (1.0 + pre * (1.0 - sig))
         inv_kept[s] = jnp.broadcast_to(inv, inv_kept.shape[1:])
         a_kept[s] = act
-        c = (cf + dot(act, blocks[s, inner:, :256])).astype(BF16)
+        c = (cf + dot(act, block[inner:, :256])).astype(BF16)
         c_kept[s + 1] = c
 
     g = cotangent[...]
     for s in reversed(range(count)):
+        block = block_of(s)
         g_kept[s] = g
         inv = inv_kept[s][:, :1]
-        gp = (dot(g, blocks[s, inner:, :256], NT) * slope_kept[s]).astype(BF16)
+        gp = (dot(g, block[inner:, :256], NT) * slope_kept[s]).astype(BF16)
         gpf = gp.astype(F32)
         p_kept[s] = gpf * inv
         if s:
             mean = jnp.sum(gpf * pre_kept[s], axis=1, keepdims=True) * (1.0 / width)
-            back = dot(gp, blocks[s, :inner, :256])
+            back = dot(gp, block[:inner, :256])
             hid = eu + c_kept[s].astype(F32)
             g = (g.astype(F32) + inv * back - (inv * inv * mean) * hid).astype(BF16)
 
-    me = place[0]
     coefs[...] = c_kept[me + 1]
     p_t = p_kept[me].T.astype(BF16)
     cp = dot(p_t, c_kept[me]).astype(BF16)
@@ -158,7 +164,7 @@
         grad = dot(p_t, emb[:, cols]) + dot(cp, basis[cols, :], NT)
         wide[:, cols] = grad * gain[:, cols]
     low = lax.broadcasted_iota(jnp.int32, (inner, 128), 1) < 64
-    copies = [pltpu.make_async_copy(slots.at[j], slots_out.at[j], sems.at[j]) for j in range(8)]
+    copies = [pltpu.make_async_copy(slots.at[j], slots_hbm.at[j], out_sems.at[j]) for j in range(8)]
     for x in range(4):
         for q in range(4):
             first = wide[:, ((2 * q) * 4 + x) * 128 : ((2 * q) * 4 + x) * 128 + 128]
@@ -173,22 +179,23 @@
         copy.wait()
 
 
-def chain(place, own, other, emb_basis, norm, cotangent, embeds, basis, gain):
+def chain(own, other, norm, emb_basis, cotangent, embeds, basis, gain):
     count = 2 * own.shape[0]
     rows, rank = cotangent.shape
     inner = 64
     width = embeds.shape[1]
+    hbm = pl.BlockSpec(memory_space=pltpu.HBM)
     vmem = pl.BlockSpec(memory_space=pltpu.VMEM)
     return pl.pallas_call(
-        functools.partial(chain_kernel, count),
-        in_specs=[pl.BlockSpec(memory_space=pltpu.SMEM)] + [vmem] * 8,
-        out_specs=[vmem, pl.BlockSpec(memory_space=pltpu.HBM)],
+        chain_kernel,
+        in_specs=[vmem] * 8,
+        out_specs=[vmem, hbm],
         out_shape=[
             jax.ShapeDtypeStruct((rows, rank), BF16),
-            jax.ShapeDtypeStruct((8, inner, 768), BF16),
+            pltpu.HBM((8, inner, 768), BF16),
         ],
         scratch_shapes=[
-            pltpu.VMEM((count,) + own.shape[1:], BF16),
+            pltpu.VMEM((2,) + own.shape, BF16),
             pltpu.VMEM((count + 1, rows, rank), BF16),
             pltpu.VMEM((count, rows, rank), BF16),
             pltpu.VMEM((count, rows, inner), F32),
@@ -202,7 +209,7 @@
         ],
         compiler_params=pltpu.CompilerParams(vmem_limit_bytes=32 * 1024 * 1024),
         name="chain",
-    )(place, own, other, emb_basis, norm, cotangent, embeds, basis, gain)
+    )(own, other, norm, emb_basis, cotangent, embeds, basis, gain)
 
 
 def middle_kernel(place, got, basis, out):
@@ -250,17 +257,14 @@
 
 
 def local(embeds, shared_basis, down_proj, up_proj, norm_gain, coef_grad):
-    half = lax.axis_index("z_hi")
-    place = jnp.stack([2 * lax.axis_index("y") + half, half]).astype(jnp.int32)
     lane = lax.axis_index(("x", "core")).astype(jnp.int32).reshape(1)
-    block, repeated, emb_basis, norm = project(
+    block, emb_basis, norm = project(
         embeds, shared_basis, down_proj[0].T, up_proj[0].T, norm_gain
     )
     crossed = lax.ppermute(block, "z_hi", [(0, 1), (1, 0)])
-    own = lax.all_to_all(repeated, "y", 0, 0, tiled=True)
-    crossed = jnp.broadcast_to(crossed[None], repeated.shape)
-    other = lax.all_to_all(crossed, "y", 0, 0, tiled=True)
-    coefs, slots = chain(place, own, other, emb_basis, norm, coef_grad, embeds, shared_basis, norm_gain)
+    own = lax.all_gather(block, "y", tiled=False)
+    other = lax.all_gather(crossed, "y", tiled=False)
+    coefs, slots = chain(own, other, norm, emb_basis, coef_grad, embeds, shared_basis, norm_gain)
     got = lax.all_to_all(slots, ("x", "core"), 0, 0, tiled=True)
     summed = middle(lane, got, shared_basis)
     got = lax.all_to_all(summed, "z_lo", 0, 0, tiled=True)

time: 99.2 us -> 88.9 us (0.90)
  the two profiles are of different devices: /device:TPU:32 before, /device:TPU:8 now
where the time goes in v3:
time: 88.9 us; the launch traced here: 88.7 us
  blocking collectives  42.6 us (48%)
  starting transfers between devices  20 us (22%)
  waiting for transfers between devices  13.2 us (15%)
  Pallas kernels  12.2 us (14%)
    all_to_all x1, blocking collectives, local(): got = lax.all_to_all(summed, 'z_lo', 0, 0, tiled=True)  16.5 us
    ppermute x1, starting transfers between devices, local(): crossed = lax.ppermute(block, 'z_hi', [(0, 1), (1, 0)])  15.7 us
    all_gather x1, blocking collectives, local(): own = lax.all_gather(block, 'y', tiled=False)  13.2 us
    all_to_all x1, waiting for transfers between devices, local(): got = lax.all_to_all(slots, ('x', 'core'), 0, 0, tiled=True)  13.2 us
    all_gather x1, blocking collectives, local(): other = lax.all_gather(crossed, 'y', tiled=False)  12.9 us
    pallas_call x1, Pallas kernels, chain(): pl.pallas_call(chain_kernel, in_specs=[vmem] * 8, out_specs=[vmem, hbm],...  6.94 us
    all_to_all x1, starting transfers between devices, local(): got = lax.all_to_all(slots, ('x', 'core'), 0, 0, tiled=True)  4.27 us
    pallas_call x1, Pallas kernels, project(): pl.pallas_call(functools.partial(project_kernel, chunk), in_specs=[hbm] *...  3.44 us
  transfers between devices with their start and end apart: 2, of which 1 were waited for; matrix products, arithmetic and copies ran while one was open for 0% of the time, Pallas kernels for 0%

profile of v3, /device:TPU:8, one launch (start us, length us, event | category | flops | bytes accessed | tf_op | source)
XLA Modules:
  0.0 88.7 jit_solution(8936743526649020681)
XLA Ops:
  0.6 0.0 copy-start
  0.6 0.0 copy-start.1
  0.7 0.0 copy-start.2
  0.7 0.0 copy-start.3
  0.7 3.4 %project.1 = (bf16[128,384]{1,0:T(8,128)(2,1)S(1)}, f32[128,256]{1,0:T(8,128)S(1)}, f32[128,128]{1,0:T(8,128)S(1)}) custom-call(bf16[128,4096]{1,0:T(8,128)(2,1)} %emb.1, bf16[4096,256]{1,0:T(8,128)(2,1)} %basis.1, bf16[64,4096]{1,0:T(8,128)(2,1)} %bitcast.15, bf16[64,4096]{1,0:T(8,128)(2,1)} %bitcast.16, f32[1,4096]{1,0:T(1,128)} %gain.1), custom_call_target="tpu_custom_call" | custom-call | tf_op jit(solution)/shard_map/project/pallas_call | solution.py:82
  4.1 15.7 %collective-permute-start = (bf16[128,384]{1,0:T(8,128)(2,1)S(1)}, bf16[128,384]{1,0:T(8,128)(2,1)S(1)}, u32[]{:S(2)}, u32[]{:S(2)}) collective-permute-start(bf16[128,384]{1,0:T(8,128)(2,1)S(1)} %get-tuple-element.7), channel_id=1, source_target_pairs={{0,64},{64,0},{1,65},{65,1},{2,66},{66,2},{3,67},{67,3},{4,68},{68... | collective-permute-start | bytes 294920 | tf_op jit(solution)/shard_map/ppermute | solution.py:264
  19.9 13.2 %all-gather = bf16[512,384]{1,0:T(8,128)(2,1)S(1)} all-gather(bf16[128,384]{1,0:T(8,128)(2,1)S(1)} %get-tuple-element.7), channel_id=2, replica_groups=mesh['y'=4,'z_hi'=2,'z_lo'=8,'x'=4,'core'=2] {'y'}, dimensions={0}, use_global_device_ids=true | all-gather | bytes 491520 | tf_op jit(solution)/shard_map/all_gather | solution.py:265
  33.0 0.0 collective-permute-done
  33.0 12.9 %all-gather.1 = bf16[512,384]{1,0:T(8,128)(2,1)S(1)} all-gather(bf16[128,384]{1,0:T(8,128)(2,1)S(1)} %collective-permute-done), channel_id=3, replica_groups=mesh['y'=4,'z_hi'=2,'z_lo'=8,'x'=4,'core'=2] {'y'}, dimensions={0}, use_global_device_ids=true | all-gather | bytes 491520 | tf_op jit(solution)/shard_map/all_gather | solution.py:266
  46.0 0.0 copy-done
  46.0 0.0 copy-done.1
  46.0 0.0 copy-done.2
  46.0 0.0 copy-done.3
  46.0 6.9 %chain.1 = (bf16[128,256]{1,0:T(8,128)(2,1)}, bf16[8,64,768]{2,1,0:T(8,128)(2,1)}) custom-call(bf16[4,128,384]{2,1,0:T(8,128)(2,1)S(1)} %bitcast.13, bf16[4,128,384]{2,1,0:T(8,128)(2,1)S(1)} %bitcast.14, f32[128,128]{1,0:T(8,128)S(1)} %get-tuple-element.8.norm, f32[128,256]{1,0:T(8,128)S(1)} %get-tuple-element.9.emb_basis, bf16[128,256]{1,0:T(8,128)(2,1)S(1)} %copy-done.2, ...), custom_call_target="tpu_custom_call" | custom-call | tf_op jit(solution)/shard_map/chain/pallas_call | solution.py:189
  52.9 4.3 %all-to-all-start = ((bf16[8,64,768]{2,1,0:T(8,128)(2,1)}), bf16[8,64,768]{2,1,0:T(8,128)(2,1)S(1)}, u32[]{:S(2)}, u32[]{:S(2)}) async-start(bf16[8,64,768]{2,1,0:T(8,128)(2,1)} %get-tuple-element.11), calls=%async_computation | async-start | bytes 1572864 | tf_op jit(solution)/shard_map/all_to_all | solution.py:268
  57.2 13.2 %all-to-all-done.got = bf16[8,64,768]{2,1,0:T(8,128)(2,1)S(1)} async-done(((bf16[8,64,768]{2,1,0:T(8,128)(2,1)}), bf16[8,64,768]{2,1,0:T(8,128)(2,1)S(1)}, u32[]{:S(2)}, u32[]{:S(2)}) %all-to-all-start) | async-done | bytes 786464 | tf_op jit(solution)/shard_map/all_to_all | solution.py:268
  70.3 0.3 middle.1
  70.6 16.5 %all_to_all.10.got = bf16[8,64,128]{2,1,0:T(8,128)(2,1)} all-to-all(bf16[8,64,128]{2,1,0:T(8,128)(2,1)S(1)} %middle.1), channel_id=1, replica_groups=mesh['y'=4,'z_hi'=2,'z_lo'=8,'x'=4,'core'=2] {'z_lo'}, dimensions={0} | all-to-all | bytes 262144 | tf_op jit(solution)/shard_map/all_to_all | solution.py:270
  87.1 1.5 %final.1 = f32[64,128]{1,0:T(8,128)} custom-call(bf16[8,64,128]{2,1,0:T(8,128)(2,1)} %all_to_all.10.got), custom_call_target="tpu_custom_call" | custom-call | tf_op jit(solution)/shard_map/final/pallas_call | solution.py:252
Async XLA Ops:
  0.6 45.3 %copy-start = (bf16[4096,256]{1,0:T(8,128)(2,1)S(1)}, bf16[4096,256]{1,0:T(8,128)(2,1)}, u32[]{:S(2)}) copy-start(bf16[4096,256]{1,0:T(8,128)(2,1)} %basis.1) | copy-start | bytes 6291460
  0.6 45.3 %copy-start.1 = (bf16[128,4096]{1,0:T(8,128)(2,1)S(1)}, bf16[128,4096]{1,0:T(8,128)(2,1)}, u32[]{:S(2)}) copy-start(bf16[128,4096]{1,0:T(8,128)(2,1)} %emb.1) | copy-start | bytes 3145732
  0.7 45.3 %copy-start.2 = (bf16[128,256]{1,0:T(8,128)(2,1)S(1)}, bf16[128,256]{1,0:T(8,128)(2,1)}, u32[]{:S(2)}) copy-start(bf16[128,256]{1,0:T(8,128)(2,1)} %cotangent.1) | copy-start | bytes 196612
  0.7 45.3 %copy-start.3 = (f32[1,4096]{1,0:T(1,128)S(1)}, f32[1,4096]{1,0:T(1,128)}, u32[]{:S(2)}) copy-start(f32[1,4096]{1,0:T(1,128)} %gain.1) | copy-start | bytes 49156
  4.1 28.9 %collective-permute-start = (bf16[128,384]{1,0:T(8,128)(2,1)S(1)}, bf16[128,384]{1,0:T(8,128)(2,1)S(1)}, u32[]{:S(2)}, u32[]{:S(2)}) collective-permute-start(bf16[128,384]{1,0:T(8,128)(2,1)S(1)} %get-tuple-element.7), channel_id=1, source_target_pairs={{0,64},{64,0},{1,65},{65,1},{2,66},{66,2},{3,67},{67,3},{4,68},{68... | collective-permute-start | bytes 294920 | tf_op jit(solution)/shard_map/ppermute | solution.py:264
  52.9 17.4 %all-to-all-start = ((bf16[8,64,768]{2,1,0:T(8,128)(2,1)}), bf16[8,64,768]{2,1,0:T(8,128)(2,1)S(1)}, u32[]{:S(2)}, u32[]{:S(2)}) async-start(bf16[8,64,768]{2,1,0:T(8,128)(2,1)} %get-tuple-element.11), calls=%async_computation | async-start | bytes 1572864 | tf_op jit(solution)/shard_map/all_to_all | solution.py:268

commit v4 on v3

v4 whole, which is shorter than its diff:
```python
import functools

import jax
import jax.numpy as jnp
from jax import lax
from jax.experimental import pallas as pl
from jax.experimental.pallas import tpu as pltpu
from jax.sharding import Mesh, PartitionSpec as P

F32 = jnp.float32
BF16 = jnp.bfloat16
EPS = 1e-05
SECTION = ("y", "z_hi")
REPLICA = ("z_lo", "x", "core")
AXES = SECTION + REPLICA
SIZES = (4, 2, 8, 4, 2)

NN = (((1,), (0,)), ((), ()))
NT = (((1,), (1,)), ((), ()))
TN = (((0,), (0,)), ((), ()))


def dot(a, b, dims=NN):
    return lax.dot_general(a, b, dims, preferred_element_type=F32)


def project_kernel(
    chunk, emb_hbm, basis_hbm, down_hbm, up_hbm, gain_hbm,
    block, part, emb_basis, norm, emb, basis, down, up, gain, sems,
):
    rows, width = emb.shape
    steps = width // chunk
    gain_copy = pltpu.make_async_copy(gain_hbm, gain, sems.at[4, 0])
    gain_copy.start()
    copies = []
    for i in range(steps):
        at = slice(i * chunk, (i + 1) * chunk)
        group = [
            pltpu.make_async_copy(down_hbm.at[:, at], down.at[:, at], sems.at[0, i]),
            pltpu.make_async_copy(up_hbm.at[:, at], up.at[:, at], sems.at[1, i]),
            pltpu.make_async_copy(emb_hbm.at[:, at], emb.at[:, at], sems.at[2, i]),
            pltpu.make_async_copy(basis_hbm.at[at, :], basis.at[at, :], sems.at[3, i]),
        ]
        for copy in group:
            copy.start()
        copies.append(group)
    gain_copy.wait()
    acc = jnp.zeros((rows + 128, basis.shape[1]), F32)
    acc_pre = jnp.zeros((rows, 64), F32)
    square = jnp.zeros((rows, 128), F32)
    for i in range(steps):
        at = slice(i * chunk, (i + 1) * chunk)
        for copy in copies[i]:
            copy.wait()
        e = emb[:, at]
        scaled = (down[:, at].astype(F32) * gain[:, at]).astype(BF16)
        stacked = jnp.concatenate([e, scaled, up[:, at]], axis=0)
        acc = acc + dot(stacked, basis[at, :])
        acc_pre = acc_pre + dot(e, scaled, NT)
        ef = e.astype(F32)
        sq = ef * ef
        for k in range(0, chunk, 128):
            square = square + sq[:, k : k + 128]
    emb_basis[...] = acc[:rows, :].T
    high = acc_pre.astype(BF16)
    block[:, :256] = acc[rows:, :].astype(BF16)
    block[:, 256:320] = high
    block[:, 320:384] = (acc_pre - high.astype(F32)).astype(BF16)
    first = lax.axis_index("core") == 0
    weights = jnp.where(first, acc[rows : rows + 64, :], acc[rows + 64 :, :])
    part[:, :256] = weights.astype(BF16)
    part[:, 256:320] = high[:64]
    part[:, 320:384] = high[64:]
    norm[...] = jnp.sum(square.T, axis=0, keepdims=True)


def project(embeds, basis, down_t, up_t, gain):
    rows, width = embeds.shape
    rank = basis.shape[1]
    inner = down_t.shape[0]
    chunk = 512
    hbm = pl.BlockSpec(memory_space=pltpu.HBM)
    vmem = pl.BlockSpec(memory_space=pltpu.VMEM)
    args = [pltpu.with_memory_space_constraint(a, pltpu.HBM) for a in (embeds, basis, down_t, up_t, gain)]
    return pl.pallas_call(
        functools.partial(project_kernel, chunk),
        in_specs=[hbm] * 5,
        out_specs=[vmem] * 4,
        out_shape=[
            jax.ShapeDtypeStruct((2 * inner, rank + 2 * inner), BF16),
            jax.ShapeDtypeStruct((inner, rank + 2 * inner), BF16),
            jax.ShapeDtypeStruct((rank, rows), F32),
            jax.ShapeDtypeStruct((1, rows), F32),
        ],
        scratch_shapes=[
            pltpu.VMEM((rows, width), BF16),
            pltpu.VMEM((width, rank), BF16),
            pltpu.VMEM((inner, width), BF16),
            pltpu.VMEM((inner, width), BF16),
            pltpu.VMEM((1, width), F32),
            pltpu.SemaphoreType.DMA((5, width // chunk)),
        ],
        compiler_params=pltpu.CompilerParams(vmem_limit_bytes=24 * 1024 * 1024),
        name="project",
    )(*args)


def chain_kernel(
    own0, own1, own2, own3, other, norm, emb_basis, cotangent, emb, basis, gain,
    coefs_hbm, slots,
    weights, turned, pre_emb, c_kept, g_kept, p_kept, a_kept, pre_kept, slope_kept, coefs, coefs_sem,
):
    count = weights.shape[0]
    width = emb.shape[1]
    inner = 64
    half = lax.axis_index("z_hi")
    core = lax.axis_index("core")
    y = lax.axis_index("y")
    me = 2 * y + half
    for k, block in enumerate((own0, own1, own2, own3)):
        s = 2 * lax.rem(y + 4 - k, 4) + half
        weights[s] = block[:, :256]
        pre_emb[s] = (block[:, 256:320].astype(F32) + block[:, 320:384].astype(F32)).T
    for k in range(count // 2):
        s = 2 * k + 1 - half
        weights[s, :inner] = other[k, 0, :, :256]
        weights[s, inner:] = other[k, 1, :, :256]
        mine = other[k, core, :, 256:384].astype(F32).T
        pre_emb[s] = jnp.concatenate([mine[:64], mine[64:]], axis=1)
    for s in range(count):
        turned[s] = weights[s].T

    eu = emb_basis[...]
    sq = norm[...]
    c = jnp.zeros(eu.shape, BF16)
    c_kept[0] = c
    invs = []
    for s in range(count):
        cf = c.astype(F32)
        pre = pre_emb[s]
        total = sq
        if s:
            pre = pre + dot(weights[s, :inner], c)
            total = total + jnp.sum(cf * (2.0 * eu + cf), axis=0, keepdims=True)
        inv = lax.rsqrt(jnp.maximum(total, 0.0) * (1.0 / width) + EPS)
        invs.append(inv)
        pre = pre * inv
        sig = 1.0 / (1.0 + jnp.exp(-pre))
        act = (pre * sig).astype(BF16)
        pre_kept[s] = pre
        slope_kept[s] = sig * (1.0 + pre * (1.0 - sig))
        a_kept[s] = act
        c = (cf + dot(turned[s, :, inner:], act)).astype(BF16)
        c_kept[s + 1] = c
    coefs[...] = c_kept[me + 1].T
    coefs_copy = pltpu.make_async_copy(coefs, coefs_hbm, coefs_sem)
    coefs_copy.start()

    g = cotangent[...].T
    for s in reversed(range(count)):
        g_kept[s] = g
        inv = invs[s]
        gp = (dot(weights[s, inner:], g) * slope_kept[s]).astype(BF16)
        gpf = gp.astype(F32)
        p_kept[s] = (gpf * inv).astype(BF16)
        if s:
            mean = jnp.sum(gpf * pre_kept[s], axis=0, keepdims=True) * (1.0 / width)
            back = dot(turned[s, :, :inner], gp)
            hid = eu + c_kept[s].astype(F32)
            g = (g.astype(F32) + inv * back - (inv * inv * mean) * hid).astype(BF16)

    p_t = p_kept[me]
    cp = dot(p_t, c_kept[me], NT).astype(BF16)
    s2 = dot(a_kept[me], g_kept[me], NT).astype(BF16)
    low = lax.broadcasted_iota(jnp.int32, (inner, 128), 1) < 64
    for x in range(4):
        spans = [slice((zl * 4 + x) * 128, (zl * 4 + x) * 128 + 128) for zl in range(8)]
        tiles = jnp.concatenate([emb[:, at] for at in spans], axis=1)
        rows = jnp.concatenate([basis[at, :] for at in spans], axis=0)
        scale = jnp.concatenate([gain[:, at] for at in spans], axis=1)
        grad = (dot(p_t, tiles) + dot(cp, rows, NT)) * scale
        for q in range(4):
            first = grad[:, 256 * q : 256 * q + 128]
            second = grad[:, 256 * q + 128 : 256 * q + 256]
            lanes = slice(q * 128, q * 128 + 128)
            slots[2 * x, :, lanes] = jnp.where(low, first, pltpu.roll(second, 64, 1)).astype(BF16)
            slots[2 * x + 1, :, lanes] = jnp.where(low, pltpu.roll(first, 64, 1), second).astype(BF16)
        for j in (2 * x, 2 * x + 1):
            slots[j, :, 512:768] = s2
    coefs_copy.wait()


def chain(own, other, norm, emb_basis, cotangent, embeds, basis, gain):
    count = 2 * len(own)
    rows, rank = cotangent.shape
    inner = 64
    hbm = pl.BlockSpec(memory_space=pltpu.HBM)
    vmem = pl.BlockSpec(memory_space=pltpu.VMEM)
    return pl.pallas_call(
        chain_kernel,
        in_specs=[vmem] * 11,
        out_specs=[hbm, vmem],
        out_shape=[
            pltpu.HBM((rows, rank), BF16),
            jax.ShapeDtypeStruct((8, inner, 768), BF16),
        ],
        scratch_shapes=[
            pltpu.VMEM((count, 2 * inner, rank), BF16),
            pltpu.VMEM((count, rank, 2 * inner), BF16),
            pltpu.VMEM((count, inner, rows), F32),
            pltpu.VMEM((count + 1, rank, rows), BF16),
            pltpu.VMEM((count, rank, rows), BF16),
            pltpu.VMEM((count, inner, rows), BF16),
            pltpu.VMEM((count, inner, rows), BF16),
            pltpu.VMEM((count, inner, rows), F32),
            pltpu.VMEM((count, inner, rows), F32),
            pltpu.VMEM((rows, rank), BF16),
            pltpu.SemaphoreType.DMA,
        ],
        compiler_params=pltpu.CompilerParams(vmem_limit_bytes=32 * 1024 * 1024),
        name="chain",
    )(*own, other, norm, emb_basis, cotangent, embeds, basis, gain)


def middle_kernel(got, basis, out):
    total = got[0].astype(F32)
    for j in range(1, got.shape[0]):
        total = total + got[j].astype(F32)
    lane = 2 * lax.axis_index("x") + lax.axis_index("core")
    rows = basis[:, lane].reshape(512, 256)
    w2 = dot(total[:, 512:].astype(BF16), rows, NT)
    both = jnp.concatenate([total[:, :512], w2], axis=0)
    out[...] = both.T.astype(BF16).reshape(out.shape)


def middle(got, basis):
    return pl.pallas_call(
        middle_kernel,
        in_specs=[pl.BlockSpec(memory_space=pltpu.VMEM)] * 2,
        out_specs=pl.BlockSpec(memory_space=pltpu.VMEM),
        out_shape=jax.ShapeDtypeStruct((8, 64, 128), BF16),
        compiler_params=pltpu.CompilerParams(vmem_limit_bytes=32 * 1024 * 1024),
        name="middle",
    )(got, basis.reshape(8, 8, 64, 256))


def final_kernel(got, out):
    total = got[0].astype(F32)
    for j in range(1, got.shape[0]):
        total = total + got[j].astype(F32)
    out[...] = total


def final(got):
    return pl.pallas_call(
        final_kernel,
        out_shape=jax.ShapeDtypeStruct(got.shape[1:], F32),
        compiler_params=pltpu.CompilerParams(vmem_limit_bytes=4 * 1024 * 1024),
        name="final",
    )(got)


def local(embeds, shared_basis, down_proj, up_proj, norm_gain, coef_grad):
    block, part, emb_basis, norm = project(
        embeds, shared_basis, down_proj[0].T, up_proj[0].T, norm_gain
    )
    crossed = lax.ppermute(part, "z_hi", [(0, 1), (1, 0)])
    own = [block] + [lax.ppermute(block, "y", [(i, (i + k) % 4) for i in range(4)]) for k in (1, 2, 3)]
    other = lax.all_gather(crossed, ("y", "core"), tiled=False).reshape((4, 2) + part.shape)
    coefs, slots = chain(own, other, norm, emb_basis, coef_grad, embeds, shared_basis, norm_gain)
    got = lax.all_to_all(slots, ("x", "core"), 0, 0, tiled=True)
    summed = middle(got, shared_basis)
    got = lax.all_to_all(summed, "z_lo", 0, 0, tiled=True)
    return coefs[None], final(got)[None]


def solution(mesh):
    fine = Mesh(mesh.devices.reshape(SIZES), AXES)
    placed = (
        P(REPLICA, None),
        P(),
        P(SECTION, None, None),
        P(SECTION, None, None),
        P(SECTION, None),
        P(REPLICA, None),
    )
    return jax.shard_map(
        local,
        mesh=fine,
        in_specs=placed,
        out_specs=(P(SECTION, REPLICA, None), P(SECTION, REPLICA, None)),
        check_vma=False,
    )
```

time: 88.9 us -> 83.9 us (0.944)
  waiting for transfers between devices: 13.2 us -> 0.01 us
  starting transfers between devices: 20 us -> 26.4 us
  blocking collectives: 42.6 us -> 45.8 us
  Pallas kernels: 12.2 us -> 10.6 us
    all_to_all x0 -> x1, blocking collectives: none -> 17.3 us  [local(): got = lax.all_to_all(slots, ('x', 'core'), 0, 0, tiled=True)]
    all_gather x2 -> x1, blocking collectives: 26.1 us -> 12.1 us  [local(): lax.all_gather(crossed, ('y', 'core'), tiled=False)]
    all_to_all x1 -> x0, waiting for transfers between devices: 13.2 us -> none  [local(): got = lax.all_to_all(slots, ('x', 'core'), 0, 0, tiled=True)]
    ppermute x1 -> x4, starting transfers between devices: 15.7 us -> 26.4 us  [the longest x1 15.7 us: local(): crossed = lax.ppermute(part, 'z_hi', [(0, 1), (1, 0)])]
    all_to_all x1 -> x0, starting transfers between devices: 4.27 us -> none  [local(): got = lax.all_to_all(slots, ('x', 'core'), 0, 0, tiled=True)]
    pallas_call x1, Pallas kernels: 1.54 us -> 0.64 us  [final(): pl.pallas_call(final_kernel, out_shape=jax.ShapeDtypeStruct(got.shape[1:]...]
  transfers between devices with their start and end apart: 2 -> 4, of which waited for: 1 -> 0; matrix products, arithmetic and copies ran while one was open for 0% -> 0% of each run, Pallas kernels for 0% -> 0%
where the time goes in v4:
time: 83.9 us; the launch traced here: 83.6 us
  blocking collectives  45.8 us (55%)
  starting transfers between devices  26.4 us (31%)
  Pallas kernels  10.6 us (13%)
    all_to_all x1, blocking collectives, local(): got = lax.all_to_all(slots, ('x', 'core'), 0, 0, tiled=True)  17.3 us
    all_to_all x1, blocking collectives, local(): got = lax.all_to_all(summed, 'z_lo', 0, 0, tiled=True)  16.4 us
    ppermute x1, starting transfers between devices, local(): crossed = lax.ppermute(part, 'z_hi', [(0, 1), (1, 0)])  15.7 us
    all_gather x1, blocking collectives, local(): lax.all_gather(crossed, ('y', 'core'), tiled=False)  12.1 us
    ppermute x3, starting transfers between devices, local(): lax.ppermute(block, 'y', [(i, (i + k) % 4) for i in range(4)])  10.7 us
    pallas_call x1, Pallas kernels, chain(): pl.pallas_call(chain_kernel, in_specs=[vmem] * 11, out_specs=[hbm, vmem],...  6.18 us
    pallas_call x1, Pallas kernels, project(): pl.pallas_call(functools.partial(project_kernel, chunk), in_specs=[hbm] *...  3.51 us
  transfers between devices with their start and end apart: 4, of which 0 were waited for; matrix products, arithmetic and copies ran while one was open for 0% of the time, Pallas kernels for 0%

profile of v4, /device:TPU:8, one launch (start us, length us, event | category | flops | bytes accessed | tf_op | source)
XLA Modules:
  0.0 83.6 jit_solution(8155070415837181608)
XLA Ops:
  0.6 0.0 copy-start
  0.6 0.0 copy-start.1
  0.7 0.0 copy-start.2
  0.7 0.0 copy-start.3
  0.7 3.5 %project.1 = (bf16[128,384]{1,0:T(8,128)(2,1)S(1)}, bf16[64,384]{1,0:T(8,128)(2,1)S(1)}, f32[256,128]{1,0:T(8,128)S(1)}, f32[1,128]{1,0:T(1,128)S(1)}) custom-call(bf16[128,4096]{1,0:T(8,128)(2,1)} %emb.1, bf16[4096,256]{1,0:T(8,128)(2,1)} %basis.1, bf16[64,4096]{1,0:T(8,128)(2,1)} %bitcast.12, bf16[64,4096]{1,0:T(8,128)(2,1)} %bitcast.13, f32[1,4096]{1,0:T(1,128)} %gain.1), custom_call_target="tpu_custom_call" | custom-call | tf_op jit(solution)/shard_map/project/pallas_call | solution.py:85
  4.2 15.7 %collective-permute-start.3 = (bf16[64,384]{1,0:T(8,128)(2,1)S(1)}, bf16[64,384]{1,0:T(8,128)(2,1)S(1)}, u32[]{:S(2)}, u32[]{:S(2)}) collective-permute-start(bf16[64,384]{1,0:T(8,128)(2,1)S(1)} %get-tuple-element.9), channel_id=1, source_target_pairs={{0,64},{64,0},{1,65},{65,1},{2,66},{66,2},{3,67},{67,3},{4,68},{68... | collective-permute-start | bytes 147464 | tf_op jit(solution)/shard_map/ppermute | solution.py:267
  19.9 2.4 %collective-permute-start.2 = (bf16[128,384]{1,0:T(8,128)(2,1)S(1)}, bf16[128,384]{1,0:T(8,128)(2,1)S(1)}, u32[]{:S(2)}, u32[]{:S(2)}) collective-permute-start(bf16[128,384]{1,0:T(8,128)(2,1)S(1)} %get-tuple-element.8.own0), channel_id=1, source_target_pairs={{0,384},{128,0},{256,128},{384,256},{1,385},{129,1},{257,129},{385... | collective-permute-start | bytes 294920 | tf_op jit(solution)/shard_map/ppermute | solution.py:268
  22.3 4.5 %collective-permute-start.1 = (bf16[128,384]{1,0:T(8,128)(2,1)S(1)}, bf16[128,384]{1,0:T(8,128)(2,1)S(1)}, u32[]{:S(2)}, u32[]{:S(2)}) collective-permute-start(bf16[128,384]{1,0:T(8,128)(2,1)S(1)} %get-tuple-element.8.own0), channel_id=1, source_target_pairs={{0,256},{128,384},{256,0},{384,128},{1,257},{129,385},{257,1},{385... | collective-permute-start | bytes 294920 | tf_op jit(solution)/shard_map/ppermute | solution.py:268
  26.8 3.8 %collective-permute-start = (bf16[128,384]{1,0:T(8,128)(2,1)S(1)}, bf16[128,384]{1,0:T(8,128)(2,1)S(1)}, u32[]{:S(2)}, u32[]{:S(2)}) collective-permute-start(bf16[128,384]{1,0:T(8,128)(2,1)S(1)} %get-tuple-element.8.own0), channel_id=1, source_target_pairs={{0,128},{128,256},{256,384},{384,0},{1,129},{129,257},{257,385},{3... | collective-permute-start | bytes 294920 | tf_op jit(solution)/shard_map/ppermute | solution.py:268
  30.6 0.0 collective-permute-done.3
  30.6 12.1 %all-gather = bf16[512,384]{1,0:T(8,128)(2,1)S(1)} all-gather(bf16[64,384]{1,0:T(8,128)(2,1)S(1)} %collective-permute-done.3), channel_id=2, replica_groups=mesh['y'=4,'z_hi'=2,'z_lo'=8,'x'=4,'core'=2] {'y','core'}, dimensions={0}, use_global_device_ids=true | all-gather | bytes 442368 | tf_op jit(solution)/shard_map/all_gather | solution.py:269
  42.8 0.0 collective-permute-done.2.own3
  42.8 0.0 collective-permute-done.1.own2
  42.8 0.0 collective-permute-done.own1
  42.8 0.0 copy-done
  42.8 0.0 copy-done.1
  42.8 0.0 copy-done.2
  42.8 0.0 copy-done.3
  42.8 6.2 %chain.1 = (bf16[128,256]{1,0:T(8,128)(2,1)}, bf16[8,64,768]{2,1,0:T(8,128)(2,1)S(1)}) custom-call(bf16[128,384]{1,0:T(8,128)(2,1)S(1)} %get-tuple-element.8.own0, bf16[128,384]{1,0:T(8,128)(2,1)S(1)} %collective-permute-done.own1, bf16[128,384]{1,0:T(8,128)(2,1)S(1)} %collective-permute-done.1.own2, bf16[128,384]{1,0:T(8,128)(2,1)S(1)} %collective-permute-done.2.own3, ...), custom_call_target="tpu_custom_call" | custom-call | tf_op jit(solution)/shard_map/chain/pallas_call | solution.py:199
  49.0 17.3 %all_to_all.10.got = bf16[8,64,768]{2,1,0:T(8,128)(2,1)S(1)} all-to-all(bf16[8,64,768]{2,1,0:T(8,128)(2,1)S(1)} %get-tuple-element.13), channel_id=1, replica_groups=mesh['y'=4,'z_hi'=2,'z_lo'=8,'x'=4,'core'=2] {'x','core'}, dimensions={0} | all-to-all | bytes 1572864 | tf_op jit(solution)/shard_map/all_to_all | solution.py:271
  66.3 0.3 middle.1
  66.6 16.4 %all_to_all.11.got = bf16[8,64,128]{2,1,0:T(8,128)(2,1)S(1)} all-to-all(bf16[8,64,128]{2,1,0:T(8,128)(2,1)S(1)} %middle.1), channel_id=1, replica_groups=mesh['y'=4,'z_hi'=2,'z_lo'=8,'x'=4,'core'=2] {'z_lo'}, dimensions={0} | all-to-all | bytes 262144 | tf_op jit(solution)/shard_map/all_to_all | solution.py:273
  83.0 0.6 final.1
Async XLA Ops:
  0.6 42.1 %copy-start = (bf16[4096,256]{1,0:T(8,128)(2,1)S(1)}, bf16[4096,256]{1,0:T(8,128)(2,1)}, u32[]{:S(2)}) copy-start(bf16[4096,256]{1,0:T(8,128)(2,1)} %basis.1) | copy-start | bytes 6291460
  0.6 42.1 %copy-start.1 = (bf16[128,4096]{1,0:T(8,128)(2,1)S(1)}, bf16[128,4096]{1,0:T(8,128)(2,1)}, u32[]{:S(2)}) copy-start(bf16[128,4096]{1,0:T(8,128)(2,1)} %emb.1) | copy-start | bytes 3145732
  0.7 42.1 %copy-start.2 = (bf16[128,256]{1,0:T(8,128)(2,1)S(1)}, bf16[128,256]{1,0:T(8,128)(2,1)}, u32[]{:S(2)}) copy-start(bf16[128,256]{1,0:T(8,128)(2,1)} %cotangent.1) | copy-start | bytes 196612
  0.7 42.1 %copy-start.3 = (f32[1,4096]{1,0:T(1,128)S(1)}, f32[1,4096]{1,0:T(1,128)}, u32[]{:S(2)}) copy-start(f32[1,4096]{1,0:T(1,128)} %gain.1) | copy-start | bytes 49156
  4.2 26.4 %collective-permute-start.3 = (bf16[64,384]{1,0:T(8,128)(2,1)S(1)}, bf16[64,384]{1,0:T(8,128)(2,1)S(1)}, u32[]{:S(2)}, u32[]{:S(2)}) collective-permute-start(bf16[64,384]{1,0:T(8,128)(2,1)S(1)} %get-tuple-element.9), channel_id=1, source_target_pairs={{0,64},{64,0},{1,65},{65,1},{2,66},{66,2},{3,67},{67,3},{4,68},{68... | collective-permute-start | bytes 147464 | tf_op jit(solution)/shard_map/ppermute | solution.py:267
  19.9 22.8 %collective-permute-start.2 = (bf16[128,384]{1,0:T(8,128)(2,1)S(1)}, bf16[128,384]{1,0:T(8,128)(2,1)S(1)}, u32[]{:S(2)}, u32[]{:S(2)}) collective-permute-start(bf16[128,384]{1,0:T(8,128)(2,1)S(1)} %get-tuple-element.8.own0), channel_id=1, source_target_pairs={{0,384},{128,0},{256,128},{384,256},{1,385},{129,1},{257,129},{385... | collective-permute-start | bytes 294920 | tf_op jit(solution)/shard_map/ppermute | solution.py:268
  22.3 20.5 %collective-permute-start.1 = (bf16[128,384]{1,0:T(8,128)(2,1)S(1)}, bf16[128,384]{1,0:T(8,128)(2,1)S(1)}, u32[]{:S(2)}, u32[]{:S(2)}) collective-permute-start(bf16[128,384]{1,0:T(8,128)(2,1)S(1)} %get-tuple-element.8.own0), channel_id=1, source_target_pairs={{0,256},{128,384},{256,0},{384,128},{1,257},{129,385},{257,1},{385... | collective-permute-start | bytes 294920 | tf_op jit(solution)/shard_map/ppermute | solution.py:268
  26.8 16.0 %collective-permute-start = (bf16[128,384]{1,0:T(8,128)(2,1)S(1)}, bf16[128,384]{1,0:T(8,128)(2,1)S(1)}, u32[]{:S(2)}, u32[]{:S(2)}) collective-permute-start(bf16[128,384]{1,0:T(8,128)(2,1)S(1)} %get-tuple-element.8.own0), channel_id=1, source_target_pairs={{0,128},{128,256},{256,384},{384,0},{1,129},{129,257},{257,385},{3... | collective-permute-start | bytes 294920 | tf_op jit(solution)/shard_map/ppermute | solution.py:268

commit v5 on v4

--- a/solution.py
+++ b/solution.py
@@ -11,9 +11,9 @@
 BF16 = jnp.bfloat16
 EPS = 1e-05
 SECTION = ("y", "z_hi")
-REPLICA = ("z_lo", "x", "core")
+REPLICA = ("z_far", "z_near", "x", "core")
 AXES = SECTION + REPLICA
-SIZES = (4, 2, 8, 4, 2)
+SIZES = (4, 2, 4, 2, 4, 2)
 
 NN = (((1,), (0,)), ((), ()))
 NT = (((1,), (1,)), ((), ()))
@@ -107,7 +107,7 @@
 
 def chain_kernel(
     own0, own1, own2, own3, other, norm, emb_basis, cotangent, emb, basis, gain,
-    coefs_hbm, slots,
+    coefs_hbm, kept, sent,
     weights, turned, pre_emb, c_kept, g_kept, p_kept, a_kept, pre_kept, slope_kept, coefs, coefs_sem,
 ):
     count = weights.shape[0]
@@ -171,22 +171,25 @@
 
     p_t = p_kept[me]
     cp = dot(p_t, c_kept[me], NT).astype(BF16)
-    s2 = dot(a_kept[me], g_kept[me], NT).astype(BF16)
+    s2 = dot(a_kept[me], g_kept[me], NT)
+    kept[8] = s2
+    sent[8] = s2.astype(BF16)
     low = lax.broadcasted_iota(jnp.int32, (inner, 128), 1) < 64
-    for x in range(4):
-        spans = [slice((zl * 4 + x) * 128, (zl * 4 + x) * 128 + 128) for zl in range(8)]
+    first_core = core == 0
+    for j in range(8):
+        spans = [slice(far * 1024 + j * 128, far * 1024 + j * 128 + 128) for far in range(4)]
         tiles = jnp.concatenate([emb[:, at] for at in spans], axis=1)
         rows = jnp.concatenate([basis[at, :] for at in spans], axis=0)
         scale = jnp.concatenate([gain[:, at] for at in spans], axis=1)
         grad = (dot(p_t, tiles) + dot(cp, rows, NT)) * scale
-        for q in range(4):
-            first = grad[:, 256 * q : 256 * q + 128]
-            second = grad[:, 256 * q + 128 : 256 * q + 256]
+        for q in range(2):
+            one = grad[:, 256 * q : 256 * q + 128]
+            two = grad[:, 256 * q + 128 : 256 * q + 256]
             lanes = slice(q * 128, q * 128 + 128)
-            slots[2 * x, :, lanes] = jnp.where(low, first, pltpu.roll(second, 64, 1)).astype(BF16)
-            slots[2 * x + 1, :, lanes] = jnp.where(low, pltpu.roll(first, 64, 1), second).astype(BF16)
-        for j in (2 * x, 2 * x + 1):
-            slots[j, :, 512:768] = s2
+            zero = jnp.where(low, one, pltpu.roll(two, 64, 1))
+            other_half = jnp.where(low, pltpu.roll(one, 64, 1), two)
+            kept[j, :, lanes] = jnp.where(first_core, zero, other_half)
+            sent[j, :, lanes] = jnp.where(first_core, other_half, zero).astype(BF16)
     coefs_copy.wait()
 
 
@@ -199,10 +202,11 @@
     return pl.pallas_call(
         chain_kernel,
         in_specs=[vmem] * 11,
-        out_specs=[hbm, vmem],
+        out_specs=[hbm, vmem, vmem],
         out_shape=[
             pltpu.HBM((rows, rank), BF16),
-            jax.ShapeDtypeStruct((8, inner, 768), BF16),
+            jax.ShapeDtypeStruct((9, inner, 256), F32),
+            jax.ShapeDtypeStruct((9, inner, 256), BF16),
         ],
         scratch_shapes=[
             pltpu.VMEM((count, 2 * inner, rank), BF16),
@@ -222,14 +226,30 @@
     )(*own, other, norm, emb_basis, cotangent, embeds, basis, gain)
 
 
+def merge_kernel(kept, got, out):
+    weights = (kept[8] + got[8].astype(F32)).astype(BF16)
+    for j in range(8):
+        out[j, :, :256] = (kept[j] + got[j].astype(F32)).astype(BF16)
+        out[j, :, 256:] = weights
+
+
+def merge(kept, got):
+    return pl.pallas_call(
+        merge_kernel,
+        out_shape=jax.ShapeDtypeStruct((8, 64, 512), BF16),
+        compiler_params=pltpu.CompilerParams(vmem_limit_bytes=8 * 1024 * 1024),
+        name="merge",
+    )(kept, got)
+
+
 def middle_kernel(got, basis, out):
     total = got[0].astype(F32)
     for j in range(1, got.shape[0]):
         total = total + got[j].astype(F32)
-    lane = 2 * lax.axis_index("x") + lax.axis_index("core")
-    rows = basis[:, lane].reshape(512, 256)
-    w2 = dot(total[:, 512:].astype(BF16), rows, NT)
-    both = jnp.concatenate([total[:, :512], w2], axis=0)
+    lane = 4 * lax.axis_index("z_near") + lax.axis_index("x")
+    rows = basis[:, lane, lax.axis_index("core")].reshape(256, 256)
+    w2 = dot(total[:, 256:].astype(BF16), rows, NT)
+    both = jnp.concatenate([total[:, :256], w2], axis=0)
     out[...] = both.T.astype(BF16).reshape(out.shape)
 
 
@@ -238,10 +258,10 @@
         middle_kernel,
         in_specs=[pl.BlockSpec(memory_space=pltpu.VMEM)] * 2,
         out_specs=pl.BlockSpec(memory_space=pltpu.VMEM),
-        out_shape=jax.ShapeDtypeStruct((8, 64, 128), BF16),
-        compiler_params=pltpu.CompilerParams(vmem_limit_bytes=32 * 1024 * 1024),
+        out_shape=jax.ShapeDtypeStruct((4, 64, 128), BF16),
+        compiler_params=pltpu.CompilerParams(vmem_limit_bytes=16 * 1024 * 1024),
         name="middle",
-    )(got, basis.reshape(8, 8, 64, 256))
+    )(got, basis.reshape(4, 8, 2, 64, 256))
 
 
 def final_kernel(got, out):
@@ -266,11 +286,12 @@
     )
     crossed = lax.ppermute(part, "z_hi", [(0, 1), (1, 0)])
     own = [block] + [lax.ppermute(block, "y", [(i, (i + k) % 4) for i in range(4)]) for k in (1, 2, 3)]
-    other = lax.all_gather(crossed, ("y", "core"), tiled=False).reshape((4, 2) + part.shape)
-    coefs, slots = chain(own, other, norm, emb_basis, coef_grad, embeds, shared_basis, norm_gain)
-    got = lax.all_to_all(slots, ("x", "core"), 0, 0, tiled=True)
-    summed = middle(got, shared_basis)
-    got = lax.all_to_all(summed, "z_lo", 0, 0, tiled=True)
+    other = lax.all_gather(crossed, ("y", "core"), tiled=False)
+    other = other.reshape((4, 2) + part.shape)
+    coefs, kept, sent = chain(own, other, norm, emb_basis, coef_grad, embeds, shared_basis, norm_gain)
+    got = lax.ppermute(sent, "core", [(0, 1), (1, 0)])
+    got = lax.all_to_all(merge(kept, got), ("z_near", "x"), 0, 0, tiled=True)
+    got = lax.all_to_all(middle(got, shared_basis), "z_far", 0, 0, tiled=True)
     return coefs[None], final(got)[None]
 
 

time: 83.9 us -> 82.8 us (0.987)
  blocking collectives: 45.8 us -> 41.2 us
  starting transfers between devices: 26.4 us -> 28.6 us
  waiting for transfers between devices: 0.01 us -> 1.23 us
    all_to_all x2, blocking collectives: 33.7 us -> 29.1 us  [the longest x1 15 us: local(): got = lax.all_to_all(merge(kept, got), ('z_near', 'x'), 0, 0, tiled=True)]
    ppermute x0 -> x1, starting transfers between devices: none -> 2.25 us  [local(): got = lax.ppermute(sent, 'core', [(0, 1), (1, 0)])]
    ppermute x0 -> x1, waiting for transfers between devices: none -> 1.22 us  [local(): got = lax.ppermute(sent, 'core', [(0, 1), (1, 0)])]
    pallas_call x1 -> x2, Pallas kernels: 6.18 us -> 6.26 us  [the longest x1 6.19 us: chain(): pl.pallas_call(chain_kernel, in_specs=[vmem] * 11, out_specs=[hbm, vmem,...]
  transfers between devices with their start and end apart: 4 -> 5, of which waited for: 0 -> 1; matrix products, arithmetic and copies ran while one was open for 0% -> 0% of each run, Pallas kernels for 0% -> 0%
where the time goes in v5:
time: 82.8 us; the launch traced here: 82.5 us
  blocking collectives  41.2 us (50%)
  starting transfers between devices  28.6 us (35%)
  Pallas kernels  10.7 us (13%)
  waiting for transfers between devices  1.23 us (1%)
    ppermute x1, starting transfers between devices, local(): crossed = lax.ppermute(part, 'z_hi', [(0, 1), (1, 0)])  15.7 us
    all_to_all x1, blocking collectives, local(): got = lax.all_to_all(merge(kept, got), ('z_near', 'x'), 0, 0, tiled=True)  15 us
    all_to_all x1, blocking collectives, local(): got = lax.all_to_all(middle(got, shared_basis), 'z_far', 0, 0, tiled=True)  14 us
    all_gather x1, blocking collectives, local(): other = lax.all_gather(crossed, ('y', 'core'), tiled=False)  12.1 us
    ppermute x3, starting transfers between devices, local(): lax.ppermute(block, 'y', [(i, (i + k) % 4) for i in range(4)])  10.7 us
    pallas_call x1, Pallas kernels, chain(): pl.pallas_call(chain_kernel, in_specs=[vmem] * 11, out_specs=[hbm, vmem,...  6.19 us
    pallas_call x1, Pallas kernels, project(): pl.pallas_call(functools.partial(project_kernel, chunk), in_specs=[hbm] *...  3.51 us
    ppermute x1, starting transfers between devices, local(): got = lax.ppermute(sent, 'core', [(0, 1), (1, 0)])  2.25 us
  transfers between devices with their start and end apart: 5, of which 1 were waited for; matrix products, arithmetic and copies ran while one was open for 0% of the time, Pallas kernels for 0%

profile of v5, /device:TPU:8, one launch (start us, length us, event | category | flops | bytes accessed | tf_op | source)
XLA Modules:
  0.0 82.5 jit_solution(4874422609521912302)
XLA Ops:
  0.6 0.0 copy-start
  0.6 0.0 copy-start.1
  0.7 0.0 copy-start.2
  0.7 0.0 copy-start.3
  0.7 3.5 %project.1 = (bf16[128,384]{1,0:T(8,128)(2,1)S(1)}, bf16[64,384]{1,0:T(8,128)(2,1)S(1)}, f32[256,128]{1,0:T(8,128)S(1)}, f32[1,128]{1,0:T(1,128)S(1)}) custom-call(bf16[128,4096]{1,0:T(8,128)(2,1)} %emb.1, bf16[4096,256]{1,0:T(8,128)(2,1)} %basis.1, bf16[64,4096]{1,0:T(8,128)(2,1)} %bitcast.12, bf16[64,4096]{1,0:T(8,128)(2,1)} %bitcast.13, f32[1,4096]{1,0:T(1,128)} %gain.1), custom_call_target="tpu_custom_call" | custom-call | tf_op jit(solution)/shard_map/project/pallas_call | solution.py:85
  4.2 15.7 %collective-permute-start.3 = (bf16[64,384]{1,0:T(8,128)(2,1)S(1)}, bf16[64,384]{1,0:T(8,128)(2,1)S(1)}, u32[]{:S(2)}, u32[]{:S(2)}) collective-permute-start(bf16[64,384]{1,0:T(8,128)(2,1)S(1)} %get-tuple-element.10), channel_id=1, source_target_pairs={{0,64},{64,0},{1,65},{65,1},{2,66},{66,2},{3,67},{67,3},{4,68},{68... | collective-permute-start | bytes 147464 | tf_op jit(solution)/shard_map/ppermute | solution.py:287
  19.9 2.4 %collective-permute-start.2 = (bf16[128,384]{1,0:T(8,128)(2,1)S(1)}, bf16[128,384]{1,0:T(8,128)(2,1)S(1)}, u32[]{:S(2)}, u32[]{:S(2)}) collective-permute-start(bf16[128,384]{1,0:T(8,128)(2,1)S(1)} %get-tuple-element.9.own0), channel_id=1, source_target_pairs={{0,384},{128,0},{256,128},{384,256},{1,385},{129,1},{257,129},{385... | collective-permute-start | bytes 294920 | tf_op jit(solution)/shard_map/ppermute | solution.py:288
  22.3 4.5 %collective-permute-start.1 = (bf16[128,384]{1,0:T(8,128)(2,1)S(1)}, bf16[128,384]{1,0:T(8,128)(2,1)S(1)}, u32[]{:S(2)}, u32[]{:S(2)}) collective-permute-start(bf16[128,384]{1,0:T(8,128)(2,1)S(1)} %get-tuple-element.9.own0), channel_id=1, source_target_pairs={{0,256},{128,384},{256,0},{384,128},{1,257},{129,385},{257,1},{385... | collective-permute-start | bytes 294920 | tf_op jit(solution)/shard_map/ppermute | solution.py:288
  26.8 3.8 %collective-permute-start = (bf16[128,384]{1,0:T(8,128)(2,1)S(1)}, bf16[128,384]{1,0:T(8,128)(2,1)S(1)}, u32[]{:S(2)}, u32[]{:S(2)}) collective-permute-start(bf16[128,384]{1,0:T(8,128)(2,1)S(1)} %get-tuple-element.9.own0), channel_id=1, source_target_pairs={{0,128},{128,256},{256,384},{384,0},{1,129},{129,257},{257,385},{3... | collective-permute-start | bytes 294920 | tf_op jit(solution)/shard_map/ppermute | solution.py:288
  30.6 0.0 collective-permute-done.3
  30.6 12.1 %all-gather = bf16[512,384]{1,0:T(8,128)(2,1)S(1)} all-gather(bf16[64,384]{1,0:T(8,128)(2,1)S(1)} %collective-permute-done.3), channel_id=2, replica_groups=mesh['y'=4,'z_hi'=2,'z_far'=4,'z_near'=2,'x'=4,'core'=2] {'y','core'}, dimensions={0}, use_global_device_ids=true | all-gather | bytes 442368 | tf_op jit(solution)/shard_map/all_gather | solution.py:289
  42.8 0.0 collective-permute-done.2.own3
  42.8 0.0 collective-permute-done.1.own2
  42.8 0.0 collective-permute-done.own1
  42.8 0.0 copy-done
  42.8 0.0 copy-done.1
  42.8 0.0 copy-done.2
  42.8 0.0 copy-done.3
  42.8 6.2 %chain.1 = (bf16[128,256]{1,0:T(8,128)(2,1)}, f32[9,64,256]{2,1,0:T(8,128)S(1)}, bf16[9,64,256]{2,1,0:T(8,128)(2,1)S(1)}) custom-call(bf16[128,384]{1,0:T(8,128)(2,1)S(1)} %get-tuple-element.9.own0, bf16[128,384]{1,0:T(8,128)(2,1)S(1)} %collective-permute-done.own1, bf16[128,384]{1,0:T(8,128)(2,1)S(1)} %collective-permute-done.1.own2, ...), custom_call_target="tpu_custom_call" | custom-call | tf_op jit(solution)/shard_map/chain/pallas_call | solution.py:202
  49.0 2.2 %collective-permute-start.4 = (bf16[9,64,256]{2,1,0:T(8,128)(2,1)S(1)}, bf16[9,64,256]{2,1,0:T(8,128)(2,1)S(1)}, u32[]{:S(2)}, u32[]{:S(2)}) collective-permute-start(bf16[9,64,256]{2,1,0:T(8,128)(2,1)S(1)} %get-tuple-element.15), channel_id=1, source_target_pairs={{0,1},{1,0},{2,3},{3,2},{4,5},{5,4},{6,7},{7,6},{8,9},{9,8},{10,11... | collective-permute-start | bytes 884744 | tf_op jit(solution)/shard_map/ppermute | solution.py:292
  51.3 1.2 %collective-permute-done.4.got = bf16[9,64,256]{2,1,0:T(8,128)(2,1)S(1)} collective-permute-done((bf16[9,64,256]{2,1,0:T(8,128)(2,1)S(1)}, bf16[9,64,256]{2,1,0:T(8,128)(2,1)S(1)}, u32[]{:S(2)}, u32[]{:S(2)}) %collective-permute-start.4) | collective-permute-done | bytes 294944 | tf_op jit(solution)/shard_map/ppermute | solution.py:292
  52.5 0.1 merge.1
  52.6 15.0 %all_to_all.10.got = bf16[8,64,512]{2,1,0:T(8,128)(2,1)S(1)} all-to-all(bf16[8,64,512]{2,1,0:T(8,128)(2,1)S(1)} %merge.1), channel_id=1, replica_groups=mesh['y'=4,'z_hi'=2,'z_far'=4,'z_near'=2,'x'=4,'core'=2] {'z_near','x'}, dimensions={0} | all-to-all | bytes 1048576 | tf_op jit(solution)/shard_map/all_to_all | solution.py:293
  67.6 0.3 middle.1
  67.9 14.0 %all_to_all.11.got = bf16[4,64,128]{2,1,0:T(8,128)(2,1)S(1)} all-to-all(bf16[4,64,128]{2,1,0:T(8,128)(2,1)S(1)} %middle.1), channel_id=1, replica_groups=mesh['y'=4,'z_hi'=2,'z_far'=4,'z_near'=2,'x'=4,'core'=2] {'z_far'}, dimensions={0} | all-to-all | bytes 131072 | tf_op jit(solution)/shard_map/all_to_all | solution.py:294
  81.9 0.6 final.1
Async XLA Ops:
  0.6 42.1 %copy-start = (bf16[4096,256]{1,0:T(8,128)(2,1)S(1)}, bf16[4096,256]{1,0:T(8,128)(2,1)}, u32[]{:S(2)}) copy-start(bf16[4096,256]{1,0:T(8,128)(2,1)} %basis.1) | copy-start | bytes 6291460
  0.6 42.1 %copy-start.1 = (bf16[128,4096]{1,0:T(8,128)(2,1)S(1)}, bf16[128,4096]{1,0:T(8,128)(2,1)}, u32[]{:S(2)}) copy-start(bf16[128,4096]{1,0:T(8,128)(2,1)} %emb.1) | copy-start | bytes 3145732
  0.7 42.1 %copy-start.2 = (bf16[128,256]{1,0:T(8,128)(2,1)S(1)}, bf16[128,256]{1,0:T(8,128)(2,1)}, u32[]{:S(2)}) copy-start(bf16[128,256]{1,0:T(8,128)(2,1)} %cotangent.1) | copy-start | bytes 196612
  0.7 42.1 %copy-start.3 = (f32[1,4096]{1,0:T(1,128)S(1)}, f32[1,4096]{1,0:T(1,128)}, u32[]{:S(2)}) copy-start(f32[1,4096]{1,0:T(1,128)} %gain.1) | copy-start | bytes 49156
  4.2 26.4 %collective-permute-start.3 = (bf16[64,384]{1,0:T(8,128)(2,1)S(1)}, bf16[64,384]{1,0:T(8,128)(2,1)S(1)}, u32[]{:S(2)}, u32[]{:S(2)}) collective-permute-start(bf16[64,384]{1,0:T(8,128)(2,1)S(1)} %get-tuple-element.10), channel_id=1, source_target_pairs={{0,64},{64,0},{1,65},{65,1},{2,66},{66,2},{3,67},{67,3},{4,68},{68... | collective-permute-start | bytes 147464 | tf_op jit(solution)/shard_map/ppermute | solution.py:287
  19.9 22.8 %collective-permute-start.2 = (bf16[128,384]{1,0:T(8,128)(2,1)S(1)}, bf16[128,384]{1,0:T(8,128)(2,1)S(1)}, u32[]{:S(2)}, u32[]{:S(2)}) collective-permute-start(bf16[128,384]{1,0:T(8,128)(2,1)S(1)} %get-tuple-element.9.own0), channel_id=1, source_target_pairs={{0,384},{128,0},{256,128},{384,256},{1,385},{129,1},{257,129},{385... | collective-permute-start | bytes 294920 | tf_op jit(solution)/shard_map/ppermute | solution.py:288
  22.3 20.5 %collective-permute-start.1 = (bf16[128,384]{1,0:T(8,128)(2,1)S(1)}, bf16[128,384]{1,0:T(8,128)(2,1)S(1)}, u32[]{:S(2)}, u32[]{:S(2)}) collective-permute-start(bf16[128,384]{1,0:T(8,128)(2,1)S(1)} %get-tuple-element.9.own0), channel_id=1, source_target_pairs={{0,256},{128,384},{256,0},{384,128},{1,257},{129,385},{257,1},{385... | collective-permute-start | bytes 294920 | tf_op jit(solution)/shard_map/ppermute | solution.py:288
  26.8 16.0 %collective-permute-start = (bf16[128,384]{1,0:T(8,128)(2,1)S(1)}, bf16[128,384]{1,0:T(8,128)(2,1)S(1)}, u32[]{:S(2)}, u32[]{:S(2)}) collective-permute-start(bf16[128,384]{1,0:T(8,128)(2,1)S(1)} %get-tuple-element.9.own0), channel_id=1, source_target_pairs={{0,128},{128,256},{256,384},{384,0},{1,129},{129,257},{257,385},{3... | collective-permute-start | bytes 294920 | tf_op jit(solution)/shard_map/ppermute | solution.py:288
  49.0 3.5 %collective-permute-start.4 = (bf16[9,64,256]{2,1,0:T(8,128)(2,1)S(1)}, bf16[9,64,256]{2,1,0:T(8,128)(2,1)S(1)}, u32[]{:S(2)}, u32[]{:S(2)}) collective-permute-start(bf16[9,64,256]{2,1,0:T(8,128)(2,1)S(1)} %get-tuple-element.15), channel_id=1, source_target_pairs={{0,1},{1,0},{2,3},{3,2},{4,5},{5,4},{6,7},{7,6},{8,9},{9,8},{10,11... | collective-permute-start | bytes 884744 | tf_op jit(solution)/shard_map/ppermute | solution.py:292

commit v6 on v5

--- a/solution.py
+++ b/solution.py
@@ -26,7 +26,7 @@
 
 def project_kernel(
     chunk, emb_hbm, basis_hbm, down_hbm, up_hbm, gain_hbm,
-    block, part, emb_basis, norm, emb, basis, down, up, gain, sems,
+    part, emb_basis, norm, emb, basis, down, up, gain, sems,
 ):
     rows, width = emb.shape
     steps = width // chunk
@@ -62,15 +62,11 @@
         for k in range(0, chunk, 128):
             square = square + sq[:, k : k + 128]
     emb_basis[...] = acc[:rows, :].T
-    high = acc_pre.astype(BF16)
-    block[:, :256] = acc[rows:, :].astype(BF16)
-    block[:, 256:320] = high
-    block[:, 320:384] = (acc_pre - high.astype(F32)).astype(BF16)
     first = lax.axis_index("core") == 0
     weights = jnp.where(first, acc[rows : rows + 64, :], acc[rows + 64 :, :])
     part[:, :256] = weights.astype(BF16)
-    part[:, 256:320] = high[:64]
-    part[:, 320:384] = high[64:]
+    part[:, 256:320] = acc_pre[:64].astype(BF16)
+    part[:, 320:384] = acc_pre[64:].astype(BF16)
     norm[...] = jnp.sum(square.T, axis=0, keepdims=True)
 
 
@@ -78,16 +74,15 @@
     rows, width = embeds.shape
     rank = basis.shape[1]
     inner = down_t.shape[0]
-    chunk = 512
+    chunk = 1024
     hbm = pl.BlockSpec(memory_space=pltpu.HBM)
     vmem = pl.BlockSpec(memory_space=pltpu.VMEM)
     args = [pltpu.with_memory_space_constraint(a, pltpu.HBM) for a in (embeds, basis, down_t, up_t, gain)]
     return pl.pallas_call(
         functools.partial(project_kernel, chunk),
         in_specs=[hbm] * 5,
-        out_specs=[vmem] * 4,
+        out_specs=[vmem] * 3,
         out_shape=[
-            jax.ShapeDtypeStruct((2 * inner, rank + 2 * inner), BF16),
             jax.ShapeDtypeStruct((inner, rank + 2 * inner), BF16),
             jax.ShapeDtypeStruct((rank, rows), F32),
             jax.ShapeDtypeStruct((1, rows), F32),
@@ -105,8 +100,22 @@
     )(*args)
 
 
+def join_kernel(part, crossed, out):
+    out[0] = part[...]
+    out[1] = crossed[...]
+
+
+def join(part, crossed):
+    return pl.pallas_call(
+        join_kernel,
+        out_shape=jax.ShapeDtypeStruct((2,) + part.shape, part.dtype),
+        compiler_params=pltpu.CompilerParams(vmem_limit_bytes=4 * 1024 * 1024),
+        name="join",
+    )(part, crossed)
+
+
 def chain_kernel(
-    own0, own1, own2, own3, other, norm, emb_basis, cotangent, emb, basis, gain,
+    every, norm, emb_basis, cotangent, emb, basis, gain,
     coefs_hbm, kept, sent,
     weights, turned, pre_emb, c_kept, g_kept, p_kept, a_kept, pre_kept, slope_kept, coefs, coefs_sem,
 ):
@@ -117,16 +126,13 @@
     core = lax.axis_index("core")
     y = lax.axis_index("y")
     me = 2 * y + half
-    for k, block in enumerate((own0, own1, own2, own3)):
-        s = 2 * lax.rem(y + 4 - k, 4) + half
-        weights[s] = block[:, :256]
-        pre_emb[s] = (block[:, 256:320].astype(F32) + block[:, 320:384].astype(F32)).T
     for k in range(count // 2):
-        s = 2 * k + 1 - half
-        weights[s, :inner] = other[k, 0, :, :256]
-        weights[s, inner:] = other[k, 1, :, :256]
-        mine = other[k, core, :, 256:384].astype(F32).T
-        pre_emb[s] = jnp.concatenate([mine[:64], mine[64:]], axis=1)
+        for side in range(2):
+            s = 2 * k + (1 - half if side else half)
+            weights[s, :inner] = every[k, 0, side, :, :256]
+            weights[s, inner:] = every[k, 1, side, :, :256]
+            mine = every[k, core, side, :, 256:384].astype(F32).T
+            pre_emb[s] = jnp.concatenate([mine[:64], mine[64:]], axis=1)
     for s in range(count):
         turned[s] = weights[s].T
 
@@ -193,15 +199,15 @@
     coefs_copy.wait()
 
 
-def chain(own, other, norm, emb_basis, cotangent, embeds, basis, gain):
-    count = 2 * len(own)
+def chain(every, norm, emb_basis, cotangent, embeds, basis, gain):
+    count = 2 * every.shape[0]
     rows, rank = cotangent.shape
     inner = 64
     hbm = pl.BlockSpec(memory_space=pltpu.HBM)
     vmem = pl.BlockSpec(memory_space=pltpu.VMEM)
     return pl.pallas_call(
         chain_kernel,
-        in_specs=[vmem] * 11,
+        in_specs=[vmem] * 7,
         out_specs=[hbm, vmem, vmem],
         out_shape=[
             pltpu.HBM((rows, rank), BF16),
@@ -223,7 +229,7 @@
         ],
         compiler_params=pltpu.CompilerParams(vmem_limit_bytes=32 * 1024 * 1024),
         name="chain",
-    )(*own, other, norm, emb_basis, cotangent, embeds, basis, gain)
+    )(every, norm, emb_basis, cotangent, embeds, basis, gain)
 
 
 def merge_kernel(kept, got, out):
@@ -281,14 +287,13 @@
 
 
 def local(embeds, shared_basis, down_proj, up_proj, norm_gain, coef_grad):
-    block, part, emb_basis, norm = project(
+    part, emb_basis, norm = project(
         embeds, shared_basis, down_proj[0].T, up_proj[0].T, norm_gain
     )
     crossed = lax.ppermute(part, "z_hi", [(0, 1), (1, 0)])
-    own = [block] + [lax.ppermute(block, "y", [(i, (i + k) % 4) for i in range(4)]) for k in (1, 2, 3)]
-    other = lax.all_gather(crossed, ("y", "core"), tiled=False)
-    other = other.reshape((4, 2) + part.shape)
-    coefs, kept, sent = chain(own, other, norm, emb_basis, coef_grad, embeds, shared_basis, norm_gain)
+    every = lax.all_gather(join(part, crossed), ("y", "core"), tiled=False)
+    every = every.reshape((4, 2, 2) + part.shape)
+    coefs, kept, sent = chain(every, norm, emb_basis, coef_grad, embeds, shared_basis, norm_gain)
     got = lax.ppermute(sent, "core", [(0, 1), (1, 0)])
     got = lax.all_to_all(merge(kept, got), ("z_near", "x"), 0, 0, tiled=True)
     got = lax.all_to_all(middle(got, shared_basis), "z_far", 0, 0, tiled=True)

time: 82.8 us -> 80.2 us (0.969)
  starting transfers between devices: 28.6 us -> 18 us
  blocking collectives: 41.2 us -> 46.8 us
  waiting for transfers between devices: 1.23 us -> 4.14 us
    ppermute x3 -> x0, starting transfers between devices: 10.7 us -> none  [local(): lax.ppermute(block, 'y', [(i, (i + k) % 4) for i in range(4)])]
    all_to_all x1, blocking collectives: 14 us -> 17.9 us  [local(): got = lax.all_to_all(middle(got, shared_basis), 'z_far', 0, 0, tiled=True)]
    ppermute x1, waiting for transfers between devices: 0.01 us -> 2.93 us  [local(): crossed = lax.ppermute(part, 'z_hi', [(0, 1), (1, 0)])]
    all_gather x1, blocking collectives: 12.1 us -> 13.7 us  [local(): every = lax.all_gather(join(part, crossed), ('y', 'core'), tiled=False)]
    pallas_call x1 -> x2, Pallas kernels: 6.19 us -> 6.03 us  [the longest x1 6.02 us: chain(): pl.pallas_call(chain_kernel, in_specs=[vmem] * 7, out_specs=[hbm, vmem, v...]
  transfers between devices with their start and end apart: 5 -> 2, of which waited for: 1 -> 2; matrix products, arithmetic and copies ran while one was open for 0% -> 0% of each run, Pallas kernels for 0% -> 0%
where the time goes in v6:
time: 80.2 us; the launch traced here: 80 us
  blocking collectives  46.8 us (58%)
  starting transfers between devices  18 us (22%)
  Pallas kernels  10.3 us (13%)
  waiting for transfers between devices  4.14 us (5%)
    all_to_all x1, blocking collectives, local(): got = lax.all_to_all(middle(got, shared_basis), 'z_far', 0, 0, tiled=True)  17.9 us
    ppermute x1, starting transfers between devices, local(): crossed = lax.ppermute(part, 'z_hi', [(0, 1), (1, 0)])  15.7 us
    all_to_all x1, blocking collectives, local(): got = lax.all_to_all(merge(kept, got), ('z_near', 'x'), 0, 0, tiled=True)  15.2 us
    all_gather x1, blocking collectives, local(): every = lax.all_gather(join(part, crossed), ('y', 'core'), tiled=False)  13.7 us
    pallas_call x1, Pallas kernels, chain(): pl.pallas_call(chain_kernel, in_specs=[vmem] * 7, out_specs=[hbm, vmem, v...  6.02 us
    pallas_call x1, Pallas kernels, project(): pl.pallas_call(functools.partial(project_kernel, chunk), in_specs=[hbm] *...  3.32 us
    ppermute x1, waiting for transfers between devices, local(): crossed = lax.ppermute(part, 'z_hi', [(0, 1), (1, 0)])  2.93 us
    ppermute x1, starting transfers between devices, local(): got = lax.ppermute(sent, 'core', [(0, 1), (1, 0)])  2.26 us
  transfers between devices with their start and end apart: 2, of which 2 were waited for; matrix products, arithmetic and copies ran while one was open for 0% of the time, Pallas kernels for 0%

profile of v6, /device:TPU:8, one launch (start us, length us, event | category | flops | bytes accessed | tf_op | source)
XLA Modules:
  0.0 80.0 jit_solution(4745796684288976234)
XLA Ops:
  0.6 0.0 copy-start
  0.6 0.0 copy-start.1
  0.7 0.0 copy-start.2
  0.7 0.0 copy-start.3
  0.7 3.3 %project.1 = (bf16[64,384]{1,0:T(8,128)(2,1)S(1)}, f32[256,128]{1,0:T(8,128)S(1)}, f32[1,128]{1,0:T(1,128)S(1)}) custom-call(bf16[128,4096]{1,0:T(8,128)(2,1)} %emb.1, bf16[4096,256]{1,0:T(8,128)(2,1)} %basis.1, bf16[64,4096]{1,0:T(8,128)(2,1)} %bitcast.12, bf16[64,4096]{1,0:T(8,128)(2,1)} %bitcast.13, f32[1,4096]{1,0:T(1,128)} %gain.1), custom_call_target="tpu_custom_call" | custom-call | tf_op jit(solution)/shard_map/project/pallas_call | solution.py:81
  4.0 15.7 %collective-permute-start = (bf16[64,384]{1,0:T(8,128)(2,1)S(1)}, bf16[64,384]{1,0:T(8,128)(2,1)S(1)}, u32[]{:S(2)}, u32[]{:S(2)}) collective-permute-start(bf16[64,384]{1,0:T(8,128)(2,1)S(1)} %get-tuple-element.8.part), channel_id=1, source_target_pairs={{0,64},{64,0},{1,65},{65,1},{2,66},{66,2},{3,67},{67,3},{4,68},{68... | collective-permute-start | bytes 147464 | tf_op jit(solution)/shard_map/ppermute | solution.py:293
  19.7 2.9 %collective-permute-done.crossed = bf16[64,384]{1,0:T(8,128)(2,1)S(1)} collective-permute-done((bf16[64,384]{1,0:T(8,128)(2,1)S(1)}, bf16[64,384]{1,0:T(8,128)(2,1)S(1)}, u32[]{:S(2)}, u32[]{:S(2)}) %collective-permute-start) | collective-permute-done | bytes 49184 | tf_op jit(solution)/shard_map/ppermute | solution.py:293
  22.7 13.7 %all-gather = bf16[16,64,384]{2,1,0:T(8,128)(2,1)S(1)} all-gather(bf16[2,64,384]{2,1,0:T(8,128)(2,1)S(1)} %join.1), channel_id=2, replica_groups=mesh['y'=4,'z_hi'=2,'z_far'=4,'z_near'=2,'x'=4,'core'=2] {'y','core'}, dimensions={0}, use_global_device_ids=true | all-gather | bytes 884736 | tf_op jit(solution)/shard_map/all_gather | solution.py:294
  36.4 0.0 copy-done
  36.4 0.0 copy-done.1
  36.4 0.0 copy-done.2
  36.4 0.0 copy-done.3
  36.4 6.0 %chain.1 = (bf16[128,256]{1,0:T(8,128)(2,1)}, f32[9,64,256]{2,1,0:T(8,128)S(1)}, bf16[9,64,256]{2,1,0:T(8,128)(2,1)S(1)}) custom-call(bf16[4,2,2,64,384]{4,3,2,1,0:T(8,128)(2,1)S(1)} %bitcast.11, f32[1,128]{1,0:T(1,128)S(1)} %get-tuple-element.9.norm, f32[256,128]{1,0:T(8,128)S(1)} %get-tuple-element.10.emb_basis, bf16[128,256]{1,0:T(8,128)(2,1)S(1)} %copy-done.2, ...), custom_call_target="tpu_custom_call" | custom-call | tf_op jit(solution)/shard_map/chain/pallas_call | solution.py:208
  42.4 2.3 %collective-permute-start.1 = (bf16[9,64,256]{2,1,0:T(8,128)(2,1)S(1)}, bf16[9,64,256]{2,1,0:T(8,128)(2,1)S(1)}, u32[]{:S(2)}, u32[]{:S(2)}) collective-permute-start(bf16[9,64,256]{2,1,0:T(8,128)(2,1)S(1)} %get-tuple-element.13), channel_id=1, source_target_pairs={{0,1},{1,0},{2,3},{3,2},{4,5},{5,4},{6,7},{7,6},{8,9},{9,8},{10,11... | collective-permute-start | bytes 884744 | tf_op jit(solution)/shard_map/ppermute | solution.py:297
  44.7 1.2 %collective-permute-done.1.got = bf16[9,64,256]{2,1,0:T(8,128)(2,1)S(1)} collective-permute-done((bf16[9,64,256]{2,1,0:T(8,128)(2,1)S(1)}, bf16[9,64,256]{2,1,0:T(8,128)(2,1)S(1)}, u32[]{:S(2)}, u32[]{:S(2)}) %collective-permute-start.1) | collective-permute-done | bytes 294944 | tf_op jit(solution)/shard_map/ppermute | solution.py:297
  45.9 0.1 merge.1
  46.0 15.2 %all_to_all.10.got = bf16[8,64,512]{2,1,0:T(8,128)(2,1)S(1)} all-to-all(bf16[8,64,512]{2,1,0:T(8,128)(2,1)S(1)} %merge.1), channel_id=1, replica_groups=mesh['y'=4,'z_hi'=2,'z_far'=4,'z_near'=2,'x'=4,'core'=2] {'z_near','x'}, dimensions={0} | all-to-all | bytes 1048576 | tf_op jit(solution)/shard_map/all_to_all | solution.py:298
  61.2 0.3 middle.1
  61.5 17.9 %all_to_all.11.got = bf16[4,64,128]{2,1,0:T(8,128)(2,1)S(1)} all-to-all(bf16[4,64,128]{2,1,0:T(8,128)(2,1)S(1)} %middle.1), channel_id=1, replica_groups=mesh['y'=4,'z_hi'=2,'z_far'=4,'z_near'=2,'x'=4,'core'=2] {'z_far'}, dimensions={0} | all-to-all | bytes 131072 | tf_op jit(solution)/shard_map/all_to_all | solution.py:299
  79.4 0.6 final.1
  (1 shorter events, 0.0 us)
Async XLA Ops:
  0.6 35.7 %copy-start = (bf16[4096,256]{1,0:T(8,128)(2,1)S(1)}, bf16[4096,256]{1,0:T(8,128)(2,1)}, u32[]{:S(2)}) copy-start(bf16[4096,256]{1,0:T(8,128)(2,1)} %basis.1) | copy-start | bytes 6291460
  0.6 35.7 %copy-start.1 = (bf16[128,4096]{1,0:T(8,128)(2,1)S(1)}, bf16[128,4096]{1,0:T(8,128)(2,1)}, u32[]{:S(2)}) copy-start(bf16[128,4096]{1,0:T(8,128)(2,1)} %emb.1) | copy-start | bytes 3145732
  0.7 35.7 %copy-start.2 = (bf16[128,256]{1,0:T(8,128)(2,1)S(1)}, bf16[128,256]{1,0:T(8,128)(2,1)}, u32[]{:S(2)}) copy-start(bf16[128,256]{1,0:T(8,128)(2,1)} %cotangent.1) | copy-start | bytes 196612
  0.7 35.7 %copy-start.3 = (f32[1,4096]{1,0:T(1,128)S(1)}, f32[1,4096]{1,0:T(1,128)}, u32[]{:S(2)}) copy-start(f32[1,4096]{1,0:T(1,128)} %gain.1) | copy-start | bytes 49156
  4.0 18.7 %collective-permute-start = (bf16[64,384]{1,0:T(8,128)(2,1)S(1)}, bf16[64,384]{1,0:T(8,128)(2,1)S(1)}, u32[]{:S(2)}, u32[]{:S(2)}) collective-permute-start(bf16[64,384]{1,0:T(8,128)(2,1)S(1)} %get-tuple-element.8.part), channel_id=1, source_target_pairs={{0,64},{64,0},{1,65},{65,1},{2,66},{66,2},{3,67},{67,3},{4,68},{68... | collective-permute-start | bytes 147464 | tf_op jit(solution)/shard_map/ppermute | solution.py:293
  42.4 3.5 %collective-permute-start.1 = (bf16[9,64,256]{2,1,0:T(8,128)(2,1)S(1)}, bf16[9,64,256]{2,1,0:T(8,128)(2,1)S(1)}, u32[]{:S(2)}, u32[]{:S(2)}) collective-permute-start(bf16[9,64,256]{2,1,0:T(8,128)(2,1)S(1)} %get-tuple-element.13), channel_id=1, source_target_pairs={{0,1},{1,0},{2,3},{3,2},{4,5},{5,4},{6,7},{7,6},{8,9},{9,8},{10,11... | collective-permute-start | bytes 884744 | tf_op jit(solution)/shard_map/ppermute | solution.py:297

commit v7 on v6

--- a/solution.py
+++ b/solution.py
@@ -26,9 +26,10 @@
 
 def project_kernel(
     chunk, emb_hbm, basis_hbm, down_hbm, up_hbm, gain_hbm,
-    part, emb_basis, norm, emb, basis, down, up, gain, sems,
+    part, emb, basis, down, up, gain, sems,
 ):
     rows, width = emb.shape
+    inner = down.shape[0]
     steps = width // chunk
     gain_copy = pltpu.make_async_copy(gain_hbm, gain, sems.at[4, 0])
     gain_copy.start()
@@ -45,29 +46,18 @@
             copy.start()
         copies.append(group)
     gain_copy.wait()
-    acc = jnp.zeros((rows + 128, basis.shape[1]), F32)
-    acc_pre = jnp.zeros((rows, 64), F32)
-    square = jnp.zeros((rows, 128), F32)
+    acc = jnp.zeros((2 * inner, basis.shape[1]), F32)
+    pre = jnp.zeros((inner, rows), F32)
     for i in range(steps):
         at = slice(i * chunk, (i + 1) * chunk)
         for copy in copies[i]:
             copy.wait()
-        e = emb[:, at]
         scaled = (down[:, at].astype(F32) * gain[:, at]).astype(BF16)
-        stacked = jnp.concatenate([e, scaled, up[:, at]], axis=0)
-        acc = acc + dot(stacked, basis[at, :])
-        acc_pre = acc_pre + dot(e, scaled, NT)
-        ef = e.astype(F32)
-        sq = ef * ef
-        for k in range(0, chunk, 128):
-            square = square + sq[:, k : k + 128]
-    emb_basis[...] = acc[:rows, :].T
+        acc = acc + dot(jnp.concatenate([scaled, up[:, at]], axis=0), basis[at, :])
+        pre = pre + dot(scaled, emb[:, at], NT)
     first = lax.axis_index("core") == 0
-    weights = jnp.where(first, acc[rows : rows + 64, :], acc[rows + 64 :, :])
-    part[:, :256] = weights.astype(BF16)
-    part[:, 256:320] = acc_pre[:64].astype(BF16)
-    part[:, 320:384] = acc_pre[64:].astype(BF16)
-    norm[...] = jnp.sum(square.T, axis=0, keepdims=True)
+    part[:, :256] = jnp.where(first, acc[:inner], acc[inner:]).astype(BF16)
+    part[:, 256:] = pre.astype(BF16)
 
 
 def project(embeds, basis, down_t, up_t, gain):
@@ -75,18 +65,12 @@
     rank = basis.shape[1]
     inner = down_t.shape[0]
     chunk = 1024
-    hbm = pl.BlockSpec(memory_space=pltpu.HBM)
-    vmem = pl.BlockSpec(memory_space=pltpu.VMEM)
     args = [pltpu.with_memory_space_constraint(a, pltpu.HBM) for a in (embeds, basis, down_t, up_t, gain)]
     return pl.pallas_call(
         functools.partial(project_kernel, chunk),
-        in_specs=[hbm] * 5,
-        out_specs=[vmem] * 3,
-        out_shape=[
-            jax.ShapeDtypeStruct((inner, rank + 2 * inner), BF16),
-            jax.ShapeDtypeStruct((rank, rows), F32),
-            jax.ShapeDtypeStruct((1, rows), F32),
-        ],
+        in_specs=[pl.BlockSpec(memory_space=pltpu.HBM)] * 5,
+        out_specs=pl.BlockSpec(memory_space=pltpu.VMEM),
+        out_shape=jax.ShapeDtypeStruct((inner, rank + rows), BF16),
         scratch_shapes=[
             pltpu.VMEM((rows, width), BF16),
             pltpu.VMEM((width, rank), BF16),
@@ -100,6 +84,39 @@
     )(*args)
 
 
+def embed_kernel(emb, basis, emb_basis, norm):
+    rows, width = emb.shape
+    chunk = 1024
+    acc = jnp.zeros((rows, basis.shape[1]), F32)
+    square = jnp.zeros((rows, 128), F32)
+    for at in range(0, width, chunk):
+        e = emb[:, at : at + chunk]
+        acc = acc + dot(e, basis[at : at + chunk, :])
+        ef = e.astype(F32)
+        sq = ef * ef
+        for k in range(0, chunk, 128):
+            square = square + sq[:, k : k + 128]
+    emb_basis[...] = acc.T
+    norm[...] = jnp.sum(square.T, axis=0, keepdims=True)
+
+
+def embed(embeds, basis):
+    rows = embeds.shape[0]
+    rank = basis.shape[1]
+    vmem = pl.BlockSpec(memory_space=pltpu.VMEM)
+    return pl.pallas_call(
+        embed_kernel,
+        in_specs=[vmem] * 2,
+        out_specs=[vmem] * 2,
+        out_shape=[
+            jax.ShapeDtypeStruct((rank, rows), F32),
+            jax.ShapeDtypeStruct((1, rows), F32),
+        ],
+        compiler_params=pltpu.CompilerParams(vmem_limit_bytes=16 * 1024 * 1024),
+        name="embed",
+    )(embeds, basis)
+
+
 def join_kernel(part, crossed, out):
     out[0] = part[...]
     out[1] = crossed[...]
@@ -117,37 +134,49 @@
 def chain_kernel(
     every, norm, emb_basis, cotangent, emb, basis, gain,
     coefs_hbm, kept, sent,
-    weights, turned, pre_emb, c_kept, g_kept, p_kept, a_kept, pre_kept, slope_kept, coefs, coefs_sem,
+    turned, links, behind, c_kept, g_kept, p_kept, a_kept, pre_kept, slope_kept, coefs, coefs_sem,
 ):
-    count = weights.shape[0]
+    count = 2 * every.shape[0]
     width = emb.shape[1]
     inner = 64
     half = lax.axis_index("z_hi")
     core = lax.axis_index("core")
-    y = lax.axis_index("y")
-    me = 2 * y + half
-    for k in range(count // 2):
-        for side in range(2):
-            s = 2 * k + (1 - half if side else half)
-            weights[s, :inner] = every[k, 0, side, :, :256]
-            weights[s, inner:] = every[k, 1, side, :, :256]
-            mine = every[k, core, side, :, 256:384].astype(F32).T
-            pre_emb[s] = jnp.concatenate([mine[:64], mine[64:]], axis=1)
+    me = 2 * lax.axis_index("y") + half
+    sides = (half, 1 - half)
+
+    def down_of(s):
+        return every[s // 2, 0, sides[s % 2], :, :256]
+
+    def up_of(s):
+        return every[s // 2, 1, sides[s % 2], :, :256]
+
     for s in range(count):
-        turned[s] = weights[s].T
+        turned[s, 0] = down_of(s).T
+        turned[s, 1] = up_of(s).T
+    for s in range(1, count):
+        links[s, 0] = dot(down_of(s), up_of(s - 1), NT).astype(BF16)
+        links[s, 1] = dot(up_of(s - 1), down_of(s), NT).astype(BF16)
 
     eu = emb_basis[...]
     sq = norm[...]
     c = jnp.zeros(eu.shape, BF16)
     c_kept[0] = c
     invs = []
+    base = None
+    act = None
     for s in range(count):
         cf = c.astype(F32)
-        pre = pre_emb[s]
+        pre = every[s // 2, core, sides[s % 2], :, 256:].astype(F32)
         total = sq
         if s:
-            pre = pre + dot(weights[s, :inner], c)
-            total = total + jnp.sum(cf * (2.0 * eu + cf), axis=0, keepdims=True)
+            pre = pre + dot(links[s, 0], act)
+            if base is not None:
+                pre = pre + base
+            hid = eu + cf
+            total = total + jnp.sum(cf * (eu + hid), axis=0, keepdims=True)
+            behind[s] = dot(up_of(s - 1), hid.astype(BF16))
+            if s + 1 < count:
+                base = dot(down_of(s + 1), c)
         inv = lax.rsqrt(jnp.maximum(total, 0.0) * (1.0 / width) + EPS)
         invs.append(inv)
         pre = pre * inv
@@ -156,24 +185,26 @@
         pre_kept[s] = pre
         slope_kept[s] = sig * (1.0 + pre * (1.0 - sig))
         a_kept[s] = act
-        c = (cf + dot(turned[s, :, inner:], act)).astype(BF16)
+        c = (cf + dot(turned[s, 1], act)).astype(BF16)
         c_kept[s + 1] = c
     coefs[...] = c_kept[me + 1].T
     coefs_copy = pltpu.make_async_copy(coefs, coefs_hbm, coefs_sem)
     coefs_copy.start()
 
     g = cotangent[...].T
+    grad_act = dot(up_of(count - 1), g)
     for s in reversed(range(count)):
         g_kept[s] = g
         inv = invs[s]
-        gp = (dot(weights[s, inner:], g) * slope_kept[s]).astype(BF16)
+        gp = (grad_act * slope_kept[s]).astype(BF16)
         gpf = gp.astype(F32)
         p_kept[s] = (gpf * inv).astype(BF16)
         if s:
-            mean = jnp.sum(gpf * pre_kept[s], axis=0, keepdims=True) * (1.0 / width)
-            back = dot(turned[s, :, :inner], gp)
+            base = dot(up_of(s - 1), g)
+            pull = inv * inv * (jnp.sum(gpf * pre_kept[s], axis=0, keepdims=True) * (1.0 / width))
+            grad_act = base + inv * dot(links[s, 1], gp) - pull * behind[s]
             hid = eu + c_kept[s].astype(F32)
-            g = (g.astype(F32) + inv * back - (inv * inv * mean) * hid).astype(BF16)
+            g = (g.astype(F32) + inv * dot(turned[s, 0], gp) - pull * hid).astype(BF16)
 
     p_t = p_kept[me]
     cp = dot(p_t, c_kept[me], NT).astype(BF16)
@@ -215,8 +246,8 @@
             jax.ShapeDtypeStruct((9, inner, 256), BF16),
         ],
         scratch_shapes=[
-            pltpu.VMEM((count, 2 * inner, rank), BF16),
-            pltpu.VMEM((count, rank, 2 * inner), BF16),
+            pltpu.VMEM((count, 2, rank, inner), BF16),
+            pltpu.VMEM((count, 2, inner, inner), BF16),
             pltpu.VMEM((count, inner, rows), F32),
             pltpu.VMEM((count + 1, rank, rows), BF16),
             pltpu.VMEM((count, rank, rows), BF16),
@@ -287,10 +318,9 @@
 
 
 def local(embeds, shared_basis, down_proj, up_proj, norm_gain, coef_grad):
-    part, emb_basis, norm = project(
-        embeds, shared_basis, down_proj[0].T, up_proj[0].T, norm_gain
-    )
+    part = project(embeds, shared_basis, down_proj[0].T, up_proj[0].T, norm_gain)
     crossed = lax.ppermute(part, "z_hi", [(0, 1), (1, 0)])
+    emb_basis, norm = embed(embeds, shared_basis)
     every = lax.all_gather(join(part, crossed), ("y", "core"), tiled=False)
     every = every.reshape((4, 2, 2) + part.shape)
     coefs, kept, sent = chain(every, norm, emb_basis, coef_grad, embeds, shared_basis, norm_gain)

time: 80.2 us -> 78.4 us (0.978)
  Pallas kernels: 10.3 us -> 8.87 us
    pallas_call x1, Pallas kernels: 6.02 us -> 4.47 us  [chain(): pl.pallas_call(chain_kernel, in_specs=[vmem] * 7, out_specs=[hbm, vmem, v...]
    pallas_call x1 -> x2, Pallas kernels: 3.32 us -> 3.44 us  [the longest x1 2.85 us: project(): pl.pallas_call(functools.partial(project_kernel, chunk), in_specs=[pl.Blo...]
  transfers between devices with their start and end apart: 2 -> 2, of which waited for: 2 -> 2; matrix products, arithmetic and copies ran while one was open for 0% -> 0% of each run, Pallas kernels for 0% -> 1%
where the time goes in v7:
time: 78.4 us; the launch traced here: 78.1 us
  blocking collectives  46.8 us (60%)
  starting transfers between devices  18.1 us (23%)
  Pallas kernels  8.87 us (11%)
  waiting for transfers between devices  3.52 us (4%)
    all_to_all x1, blocking collectives, local(): got = lax.all_to_all(middle(got, shared_basis), 'z_far', 0, 0, tiled=True)  17.9 us
    ppermute x1, starting transfers between devices, local(): crossed = lax.ppermute(part, 'z_hi', [(0, 1), (1, 0)])  15.9 us
    all_to_all x1, blocking collectives, local(): got = lax.all_to_all(merge(kept, got), ('z_near', 'x'), 0, 0, tiled=True)  15.2 us
    all_gather x1, blocking collectives, local(): every = lax.all_gather(join(part, crossed), ('y', 'core'), tiled=False)  13.7 us
    pallas_call x1, Pallas kernels, chain(): pl.pallas_call(chain_kernel, in_specs=[vmem] * 7, out_specs=[hbm, vmem, v...  4.47 us
    pallas_call x1, Pallas kernels, project(): pl.pallas_call(functools.partial(project_kernel, chunk), in_specs=[pl.Blo...  2.85 us
    ppermute x1, waiting for transfers between devices, local(): crossed = lax.ppermute(part, 'z_hi', [(0, 1), (1, 0)])  2.31 us
    ppermute x1, starting transfers between devices, local(): got = lax.ppermute(sent, 'core', [(0, 1), (1, 0)])  2.26 us
  transfers between devices with their start and end apart: 2, of which 2 were waited for; matrix products, arithmetic and copies ran while one was open for 0% of the time, Pallas kernels for 1%

profile of v7, /device:TPU:8, one launch (start us, length us, event | category | flops | bytes accessed | tf_op | source)
XLA Modules:
  0.0 78.1 jit_solution(4092516807516115759)
XLA Ops:
  0.6 0.0 copy-start
  0.6 0.0 copy-start.1
  0.7 2.8 %project.1.part = bf16[64,384]{1,0:T(8,128)(2,1)S(1)} custom-call(bf16[128,4096]{1,0:T(8,128)(2,1)} %emb.3, bf16[4096,256]{1,0:T(8,128)(2,1)} %basis.3, bf16[64,4096]{1,0:T(8,128)(2,1)} %bitcast.12, bf16[64,4096]{1,0:T(8,128)(2,1)} %bitcast.13, f32[1,4096]{1,0:T(1,128)} %gain.1), custom_call_target="tpu_custom_call" | custom-call | tf_op jit(solution)/shard_map/project/pallas_call | solution.py:69
  3.5 0.0 copy-start.2
  3.5 0.0 copy-start.3
  3.5 15.9 %collective-permute-start = (bf16[64,384]{1,0:T(8,128)(2,1)S(1)}, bf16[64,384]{1,0:T(8,128)(2,1)S(1)}, u32[]{:S(2)}, u32[]{:S(2)}) collective-permute-start(bf16[64,384]{1,0:T(8,128)(2,1)S(1)} %project.1.part), channel_id=1, source_target_pairs={{0,64},{64,0},{1,65},{65,1},{2,66},{66,2},{3,67},{67,3},{4,68},{68... | collective-permute-start | bytes 147464 | tf_op jit(solution)/shard_map/ppermute | solution.py:322
  19.4 0.0 copy-done
  19.4 0.0 copy-done.1
  19.4 0.6 embed.1
  20.0 2.3 %collective-permute-done.crossed = bf16[64,384]{1,0:T(8,128)(2,1)S(1)} collective-permute-done((bf16[64,384]{1,0:T(8,128)(2,1)S(1)}, bf16[64,384]{1,0:T(8,128)(2,1)S(1)}, u32[]{:S(2)}, u32[]{:S(2)}) %collective-permute-start) | collective-permute-done | bytes 49184 | tf_op jit(solution)/shard_map/ppermute | solution.py:322
  22.3 13.7 %all-gather = bf16[16,64,384]{2,1,0:T(8,128)(2,1)S(1)} all-gather(bf16[2,64,384]{2,1,0:T(8,128)(2,1)S(1)} %join.1), channel_id=2, replica_groups=mesh['y'=4,'z_hi'=2,'z_far'=4,'z_near'=2,'x'=4,'core'=2] {'y','core'}, dimensions={0}, use_global_device_ids=true | all-gather | bytes 884736 | tf_op jit(solution)/shard_map/all_gather | solution.py:324
  36.0 0.0 copy-done.2
  36.0 0.0 copy-done.3
  36.0 4.5 %chain.1 = (bf16[128,256]{1,0:T(8,128)(2,1)}, f32[9,64,256]{2,1,0:T(8,128)S(1)}, bf16[9,64,256]{2,1,0:T(8,128)(2,1)S(1)}) custom-call(bf16[4,2,2,64,384]{4,3,2,1,0:T(8,128)(2,1)S(1)} %bitcast.11, f32[1,128]{1,0:T(1,128)S(1)} %get-tuple-element.7.norm, f32[256,128]{1,0:T(8,128)S(1)} %get-tuple-element.8.emb_basis, bf16[128,256]{1,0:T(8,128)(2,1)S(1)} %copy-done.2, ...), custom_call_target="tpu_custom_call" | custom-call | tf_op jit(solution)/shard_map/chain/pallas_call | solution.py:239
  40.5 2.3 %collective-permute-start.1 = (bf16[9,64,256]{2,1,0:T(8,128)(2,1)S(1)}, bf16[9,64,256]{2,1,0:T(8,128)(2,1)S(1)}, u32[]{:S(2)}, u32[]{:S(2)}) collective-permute-start(bf16[9,64,256]{2,1,0:T(8,128)(2,1)S(1)} %get-tuple-element.11), channel_id=1, source_target_pairs={{0,1},{1,0},{2,3},{3,2},{4,5},{5,4},{6,7},{7,6},{8,9},{9,8},{10,11... | collective-permute-start | bytes 884744 | tf_op jit(solution)/shard_map/ppermute | solution.py:327
  42.8 1.2 %collective-permute-done.1.got = bf16[9,64,256]{2,1,0:T(8,128)(2,1)S(1)} collective-permute-done((bf16[9,64,256]{2,1,0:T(8,128)(2,1)S(1)}, bf16[9,64,256]{2,1,0:T(8,128)(2,1)S(1)}, u32[]{:S(2)}, u32[]{:S(2)}) %collective-permute-start.1) | collective-permute-done | bytes 294944 | tf_op jit(solution)/shard_map/ppermute | solution.py:327
  44.0 0.1 merge.1
  44.1 15.2 %all_to_all.10.got = bf16[8,64,512]{2,1,0:T(8,128)(2,1)S(1)} all-to-all(bf16[8,64,512]{2,1,0:T(8,128)(2,1)S(1)} %merge.1), channel_id=1, replica_groups=mesh['y'=4,'z_hi'=2,'z_far'=4,'z_near'=2,'x'=4,'core'=2] {'z_near','x'}, dimensions={0} | all-to-all | bytes 1048576 | tf_op jit(solution)/shard_map/all_to_all | solution.py:328
  59.3 0.3 middle.1
  59.6 17.9 %all_to_all.11.got = bf16[4,64,128]{2,1,0:T(8,128)(2,1)S(1)} all-to-all(bf16[4,64,128]{2,1,0:T(8,128)(2,1)S(1)} %middle.1), channel_id=1, replica_groups=mesh['y'=4,'z_hi'=2,'z_far'=4,'z_near'=2,'x'=4,'core'=2] {'z_far'}, dimensions={0} | all-to-all | bytes 131072 | tf_op jit(solution)/shard_map/all_to_all | solution.py:329
  77.5 0.6 final.1
  (1 shorter events, 0.0 us)
Async XLA Ops:
  0.6 18.8 %copy-start = (bf16[4096,256]{1,0:T(8,128)(2,1)S(1)}, bf16[4096,256]{1,0:T(8,128)(2,1)}, u32[]{:S(2)}) copy-start(bf16[4096,256]{1,0:T(8,128)(2,1)} %basis.3) | copy-start | bytes 6291460
  0.6 18.8 %copy-start.1 = (bf16[128,4096]{1,0:T(8,128)(2,1)S(1)}, bf16[128,4096]{1,0:T(8,128)(2,1)}, u32[]{:S(2)}) copy-start(bf16[128,4096]{1,0:T(8,128)(2,1)} %emb.3) | copy-start | bytes 3145732
  3.5 32.5 %copy-start.2 = (bf16[128,256]{1,0:T(8,128)(2,1)S(1)}, bf16[128,256]{1,0:T(8,128)(2,1)}, u32[]{:S(2)}) copy-start(bf16[128,256]{1,0:T(8,128)(2,1)} %cotangent.1) | copy-start | bytes 196612
  3.5 32.5 %copy-start.3 = (f32[1,4096]{1,0:T(1,128)S(1)}, f32[1,4096]{1,0:T(1,128)}, u32[]{:S(2)}) copy-start(f32[1,4096]{1,0:T(1,128)} %gain.1) | copy-start | bytes 49156
  3.5 18.8 %collective-permute-start = (bf16[64,384]{1,0:T(8,128)(2,1)S(1)}, bf16[64,384]{1,0:T(8,128)(2,1)S(1)}, u32[]{:S(2)}, u32[]{:S(2)}) collective-permute-start(bf16[64,384]{1,0:T(8,128)(2,1)S(1)} %project.1.part), channel_id=1, source_target_pairs={{0,64},{64,0},{1,65},{65,1},{2,66},{66,2},{3,67},{67,3},{4,68},{68... | collective-permute-start | bytes 147464 | tf_op jit(solution)/shard_map/ppermute | solution.py:322
  40.5 3.5 %collective-permute-start.1 = (bf16[9,64,256]{2,1,0:T(8,128)(2,1)S(1)}, bf16[9,64,256]{2,1,0:T(8,128)(2,1)S(1)}, u32[]{:S(2)}, u32[]{:S(2)}) collective-permute-start(bf16[9,64,256]{2,1,0:T(8,128)(2,1)S(1)} %get-tuple-element.11), channel_id=1, source_target_pairs={{0,1},{1,0},{2,3},{3,2},{4,5},{5,4},{6,7},{7,6},{8,9},{9,8},{10,11... | collective-permute-start | bytes 884744 | tf_op jit(solution)/shard_map/ppermute | solution.py:327

commit v8 on v7

--- a/solution.py
+++ b/solution.py
@@ -84,7 +84,8 @@
     )(*args)
 
 
-def embed_kernel(emb, basis, emb_basis, norm):
+def embed_kernel(emb, basis, gain, cotangent, after, emb_basis, norm, mine, gain_mine, share_wide, share):
+    del after
     rows, width = emb.shape
     chunk = 1024
     acc = jnp.zeros((rows, basis.shape[1]), F32)
@@ -98,23 +99,54 @@
             square = square + sq[:, k : k + 128]
     emb_basis[...] = acc.T
     norm[...] = jnp.sum(square.T, axis=0, keepdims=True)
-
-
-def embed(embeds, basis):
-    rows = embeds.shape[0]
+    high = acc.astype(BF16)
+    share[:, 512:768] = high
+    share[:, 768:1024] = (acc - high.astype(F32)).astype(BF16)
+    share[:, 1024:1280] = cotangent[...]
+    total = jnp.broadcast_to(jnp.sum(square, axis=1, keepdims=True), (rows, 128))
+    first = total.astype(BF16).astype(F32)
+    second = (total - first).astype(BF16).astype(F32)
+    lane = lax.broadcasted_iota(jnp.int32, (rows, 128), 1)
+    parts = jnp.where(lane == 0, first, jnp.where(lane == 1, second, total - first - second))
+    share[:, 1280:1408] = parts.astype(BF16)
+    even = lax.axis_index("core") == 0
+    for j in range(8):
+        for q in range(2):
+            one = slice(2048 * q + j * 128, 2048 * q + j * 128 + 128)
+            two = slice(2048 * q + 1024 + j * 128, 2048 * q + 1024 + j * 128 + 128)
+            lanes = slice(j * 256 + q * 128, j * 256 + q * 128 + 128)
+            for source, target, rest in ((emb, mine, share), (gain, gain_mine, None)):
+                left = source[:, one].astype(F32)
+                right = source[:, two].astype(F32)
+                low = lax.broadcasted_iota(jnp.int32, left.shape, 1) < 64
+                zero = jnp.where(low, left, pltpu.roll(right, 64, 1))
+                other = jnp.where(low, pltpu.roll(left, 64, 1), right)
+                target[:, lanes] = jnp.where(even, zero, other).astype(target.dtype)
+                if rest is not None and j < 6:
+                    share_wide[:, lanes] = jnp.where(even, other, zero).astype(rest.dtype)
+                elif rest is not None:
+                    rest[:, lanes.start - 1536 : lanes.stop - 1536] = jnp.where(even, other, zero).astype(rest.dtype)
+
+
+def embed(embeds, basis, gain, cotangent, after):
+    rows, width = embeds.shape
     rank = basis.shape[1]
     vmem = pl.BlockSpec(memory_space=pltpu.VMEM)
     return pl.pallas_call(
         embed_kernel,
-        in_specs=[vmem] * 2,
-        out_specs=[vmem] * 2,
+        in_specs=[vmem] * 4 + [pl.BlockSpec(memory_space=pl.ANY)],
+        out_specs=[vmem] * 6,
         out_shape=[
             jax.ShapeDtypeStruct((rank, rows), F32),
             jax.ShapeDtypeStruct((1, rows), F32),
+            jax.ShapeDtypeStruct((rows, width // 2), BF16),
+            jax.ShapeDtypeStruct((1, width // 2), F32),
+            jax.ShapeDtypeStruct((rows, 1536), BF16),
+            jax.ShapeDtypeStruct((rows, width // 2 - 1536 + 3 * rank + 128), BF16),
         ],
         compiler_params=pltpu.CompilerParams(vmem_limit_bytes=16 * 1024 * 1024),
         name="embed",
-    )(embeds, basis)
+    )(embeds, basis, gain, cotangent, after)
 
 
 def join_kernel(part, crossed, out):
@@ -132,12 +164,12 @@
 
 
 def chain_kernel(
-    every, norm, emb_basis, cotangent, emb, basis, gain,
-    coefs_hbm, kept, sent,
+    every, norm, emb_basis, cotangent, mine, basis, gain, share_wide, share,
+    coefs_hbm, slots,
     turned, links, behind, c_kept, g_kept, p_kept, a_kept, pre_kept, slope_kept, coefs, coefs_sem,
 ):
     count = 2 * every.shape[0]
-    width = emb.shape[1]
+    rows, width = mine.shape[0], 2 * mine.shape[1]
     inner = 64
     half = lax.axis_index("z_hi")
     core = lax.axis_index("core")
@@ -157,8 +189,10 @@
         links[s, 0] = dot(down_of(s), up_of(s - 1), NT).astype(BF16)
         links[s, 1] = dot(up_of(s - 1), down_of(s), NT).astype(BF16)
 
-    eu = emb_basis[...]
-    sq = norm[...]
+    theirs = (share[:, 512:768].astype(F32) + share[:, 768:1024].astype(F32)).T
+    parts = share[:, 1280:1408].astype(F32).T
+    eu = jnp.concatenate([emb_basis[...], theirs], axis=1)
+    sq = jnp.concatenate([norm[...], parts[0:1] + parts[1:2] + parts[2:3]], axis=1)
     c = jnp.zeros(eu.shape, BF16)
     c_kept[0] = c
     invs = []
@@ -166,7 +200,9 @@
     act = None
     for s in range(count):
         cf = c.astype(F32)
-        pre = every[s // 2, core, sides[s % 2], :, 256:].astype(F32)
+        pre = jnp.concatenate(
+            [every[s // 2, k, sides[s % 2], :, 256:].astype(F32) for k in (core, 1 - core)], axis=1
+        )
         total = sq
         if s:
             pre = pre + dot(links[s, 0], act)
@@ -187,11 +223,11 @@
         a_kept[s] = act
         c = (cf + dot(turned[s, 1], act)).astype(BF16)
         c_kept[s + 1] = c
-    coefs[...] = c_kept[me + 1].T
+    coefs[...] = c_kept[me + 1, :, :rows].T
     coefs_copy = pltpu.make_async_copy(coefs, coefs_hbm, coefs_sem)
     coefs_copy.start()
 
-    g = cotangent[...].T
+    g = jnp.concatenate([cotangent[...].T, share[:, 1024:1280].T], axis=1)
     grad_act = dot(up_of(count - 1), g)
     for s in reversed(range(count)):
         g_kept[s] = g
@@ -208,75 +244,48 @@
 
     p_t = p_kept[me]
     cp = dot(p_t, c_kept[me], NT).astype(BF16)
-    s2 = dot(a_kept[me], g_kept[me], NT)
-    kept[8] = s2
-    sent[8] = s2.astype(BF16)
-    low = lax.broadcasted_iota(jnp.int32, (inner, 128), 1) < 64
-    first_core = core == 0
+    s2 = dot(a_kept[me], g_kept[me], NT).astype(BF16)
     for j in range(8):
-        spans = [slice(far * 1024 + j * 128, far * 1024 + j * 128 + 128) for far in range(4)]
-        tiles = jnp.concatenate([emb[:, at] for at in spans], axis=1)
-        rows = jnp.concatenate([basis[at, :] for at in spans], axis=0)
-        scale = jnp.concatenate([gain[:, at] for at in spans], axis=1)
-        grad = (dot(p_t, tiles) + dot(cp, rows, NT)) * scale
-        for q in range(2):
-            one = grad[:, 256 * q : 256 * q + 128]
-            two = grad[:, 256 * q + 128 : 256 * q + 256]
-            lanes = slice(q * 128, q * 128 + 128)
-            zero = jnp.where(low, one, pltpu.roll(two, 64, 1))
-            other_half = jnp.where(low, pltpu.roll(one, 64, 1), two)
-            kept[j, :, lanes] = jnp.where(first_core, zero, other_half)
-            sent[j, :, lanes] = jnp.where(first_core, other_half, zero).astype(BF16)
+        lanes = slice(j * 256, j * 256 + 256)
+        rest = share_wide[:, lanes] if j < 6 else share[:, j * 256 - 1536 : j * 256 - 1280]
+        tokens = jnp.concatenate([mine[:, lanes], rest], axis=0)
+        spans = jnp.concatenate([basis[far, j, core] for far in range(4)], axis=0)
+        slots[j, :, :256] = ((dot(p_t, tokens) + dot(cp, spans, NT)) * gain[:, lanes]).astype(BF16)
+        slots[j, :, 256:] = s2
     coefs_copy.wait()
 
 
-def chain(every, norm, emb_basis, cotangent, embeds, basis, gain):
+def chain(every, norm, emb_basis, cotangent, mine, basis, gain, share_wide, share):
     count = 2 * every.shape[0]
     rows, rank = cotangent.shape
+    tokens = 2 * rows
     inner = 64
     hbm = pl.BlockSpec(memory_space=pltpu.HBM)
     vmem = pl.BlockSpec(memory_space=pltpu.VMEM)
     return pl.pallas_call(
         chain_kernel,
-        in_specs=[vmem] * 7,
-        out_specs=[hbm, vmem, vmem],
+        in_specs=[vmem] * 9,
+        out_specs=[hbm, vmem],
         out_shape=[
             pltpu.HBM((rows, rank), BF16),
-            jax.ShapeDtypeStruct((9, inner, 256), F32),
-            jax.ShapeDtypeStruct((9, inner, 256), BF16),
+            jax.ShapeDtypeStruct((8, inner, 2 * rank), BF16),
         ],
         scratch_shapes=[
             pltpu.VMEM((count, 2, rank, inner), BF16),
             pltpu.VMEM((count, 2, inner, inner), BF16),
-            pltpu.VMEM((count, inner, rows), F32),
-            pltpu.VMEM((count + 1, rank, rows), BF16),
-            pltpu.VMEM((count, rank, rows), BF16),
-            pltpu.VMEM((count, inner, rows), BF16),
-            pltpu.VMEM((count, inner, rows), BF16),
-            pltpu.VMEM((count, inner, rows), F32),
-            pltpu.VMEM((count, inner, rows), F32),
+            pltpu.VMEM((count, inner, tokens), F32),
+            pltpu.VMEM((count + 1, rank, tokens), BF16),
+            pltpu.VMEM((count, rank, tokens), BF16),
+            pltpu.VMEM((count, inner, tokens), BF16),
+            pltpu.VMEM((count, inner, tokens), BF16),
+            pltpu.VMEM((count, inner, tokens), F32),
+            pltpu.VMEM((count, inner, tokens), F32),
             pltpu.VMEM((rows, rank), BF16),
             pltpu.SemaphoreType.DMA,
         ],
         compiler_params=pltpu.CompilerParams(vmem_limit_bytes=32 * 1024 * 1024),
         name="chain",
-    )(every, norm, emb_basis, cotangent, embeds, basis, gain)
-
-
-def merge_kernel(kept, got, out):
-    weights = (kept[8] + got[8].astype(F32)).astype(BF16)
-    for j in range(8):
-        out[j, :, :256] = (kept[j] + got[j].astype(F32)).astype(BF16)
-        out[j, :, 256:] = weights
-
-
-def merge(kept, got):
-    return pl.pallas_call(
-        merge_kernel,
-        out_shape=jax.ShapeDtypeStruct((8, 64, 512), BF16),
-        compiler_params=pltpu.CompilerParams(vmem_limit_bytes=8 * 1024 * 1024),
-        name="merge",
-    )(kept, got)
+    )(every, norm, emb_basis, cotangent, mine, basis.reshape(4, 8, 2, 64, 256), gain, share_wide, share)
 
 
 def middle_kernel(got, basis, out):
@@ -320,12 +329,13 @@
 def local(embeds, shared_basis, down_proj, up_proj, norm_gain, coef_grad):
     part = project(embeds, shared_basis, down_proj[0].T, up_proj[0].T, norm_gain)
     crossed = lax.ppermute(part, "z_hi", [(0, 1), (1, 0)])
-    emb_basis, norm = embed(embeds, shared_basis)
+    emb_basis, norm, mine, gain, share_wide, share = embed(embeds, shared_basis, norm_gain, coef_grad, part)
+    share_wide = lax.ppermute(share_wide, "core", [(0, 1), (1, 0)])
+    share = lax.ppermute(share, "core", [(0, 1), (1, 0)])
     every = lax.all_gather(join(part, crossed), ("y", "core"), tiled=False)
     every = every.reshape((4, 2, 2) + part.shape)
-    coefs, kept, sent = chain(every, norm, emb_basis, coef_grad, embeds, shared_basis, norm_gain)
-    got = lax.ppermute(sent, "core", [(0, 1), (1, 0)])
-    got = lax.all_to_all(merge(kept, got), ("z_near", "x"), 0, 0, tiled=True)
+    coefs, slots = chain(every, norm, emb_basis, coef_grad, mine, shared_basis, gain, share_wide, share)
+    got = lax.all_to_all(slots, ("z_near", "x"), 0, 0, tiled=True)
     got = lax.all_to_all(middle(got, shared_basis), "z_far", 0, 0, tiled=True)
     return coefs[None], final(got)[None]
 

time: 78.4 us -> 75 us (0.957)
  waiting for transfers between devices: 3.52 us -> 0.01 us
  blocking collectives: 46.8 us -> 44.4 us
  starting transfers between devices: 18.1 us -> 20 us
    ppermute x1, waiting for transfers between devices: 2.31 us -> 0.01 us  [local(): crossed = lax.ppermute(part, 'z_hi', [(0, 1), (1, 0)])]
    all_to_all x1, blocking collectives: 17.9 us -> 15.7 us  [local(): got = lax.all_to_all(middle(got, shared_basis), 'z_far', 0, 0, tiled=True)]
    ppermute x1 -> x2, starting transfers between devices: 2.26 us -> 4.32 us  [the longest x1 2.41 us: local(): share = lax.ppermute(share, 'core', [(0, 1), (1, 0)])]
    ppermute x1 -> x2, waiting for transfers between devices: 1.21 us -> 0.01 us  [the longest x1 0.01 us: local(): share = lax.ppermute(share, 'core', [(0, 1), (1, 0)])]
    pallas_call x3 -> x2, Pallas kernels: 5.11 us -> 5.71 us  [the longest x1 4.74 us: chain(): pl.pallas_call(chain_kernel, in_specs=[vmem] * 9, out_specs=[hbm, vmem],...]
  transfers between devices with their start and end apart: 2 -> 3, of which waited for: 2 -> 0; matrix products, arithmetic and copies ran while one was open for 0% -> 0% of each run, Pallas kernels for 1% -> 1%
where the time goes in v8:
time: 75 us; the launch traced here: 74.7 us
  blocking collectives  44.4 us (59%)
  starting transfers between devices  20 us (27%)
  Pallas kernels  9.48 us (13%)
  between operations  0.76 us (1%)
    ppermute x1, starting transfers between devices, local(): crossed = lax.ppermute(part, 'z_hi', [(0, 1), (1, 0)])  15.7 us
    all_to_all x1, blocking collectives, local(): got = lax.all_to_all(middle(got, shared_basis), 'z_far', 0, 0, tiled=True)  15.7 us
    all_to_all x1, blocking collectives, local(): got = lax.all_to_all(slots, ('z_near', 'x'), 0, 0, tiled=True)  15 us
    all_gather x1, blocking collectives, local(): every = lax.all_gather(join(part, crossed), ('y', 'core'), tiled=False)  13.7 us
    pallas_call x1, Pallas kernels, chain(): pl.pallas_call(chain_kernel, in_specs=[vmem] * 9, out_specs=[hbm, vmem],...  4.74 us
    pallas_call x1, Pallas kernels, project(): pl.pallas_call(functools.partial(project_kernel, chunk), in_specs=[pl.Blo...  2.85 us
    ppermute x1, starting transfers between devices, local(): share = lax.ppermute(share, 'core', [(0, 1), (1, 0)])  2.41 us
    ppermute x1, starting transfers between devices, local(): share_wide = lax.ppermute(share_wide, 'core', [(0, 1), (1, 0)])  1.91 us
  transfers between devices with their start and end apart: 3, of which 0 were waited for; matrix products, arithmetic and copies ran while one was open for 0% of the time, Pallas kernels for 1%

profile of v8, /device:TPU:8, one launch (start us, length us, event | category | flops | bytes accessed | tf_op | source)
XLA Modules:
  0.0 74.7 jit_solution(14876116820809184495)
XLA Ops:
  0.6 0.0 copy-start
  0.6 0.0 copy-start.1
  0.7 0.0 copy-start.2
  0.7 0.0 copy-start.3
  0.7 2.9 %project.1.part.after = bf16[64,384]{1,0:T(8,128)(2,1)S(1)} custom-call(bf16[128,4096]{1,0:T(8,128)(2,1)} %emb.1, bf16[4096,256]{1,0:T(8,128)(2,1)} %basis.1, bf16[64,4096]{1,0:T(8,128)(2,1)} %bitcast.13, bf16[64,4096]{1,0:T(8,128)(2,1)} %bitcast.14, f32[1,4096]{1,0:T(1,128)} %gain.1), custom_call_target="tpu_custom_call" | custom-call | tf_op jit(solution)/shard_map/project/pallas_call | solution.py:69
  3.5 15.7 %collective-permute-start = (bf16[64,384]{1,0:T(8,128)(2,1)S(1)}, bf16[64,384]{1,0:T(8,128)(2,1)S(1)}, u32[]{:S(2)}, u32[]{:S(2)}) collective-permute-start(bf16[64,384]{1,0:T(8,128)(2,1)S(1)} %project.1.part.after), channel_id=1, source_target_pairs={{0,64},{64,0},{1,65},{65,1},{2,66},{66,2},{3,67},{67,3},{4,68},{68... | collective-permute-start | bytes 147464 | tf_op jit(solution)/shard_map/ppermute | solution.py:331
  19.3 0.0 copy-done
  19.3 0.0 copy-done.1
  19.3 0.0 copy-done.2
  19.3 0.0 copy-done.3
  19.3 1.0 %embed.1 = (f32[256,128]{1,0:T(8,128)S(1)}, f32[1,128]{1,0:T(1,128)S(1)}, bf16[128,2048]{1,0:T(8,128)(2,1)S(1)}, f32[1,2048]{1,0:T(1,128)S(1)}, bf16[128,1536]{1...) custom-call(bf16[128,4096]{1,0:T(8,128)(2,1)S(1)} %copy-done.1, bf16[4096,256]{1,0:T(8,128)(2,1)S(1)} %copy-done, ...), custom_call_target="tpu_custom_call" | custom-call | tf_op jit(solution)/shard_map/embed/pallas_call | solution.py:135
  20.3 1.9 %collective-permute-start.1 = (bf16[128,1536]{1,0:T(8,128)(2,1)S(1)}, bf16[128,1536]{1,0:T(8,128)(2,1)S(1)}, u32[]{:S(2)}, u32[]{:S(2)}) collective-permute-start(bf16[128,1536]{1,0:T(8,128)(2,1)S(1)} %get-tuple-element.14), channel_id=1, source_target_pairs={{0,1},{1,0},{2,3},{3,2},{4,5},{5,4},{6,7},{7,6},{8,9},{9,8},{10,11... | collective-permute-start | bytes 1179656 | tf_op jit(solution)/shard_map/ppermute | solution.py:333
  22.2 2.4 %collective-permute-start.2 = (bf16[128,1408]{1,0:T(8,128)(2,1)S(1)}, bf16[128,1408]{1,0:T(8,128)(2,1)S(1)}, u32[]{:S(2)}, u32[]{:S(2)}) collective-permute-start(bf16[128,1408]{1,0:T(8,128)(2,1)S(1)} %get-tuple-element.15), channel_id=1, source_target_pairs={{0,1},{1,0},{2,3},{3,2},{4,5},{5,4},{6,7},{7,6},{8,9},{9,8},{10,11... | collective-permute-start | bytes 1081352 | tf_op jit(solution)/shard_map/ppermute | solution.py:334
  24.6 0.0 collective-permute-done.crossed
  24.6 13.7 %all-gather = bf16[16,64,384]{2,1,0:T(8,128)(2,1)S(1)} all-gather(bf16[2,64,384]{2,1,0:T(8,128)(2,1)S(1)} %join.1), channel_id=2, replica_groups=mesh['y'=4,'z_hi'=2,'z_far'=4,'z_near'=2,'x'=4,'core'=2] {'y','core'}, dimensions={0}, use_global_device_ids=true | all-gather | bytes 884736 | tf_op jit(solution)/shard_map/all_gather | solution.py:335
  38.3 0.0 collective-permute-done.2.share
  38.3 0.0 collective-permute-done.1.share_wide
  38.3 4.7 %chain.1 = (bf16[128,256]{1,0:T(8,128)(2,1)}, bf16[8,64,512]{2,1,0:T(8,128)(2,1)S(1)}) custom-call(bf16[4,2,2,64,384]{4,3,2,1,0:T(8,128)(2,1)S(1)} %bitcast.12, f32[1,128]{1,0:T(1,128)S(1)} %get-tuple-element.10.norm, f32[256,128]{1,0:T(8,128)S(1)} %get-tuple-element.11.emb_basis, bf16[128,256]{1,0:T(8,128)(2,1)S(1)} %copy-done.2, ...), custom_call_target="tpu_custom_call" | custom-call | tf_op jit(solution)/shard_map/chain/pallas_call | solution.py:265
  43.1 15.0 %all_to_all.10.got = bf16[8,64,512]{2,1,0:T(8,128)(2,1)S(1)} all-to-all(bf16[8,64,512]{2,1,0:T(8,128)(2,1)S(1)} %get-tuple-element.17), channel_id=1, replica_groups=mesh['y'=4,'z_hi'=2,'z_far'=4,'z_near'=2,'x'=4,'core'=2] {'z_near','x'}, dimensions={0} | all-to-all | bytes 1048576 | tf_op jit(solution)/shard_map/all_to_all | solution.py:338
  58.1 0.3 middle.1
  58.4 15.7 %all_to_all.11.got = bf16[4,64,128]{2,1,0:T(8,128)(2,1)S(1)} all-to-all(bf16[4,64,128]{2,1,0:T(8,128)(2,1)S(1)} %middle.1), channel_id=1, replica_groups=mesh['y'=4,'z_hi'=2,'z_far'=4,'z_near'=2,'x'=4,'core'=2] {'z_far'}, dimensions={0} | all-to-all | bytes 131072 | tf_op jit(solution)/shard_map/all_to_all | solution.py:339
  74.1 0.6 final.1
  (1 shorter events, 0.0 us)
Async XLA Ops:
  0.6 18.6 %copy-start = (bf16[4096,256]{1,0:T(8,128)(2,1)S(1)}, bf16[4096,256]{1,0:T(8,128)(2,1)}, u32[]{:S(2)}) copy-start(bf16[4096,256]{1,0:T(8,128)(2,1)} %basis.1) | copy-start | bytes 6291460
  0.6 18.6 %copy-start.1 = (bf16[128,4096]{1,0:T(8,128)(2,1)S(1)}, bf16[128,4096]{1,0:T(8,128)(2,1)}, u32[]{:S(2)}) copy-start(bf16[128,4096]{1,0:T(8,128)(2,1)} %emb.1) | copy-start | bytes 3145732
  0.7 18.6 %copy-start.2 = (bf16[128,256]{1,0:T(8,128)(2,1)S(1)}, bf16[128,256]{1,0:T(8,128)(2,1)}, u32[]{:S(2)}) copy-start(bf16[128,256]{1,0:T(8,128)(2,1)} %cotangent.3) | copy-start | bytes 196612
  0.7 18.6 %copy-start.3 = (f32[1,4096]{1,0:T(1,128)S(1)}, f32[1,4096]{1,0:T(1,128)}, u32[]{:S(2)}) copy-start(f32[1,4096]{1,0:T(1,128)} %gain.1) | copy-start | bytes 49156
  3.5 21.1 %collective-permute-start = (bf16[64,384]{1,0:T(8,128)(2,1)S(1)}, bf16[64,384]{1,0:T(8,128)(2,1)S(1)}, u32[]{:S(2)}, u32[]{:S(2)}) collective-permute-start(bf16[64,384]{1,0:T(8,128)(2,1)S(1)} %project.1.part.after), channel_id=1, source_target_pairs={{0,64},{64,0},{1,65},{65,1},{2,66},{66,2},{3,67},{67,3},{4,68},{68... | collective-permute-start | bytes 147464 | tf_op jit(solution)/shard_map/ppermute | solution.py:331
  20.3 18.1 %collective-permute-start.1 = (bf16[128,1536]{1,0:T(8,128)(2,1)S(1)}, bf16[128,1536]{1,0:T(8,128)(2,1)S(1)}, u32[]{:S(2)}, u32[]{:S(2)}) collective-permute-start(bf16[128,1536]{1,0:T(8,128)(2,1)S(1)} %get-tuple-element.14), channel_id=1, source_target_pairs={{0,1},{1,0},{2,3},{3,2},{4,5},{5,4},{6,7},{7,6},{8,9},{9,8},{10,11... | collective-permute-start | bytes 1179656 | tf_op jit(solution)/shard_map/ppermute | solution.py:333
  22.2 16.1 %collective-permute-start.2 = (bf16[128,1408]{1,0:T(8,128)(2,1)S(1)}, bf16[128,1408]{1,0:T(8,128)(2,1)S(1)}, u32[]{:S(2)}, u32[]{:S(2)}) collective-permute-start(bf16[128,1408]{1,0:T(8,128)(2,1)S(1)} %get-tuple-element.15), channel_id=1, source_target_pairs={{0,1},{1,0},{2,3},{3,2},{4,5},{5,4},{6,7},{7,6},{8,9},{9,8},{10,11... | collective-permute-start | bytes 1081352 | tf_op jit(solution)/shard_map/ppermute | solution.py:334

commit v9 on v8

--- a/solution.py
+++ b/solution.py
@@ -25,38 +25,40 @@
 
 
 def project_kernel(
-    chunk, emb_hbm, basis_hbm, down_hbm, up_hbm, gain_hbm,
+    sizes, emb_hbm, basis_hbm, down_hbm, up_hbm, gain_hbm,
     part, emb, basis, down, up, gain, sems,
 ):
     rows, width = emb.shape
     inner = down.shape[0]
-    steps = width // chunk
+    half = pl.ds(pl.multiple_of(lax.axis_index("core") * 128, 128), 128)
     gain_copy = pltpu.make_async_copy(gain_hbm, gain, sems.at[4, 0])
     gain_copy.start()
-    copies = []
-    for i in range(steps):
-        at = slice(i * chunk, (i + 1) * chunk)
+    spans, copies = [], []
+    begin = 0
+    for i, size in enumerate(sizes):
+        at = slice(begin, begin + size)
+        begin += size
         group = [
+            pltpu.make_async_copy(basis_hbm.at[at, half], basis.at[at, :], sems.at[3, i]),
+            pltpu.make_async_copy(emb_hbm.at[:, at], emb.at[:, at], sems.at[2, i]),
             pltpu.make_async_copy(down_hbm.at[:, at], down.at[:, at], sems.at[0, i]),
             pltpu.make_async_copy(up_hbm.at[:, at], up.at[:, at], sems.at[1, i]),
-            pltpu.make_async_copy(emb_hbm.at[:, at], emb.at[:, at], sems.at[2, i]),
-            pltpu.make_async_copy(basis_hbm.at[at, :], basis.at[at, :], sems.at[3, i]),
         ]
         for copy in group:
             copy.start()
+        spans.append(at)
         copies.append(group)
     gain_copy.wait()
-    acc = jnp.zeros((2 * inner, basis.shape[1]), F32)
+    acc = jnp.zeros((2 * inner, 128), F32)
     pre = jnp.zeros((inner, rows), F32)
-    for i in range(steps):
-        at = slice(i * chunk, (i + 1) * chunk)
-        for copy in copies[i]:
+    for at, group in zip(spans, copies):
+        for copy in group:
             copy.wait()
         scaled = (down[:, at].astype(F32) * gain[:, at]).astype(BF16)
         acc = acc + dot(jnp.concatenate([scaled, up[:, at]], axis=0), basis[at, :])
         pre = pre + dot(scaled, emb[:, at], NT)
-    first = lax.axis_index("core") == 0
-    part[:, :256] = jnp.where(first, acc[:inner], acc[inner:]).astype(BF16)
+    part[:, :128] = acc[:inner].astype(BF16)
+    part[:, 128:256] = acc[inner:].astype(BF16)
     part[:, 256:] = pre.astype(BF16)
 
 
@@ -64,20 +66,20 @@
     rows, width = embeds.shape
     rank = basis.shape[1]
     inner = down_t.shape[0]
-    chunk = 1024
+    sizes = (1024,) * 4
     args = [pltpu.with_memory_space_constraint(a, pltpu.HBM) for a in (embeds, basis, down_t, up_t, gain)]
     return pl.pallas_call(
-        functools.partial(project_kernel, chunk),
+        functools.partial(project_kernel, sizes),
         in_specs=[pl.BlockSpec(memory_space=pltpu.HBM)] * 5,
         out_specs=pl.BlockSpec(memory_space=pltpu.VMEM),
         out_shape=jax.ShapeDtypeStruct((inner, rank + rows), BF16),
         scratch_shapes=[
             pltpu.VMEM((rows, width), BF16),
-            pltpu.VMEM((width, rank), BF16),
+            pltpu.VMEM((width, 128), BF16),
             pltpu.VMEM((inner, width), BF16),
             pltpu.VMEM((inner, width), BF16),
             pltpu.VMEM((1, width), F32),
-            pltpu.SemaphoreType.DMA((5, width // chunk)),
+            pltpu.SemaphoreType.DMA((5, len(sizes))),
         ],
         compiler_params=pltpu.CompilerParams(vmem_limit_bytes=24 * 1024 * 1024),
         name="project",
@@ -177,10 +179,10 @@
     sides = (half, 1 - half)
 
     def down_of(s):
-        return every[s // 2, 0, sides[s % 2], :, :256]
+        return jnp.concatenate([every[s // 2, k, sides[s % 2], :, :128] for k in range(2)], axis=1)
 
     def up_of(s):
-        return every[s // 2, 1, sides[s % 2], :, :256]
+        return jnp.concatenate([every[s // 2, k, sides[s % 2], :, 128:256] for k in range(2)], axis=1)
 
     for s in range(count):
         turned[s, 0] = down_of(s).T

time: 75 us -> 74.8 us (level)
  no operation moved by 1% of the time
where the time goes in v9:
time: 74.8 us; the launch traced here: 74.5 us
  blocking collectives  44.4 us (59%)
  starting transfers between devices  20 us (27%)
  Pallas kernels  9.31 us (12%)
  between operations  0.76 us (1%)
    ppermute x1, starting transfers between devices, local(): crossed = lax.ppermute(part, 'z_hi', [(0, 1), (1, 0)])  15.7 us
    all_to_all x1, blocking collectives, local(): got = lax.all_to_all(middle(got, shared_basis), 'z_far', 0, 0, tiled=True)  15.7 us
    all_to_all x1, blocking collectives, local(): got = lax.all_to_all(slots, ('z_near', 'x'), 0, 0, tiled=True)  15 us
    all_gather x1, blocking collectives, local(): every = lax.all_gather(join(part, crossed), ('y', 'core'), tiled=False)  13.7 us
    pallas_call x1, Pallas kernels, chain(): pl.pallas_call(chain_kernel, in_specs=[vmem] * 9, out_specs=[hbm, vmem],...  4.75 us
    pallas_call x1, Pallas kernels, project(): pl.pallas_call(functools.partial(project_kernel, sizes), in_specs=[pl.Blo...  2.67 us
    ppermute x1, starting transfers between devices, local(): share = lax.ppermute(share, 'core', [(0, 1), (1, 0)])  2.41 us
    ppermute x1, starting transfers between devices, local(): share_wide = lax.ppermute(share_wide, 'core', [(0, 1), (1, 0)])  1.91 us
  transfers between devices with their start and end apart: 3, of which 0 were waited for; matrix products, arithmetic and copies ran while one was open for 0% of the time, Pallas kernels for 1%

profile of v9, /device:TPU:8, one launch (start us, length us, event | category | flops | bytes accessed | tf_op | source)
XLA Modules:
  0.0 74.5 jit_solution(14185722928964515749)
XLA Ops:
  0.6 0.0 copy-start
  0.6 0.0 copy-start.1
  0.7 0.0 copy-start.2
  0.7 0.0 copy-start.3
  0.7 2.7 %project.1.part.after = bf16[64,384]{1,0:T(8,128)(2,1)S(1)} custom-call(bf16[128,4096]{1,0:T(8,128)(2,1)} %emb.1, bf16[4096,256]{1,0:T(8,128)(2,1)} %basis.1, bf16[64,4096]{1,0:T(8,128)(2,1)} %bitcast.13, bf16[64,4096]{1,0:T(8,128)(2,1)} %bitcast.14, f32[1,4096]{1,0:T(1,128)} %gain.1), custom_call_target="tpu_custom_call" | custom-call | tf_op jit(solution)/shard_map/project/pallas_call | solution.py:71
  3.4 15.7 %collective-permute-start = (bf16[64,384]{1,0:T(8,128)(2,1)S(1)}, bf16[64,384]{1,0:T(8,128)(2,1)S(1)}, u32[]{:S(2)}, u32[]{:S(2)}) collective-permute-start(bf16[64,384]{1,0:T(8,128)(2,1)S(1)} %project.1.part.after), channel_id=1, source_target_pairs={{0,64},{64,0},{1,65},{65,1},{2,66},{66,2},{3,67},{67,3},{4,68},{68... | collective-permute-start | bytes 147464 | tf_op jit(solution)/shard_map/ppermute | solution.py:333
  19.1 0.0 copy-done
  19.1 0.0 copy-done.1
  19.1 0.0 copy-done.2
  19.1 0.0 copy-done.3
  19.1 1.0 %embed.1 = (f32[256,128]{1,0:T(8,128)S(1)}, f32[1,128]{1,0:T(1,128)S(1)}, bf16[128,2048]{1,0:T(8,128)(2,1)S(1)}, f32[1,2048]{1,0:T(1,128)S(1)}, bf16[128,1536]{1...) custom-call(bf16[128,4096]{1,0:T(8,128)(2,1)S(1)} %copy-done.1, bf16[4096,256]{1,0:T(8,128)(2,1)S(1)} %copy-done, ...), custom_call_target="tpu_custom_call" | custom-call | tf_op jit(solution)/shard_map/embed/pallas_call | solution.py:137
  20.1 1.9 %collective-permute-start.1 = (bf16[128,1536]{1,0:T(8,128)(2,1)S(1)}, bf16[128,1536]{1,0:T(8,128)(2,1)S(1)}, u32[]{:S(2)}, u32[]{:S(2)}) collective-permute-start(bf16[128,1536]{1,0:T(8,128)(2,1)S(1)} %get-tuple-element.14), channel_id=1, source_target_pairs={{0,1},{1,0},{2,3},{3,2},{4,5},{5,4},{6,7},{7,6},{8,9},{9,8},{10,11... | collective-permute-start | bytes 1179656 | tf_op jit(solution)/shard_map/ppermute | solution.py:335
  22.0 2.4 %collective-permute-start.2 = (bf16[128,1408]{1,0:T(8,128)(2,1)S(1)}, bf16[128,1408]{1,0:T(8,128)(2,1)S(1)}, u32[]{:S(2)}, u32[]{:S(2)}) collective-permute-start(bf16[128,1408]{1,0:T(8,128)(2,1)S(1)} %get-tuple-element.15), channel_id=1, source_target_pairs={{0,1},{1,0},{2,3},{3,2},{4,5},{5,4},{6,7},{7,6},{8,9},{9,8},{10,11... | collective-permute-start | bytes 1081352 | tf_op jit(solution)/shard_map/ppermute | solution.py:336
  24.4 0.0 collective-permute-done.crossed
  24.5 13.7 %all-gather = bf16[16,64,384]{2,1,0:T(8,128)(2,1)S(1)} all-gather(bf16[2,64,384]{2,1,0:T(8,128)(2,1)S(1)} %join.1), channel_id=2, replica_groups=mesh['y'=4,'z_hi'=2,'z_far'=4,'z_near'=2,'x'=4,'core'=2] {'y','core'}, dimensions={0}, use_global_device_ids=true | all-gather | bytes 884736 | tf_op jit(solution)/shard_map/all_gather | solution.py:337
  38.2 0.0 collective-permute-done.2.share
  38.2 0.0 collective-permute-done.1.share_wide
  38.2 4.7 %chain.1 = (bf16[128,256]{1,0:T(8,128)(2,1)}, bf16[8,64,512]{2,1,0:T(8,128)(2,1)S(1)}) custom-call(bf16[4,2,2,64,384]{4,3,2,1,0:T(8,128)(2,1)S(1)} %bitcast.12, f32[1,128]{1,0:T(1,128)S(1)} %get-tuple-element.10.norm, f32[256,128]{1,0:T(8,128)S(1)} %get-tuple-element.11.emb_basis, bf16[128,256]{1,0:T(8,128)(2,1)S(1)} %copy-done.2, ...), custom_call_target="tpu_custom_call" | custom-call | tf_op jit(solution)/shard_map/chain/pallas_call | solution.py:267
  42.9 15.0 %all_to_all.10.got = bf16[8,64,512]{2,1,0:T(8,128)(2,1)S(1)} all-to-all(bf16[8,64,512]{2,1,0:T(8,128)(2,1)S(1)} %get-tuple-element.17), channel_id=1, replica_groups=mesh['y'=4,'z_hi'=2,'z_far'=4,'z_near'=2,'x'=4,'core'=2] {'z_near','x'}, dimensions={0} | all-to-all | bytes 1048576 | tf_op jit(solution)/shard_map/all_to_all | solution.py:340
  58.0 0.3 middle.1
  58.2 15.7 %all_to_all.11.got = bf16[4,64,128]{2,1,0:T(8,128)(2,1)S(1)} all-to-all(bf16[4,64,128]{2,1,0:T(8,128)(2,1)S(1)} %middle.1), channel_id=1, replica_groups=mesh['y'=4,'z_hi'=2,'z_far'=4,'z_near'=2,'x'=4,'core'=2] {'z_far'}, dimensions={0} | all-to-all | bytes 131072 | tf_op jit(solution)/shard_map/all_to_all | solution.py:341
  73.9 0.6 final.1
  (1 shorter events, 0.0 us)
Async XLA Ops:
  0.6 18.5 %copy-start = (bf16[4096,256]{1,0:T(8,128)(2,1)S(1)}, bf16[4096,256]{1,0:T(8,128)(2,1)}, u32[]{:S(2)}) copy-start(bf16[4096,256]{1,0:T(8,128)(2,1)} %basis.1) | copy-start | bytes 6291460
  0.6 18.5 %copy-start.1 = (bf16[128,4096]{1,0:T(8,128)(2,1)S(1)}, bf16[128,4096]{1,0:T(8,128)(2,1)}, u32[]{:S(2)}) copy-start(bf16[128,4096]{1,0:T(8,128)(2,1)} %emb.1) | copy-start | bytes 3145732
  0.7 18.5 %copy-start.2 = (bf16[128,256]{1,0:T(8,128)(2,1)S(1)}, bf16[128,256]{1,0:T(8,128)(2,1)}, u32[]{:S(2)}) copy-start(bf16[128,256]{1,0:T(8,128)(2,1)} %cotangent.3) | copy-start | bytes 196612
  0.7 18.5 %copy-start.3 = (f32[1,4096]{1,0:T(1,128)S(1)}, f32[1,4096]{1,0:T(1,128)}, u32[]{:S(2)}) copy-start(f32[1,4096]{1,0:T(1,128)} %gain.1) | copy-start | bytes 49156
  3.4 21.1 %collective-permute-start = (bf16[64,384]{1,0:T(8,128)(2,1)S(1)}, bf16[64,384]{1,0:T(8,128)(2,1)S(1)}, u32[]{:S(2)}, u32[]{:S(2)}) collective-permute-start(bf16[64,384]{1,0:T(8,128)(2,1)S(1)} %project.1.part.after), channel_id=1, source_target_pairs={{0,64},{64,0},{1,65},{65,1},{2,66},{66,2},{3,67},{67,3},{4,68},{68... | collective-permute-start | bytes 147464 | tf_op jit(solution)/shard_map/ppermute | solution.py:333
  20.1 18.1 %collective-permute-start.1 = (bf16[128,1536]{1,0:T(8,128)(2,1)S(1)}, bf16[128,1536]{1,0:T(8,128)(2,1)S(1)}, u32[]{:S(2)}, u32[]{:S(2)}) collective-permute-start(bf16[128,1536]{1,0:T(8,128)(2,1)S(1)} %get-tuple-element.14), channel_id=1, source_target_pairs={{0,1},{1,0},{2,3},{3,2},{4,5},{5,4},{6,7},{7,6},{8,9},{9,8},{10,11... | collective-permute-start | bytes 1179656 | tf_op jit(solution)/shard_map/ppermute | solution.py:335
  22.0 16.1 %collective-permute-start.2 = (bf16[128,1408]{1,0:T(8,128)(2,1)S(1)}, bf16[128,1408]{1,0:T(8,128)(2,1)S(1)}, u32[]{:S(2)}, u32[]{:S(2)}) collective-permute-start(bf16[128,1408]{1,0:T(8,128)(2,1)S(1)} %get-tuple-element.15), channel_id=1, source_target_pairs={{0,1},{1,0},{2,3},{3,2},{4,5},{5,4},{6,7},{7,6},{8,9},{9,8},{10,11... | collective-permute-start | bytes 1081352 | tf_op jit(solution)/shard_map/ppermute | solution.py:336

commit v10 on v9

--- a/solution.py
+++ b/solution.py
@@ -86,7 +86,7 @@
     )(*args)
 
 
-def embed_kernel(emb, basis, gain, cotangent, after, emb_basis, norm, mine, gain_mine, share_wide, share):
+def embed_kernel(emb, basis, gain, cotangent, after, emb_basis, norm, cot_turned, mine, gain_mine, share_wide, share):
     del after
     rows, width = emb.shape
     chunk = 1024
@@ -99,17 +99,22 @@
         sq = ef * ef
         for k in range(0, chunk, 128):
             square = square + sq[:, k : k + 128]
-    emb_basis[...] = acc.T
-    norm[...] = jnp.sum(square.T, axis=0, keepdims=True)
-    high = acc.astype(BF16)
-    share[:, 512:768] = high
-    share[:, 768:1024] = (acc - high.astype(F32)).astype(BF16)
-    share[:, 1024:1280] = cotangent[...]
-    total = jnp.broadcast_to(jnp.sum(square, axis=1, keepdims=True), (rows, 128))
+    turned = acc.T
+    emb_basis[...] = turned
+    high = turned.astype(BF16)
+    low_part = (turned - high.astype(F32)).astype(BF16)
+    cot = cotangent[...].T
+    cot_turned[...] = cot
+    for begin, whole in ((512, high), (768, low_part), (1024, cot)):
+        share[:, begin : begin + 128] = whole[:rows]
+        share[:, begin + 128 : begin + 256] = whole[rows:]
+    total = jnp.sum(square.T, axis=0, keepdims=True)
+    norm[...] = total
+    total = jnp.broadcast_to(total, (rows, 128))
     first = total.astype(BF16).astype(F32)
     second = (total - first).astype(BF16).astype(F32)
-    lane = lax.broadcasted_iota(jnp.int32, (rows, 128), 1)
-    parts = jnp.where(lane == 0, first, jnp.where(lane == 1, second, total - first - second))
+    row = lax.broadcasted_iota(jnp.int32, (rows, 128), 0)
+    parts = jnp.where(row == 0, first, jnp.where(row == 1, second, total - first - second))
     share[:, 1280:1408] = parts.astype(BF16)
     even = lax.axis_index("core") == 0
     for j in range(8):
@@ -137,10 +142,11 @@
     return pl.pallas_call(
         embed_kernel,
         in_specs=[vmem] * 4 + [pl.BlockSpec(memory_space=pl.ANY)],
-        out_specs=[vmem] * 6,
+        out_specs=[vmem] * 7,
         out_shape=[
             jax.ShapeDtypeStruct((rank, rows), F32),
             jax.ShapeDtypeStruct((1, rows), F32),
+            jax.ShapeDtypeStruct((rank, rows), BF16),
             jax.ShapeDtypeStruct((rows, width // 2), BF16),
             jax.ShapeDtypeStruct((1, width // 2), F32),
             jax.ShapeDtypeStruct((rows, 1536), BF16),
@@ -191,8 +197,10 @@
         links[s, 0] = dot(down_of(s), up_of(s - 1), NT).astype(BF16)
         links[s, 1] = dot(up_of(s - 1), down_of(s), NT).astype(BF16)
 
-    theirs = (share[:, 512:768].astype(F32) + share[:, 768:1024].astype(F32)).T
-    parts = share[:, 1280:1408].astype(F32).T
+    theirs = jnp.concatenate(
+        [share[:, at : at + 128].astype(F32) + share[:, at + 256 : at + 384].astype(F32) for at in (512, 640)], axis=0
+    )
+    parts = share[:16, 1280:1408].astype(F32)
     eu = jnp.concatenate([emb_basis[...], theirs], axis=1)
     sq = jnp.concatenate([norm[...], parts[0:1] + parts[1:2] + parts[2:3]], axis=1)
     c = jnp.zeros(eu.shape, BF16)
@@ -229,7 +237,9 @@
     coefs_copy = pltpu.make_async_copy(coefs, coefs_hbm, coefs_sem)
     coefs_copy.start()
 
-    g = jnp.concatenate([cotangent[...].T, share[:, 1024:1280].T], axis=1)
+    g = jnp.concatenate(
+        [cotangent[...], jnp.concatenate([share[:, 1024:1152], share[:, 1152:1280]], axis=0)], axis=1
+    )
     grad_act = dot(up_of(count - 1), g)
     for s in reversed(range(count)):
         g_kept[s] = g
@@ -259,7 +269,7 @@
 
 def chain(every, norm, emb_basis, cotangent, mine, basis, gain, share_wide, share):
     count = 2 * every.shape[0]
-    rows, rank = cotangent.shape
+    rank, rows = cotangent.shape
     tokens = 2 * rows
     inner = 64
     hbm = pl.BlockSpec(memory_space=pltpu.HBM)
@@ -331,12 +341,12 @@
 def local(embeds, shared_basis, down_proj, up_proj, norm_gain, coef_grad):
     part = project(embeds, shared_basis, down_proj[0].T, up_proj[0].T, norm_gain)
     crossed = lax.ppermute(part, "z_hi", [(0, 1), (1, 0)])
-    emb_basis, norm, mine, gain, share_wide, share = embed(embeds, shared_basis, norm_gain, coef_grad, part)
+    emb_basis, norm, cot, mine, gain, share_wide, share = embed(embeds, shared_basis, norm_gain, coef_grad, part)
     share_wide = lax.ppermute(share_wide, "core", [(0, 1), (1, 0)])
     share = lax.ppermute(share, "core", [(0, 1), (1, 0)])
     every = lax.all_gather(join(part, crossed), ("y", "core"), tiled=False)
     every = every.reshape((4, 2, 2) + part.shape)
-    coefs, slots = chain(every, norm, emb_basis, coef_grad, mine, shared_basis, gain, share_wide, share)
+    coefs, slots = chain(every, norm, emb_basis, cot, mine, shared_basis, gain, share_wide, share)
     got = lax.all_to_all(slots, ("z_near", "x"), 0, 0, tiled=True)
     got = lax.all_to_all(middle(got, shared_basis), "z_far", 0, 0, tiled=True)
     return coefs[None], final(got)[None]

time: 74.8 us -> 74.8 us (level)
  no operation moved by 1% of the time
where the time goes in v10:
time: 74.8 us; the launch traced here: 74.5 us
  blocking collectives  44.4 us (59%)
  starting transfers between devices  20 us (27%)
  Pallas kernels  9.27 us (12%)
  between operations  0.76 us (1%)
    ppermute x1, starting transfers between devices, local(): crossed = lax.ppermute(part, 'z_hi', [(0, 1), (1, 0)])  15.7 us
    all_to_all x1, blocking collectives, local(): got = lax.all_to_all(middle(got, shared_basis), 'z_far', 0, 0, tiled=True)  15.7 us
    all_to_all x1, blocking collectives, local(): got = lax.all_to_all(slots, ('z_near', 'x'), 0, 0, tiled=True)  15 us
    all_gather x1, blocking collectives, local(): every = lax.all_gather(join(part, crossed), ('y', 'core'), tiled=False)  13.7 us
    pallas_call x1, Pallas kernels, chain(): pl.pallas_call(chain_kernel, in_specs=[vmem] * 9, out_specs=[hbm, vmem],...  4.76 us
    pallas_call x1, Pallas kernels, project(): pl.pallas_call(functools.partial(project_kernel, sizes), in_specs=[pl.Blo...  2.67 us
    ppermute x1, starting transfers between devices, local(): share = lax.ppermute(share, 'core', [(0, 1), (1, 0)])  2.41 us
    ppermute x1, starting transfers between devices, local(): share_wide = lax.ppermute(share_wide, 'core', [(0, 1), (1, 0)])  1.92 us
  transfers between devices with their start and end apart: 3, of which 0 were waited for; matrix products, arithmetic and copies ran while one was open for 0% of the time, Pallas kernels for 1%

profile of v10, /device:TPU:8, one launch (start us, length us, event | category | flops | bytes accessed | tf_op | source)
XLA Modules:
  0.0 74.5 jit_solution(15487333614266100902)
XLA Ops:
  0.6 0.0 copy-start
  0.6 0.0 copy-start.1
  0.7 0.0 copy-start.2
  0.7 0.0 copy-start.3
  0.7 2.7 %project.1.part.after = bf16[64,384]{1,0:T(8,128)(2,1)S(1)} custom-call(bf16[128,4096]{1,0:T(8,128)(2,1)} %emb.1, bf16[4096,256]{1,0:T(8,128)(2,1)} %basis.1, bf16[64,4096]{1,0:T(8,128)(2,1)} %bitcast.13, bf16[64,4096]{1,0:T(8,128)(2,1)} %bitcast.14, f32[1,4096]{1,0:T(1,128)} %gain.1), custom_call_target="tpu_custom_call" | custom-call | tf_op jit(solution)/shard_map/project/pallas_call | solution.py:71
  3.4 15.7 %collective-permute-start = (bf16[64,384]{1,0:T(8,128)(2,1)S(1)}, bf16[64,384]{1,0:T(8,128)(2,1)S(1)}, u32[]{:S(2)}, u32[]{:S(2)}) collective-permute-start(bf16[64,384]{1,0:T(8,128)(2,1)S(1)} %project.1.part.after), channel_id=1, source_target_pairs={{0,64},{64,0},{1,65},{65,1},{2,66},{66,2},{3,67},{67,3},{4,68},{68... | collective-permute-start | bytes 147464 | tf_op jit(solution)/shard_map/ppermute | solution.py:343
  19.1 0.0 copy-done
  19.1 0.0 copy-done.1
  19.1 0.0 copy-done.2
  19.1 0.0 copy-done.3
  19.1 0.9 %embed.1 = (f32[256,128]{1,0:T(8,128)S(1)}, f32[1,128]{1,0:T(1,128)S(1)}, bf16[256,128]{1,0:T(8,128)(2,1)S(1)}, bf16[128,2048]{1,0:T(8,128)(2,1)S(1)}, f32[1,204...) custom-call(bf16[128,4096]{1,0:T(8,128)(2,1)S(1)} %copy-done.1, ...), custom_call_target="tpu_custom_call" | custom-call | tf_op jit(solution)/shard_map/embed/pallas_call | solution.py:142
  20.1 1.9 %collective-permute-start.1 = (bf16[128,1536]{1,0:T(8,128)(2,1)S(1)}, bf16[128,1536]{1,0:T(8,128)(2,1)S(1)}, u32[]{:S(2)}, u32[]{:S(2)}) collective-permute-start(bf16[128,1536]{1,0:T(8,128)(2,1)S(1)} %get-tuple-element.16), channel_id=1, source_target_pairs={{0,1},{1,0},{2,3},{3,2},{4,5},{5,4},{6,7},{7,6},{8,9},{9,8},{10,11... | collective-permute-start | bytes 1179656 | tf_op jit(solution)/shard_map/ppermute | solution.py:345
  22.0 2.4 %collective-permute-start.2 = (bf16[128,1408]{1,0:T(8,128)(2,1)S(1)}, bf16[128,1408]{1,0:T(8,128)(2,1)S(1)}, u32[]{:S(2)}, u32[]{:S(2)}) collective-permute-start(bf16[128,1408]{1,0:T(8,128)(2,1)S(1)} %get-tuple-element.17), channel_id=1, source_target_pairs={{0,1},{1,0},{2,3},{3,2},{4,5},{5,4},{6,7},{7,6},{8,9},{9,8},{10,11... | collective-permute-start | bytes 1081352 | tf_op jit(solution)/shard_map/ppermute | solution.py:346
  24.4 0.0 collective-permute-done.crossed
  24.4 13.7 %all-gather = bf16[16,64,384]{2,1,0:T(8,128)(2,1)S(1)} all-gather(bf16[2,64,384]{2,1,0:T(8,128)(2,1)S(1)} %join.1), channel_id=2, replica_groups=mesh['y'=4,'z_hi'=2,'z_far'=4,'z_near'=2,'x'=4,'core'=2] {'y','core'}, dimensions={0}, use_global_device_ids=true | all-gather | bytes 884736 | tf_op jit(solution)/shard_map/all_gather | solution.py:347
  38.1 0.0 collective-permute-done.2.share
  38.1 0.0 collective-permute-done.1.share_wide
  38.1 4.8 %chain.1 = (bf16[128,256]{1,0:T(8,128)(2,1)}, bf16[8,64,512]{2,1,0:T(8,128)(2,1)S(1)}) custom-call(bf16[4,2,2,64,384]{4,3,2,1,0:T(8,128)(2,1)S(1)} %bitcast.12, f32[1,128]{1,0:T(1,128)S(1)} %get-tuple-element.11.norm, f32[256,128]{1,0:T(8,128)S(1)} %get-tuple-element.12.emb_basis, bf16[256,128]{1,0:T(8,128)(2,1)S(1)} %get-tuple-element.13.cotangent, ...), custom_call_target="tpu_custom_call" | custom-call | tf_op jit(solution)/shard_map/chain/pallas_call | solution.py:277
  42.9 15.0 %all_to_all.10.got = bf16[8,64,512]{2,1,0:T(8,128)(2,1)S(1)} all-to-all(bf16[8,64,512]{2,1,0:T(8,128)(2,1)S(1)} %get-tuple-element.19), channel_id=1, replica_groups=mesh['y'=4,'z_hi'=2,'z_far'=4,'z_near'=2,'x'=4,'core'=2] {'z_near','x'}, dimensions={0} | all-to-all | bytes 1048576 | tf_op jit(solution)/shard_map/all_to_all | solution.py:350
  57.9 0.3 middle.1
  58.2 15.7 %all_to_all.11.got = bf16[4,64,128]{2,1,0:T(8,128)(2,1)S(1)} all-to-all(bf16[4,64,128]{2,1,0:T(8,128)(2,1)S(1)} %middle.1), channel_id=1, replica_groups=mesh['y'=4,'z_hi'=2,'z_far'=4,'z_near'=2,'x'=4,'core'=2] {'z_far'}, dimensions={0} | all-to-all | bytes 131072 | tf_op jit(solution)/shard_map/all_to_all | solution.py:351
  73.9 0.6 final.1
  (1 shorter events, 0.0 us)
Async XLA Ops:
  0.6 18.5 %copy-start = (bf16[4096,256]{1,0:T(8,128)(2,1)S(1)}, bf16[4096,256]{1,0:T(8,128)(2,1)}, u32[]{:S(2)}) copy-start(bf16[4096,256]{1,0:T(8,128)(2,1)} %basis.1) | copy-start | bytes 6291460
  0.6 18.5 %copy-start.1 = (bf16[128,4096]{1,0:T(8,128)(2,1)S(1)}, bf16[128,4096]{1,0:T(8,128)(2,1)}, u32[]{:S(2)}) copy-start(bf16[128,4096]{1,0:T(8,128)(2,1)} %emb.1) | copy-start | bytes 3145732
  0.7 18.5 %copy-start.2 = (f32[1,4096]{1,0:T(1,128)S(1)}, f32[1,4096]{1,0:T(1,128)}, u32[]{:S(2)}) copy-start(f32[1,4096]{1,0:T(1,128)} %gain.1) | copy-start | bytes 49156
  0.7 18.5 %copy-start.3 = (bf16[128,256]{1,0:T(8,128)(2,1)S(1)}, bf16[128,256]{1,0:T(8,128)(2,1)}, u32[]{:S(2)}) copy-start(bf16[128,256]{1,0:T(8,128)(2,1)} %cotangent.1) | copy-start | bytes 196612
  3.4 21.0 %collective-permute-start = (bf16[64,384]{1,0:T(8,128)(2,1)S(1)}, bf16[64,384]{1,0:T(8,128)(2,1)S(1)}, u32[]{:S(2)}, u32[]{:S(2)}) collective-permute-start(bf16[64,384]{1,0:T(8,128)(2,1)S(1)} %project.1.part.after), channel_id=1, source_target_pairs={{0,64},{64,0},{1,65},{65,1},{2,66},{66,2},{3,67},{67,3},{4,68},{68... | collective-permute-start | bytes 147464 | tf_op jit(solution)/shard_map/ppermute | solution.py:343
  20.1 18.1 %collective-permute-start.1 = (bf16[128,1536]{1,0:T(8,128)(2,1)S(1)}, bf16[128,1536]{1,0:T(8,128)(2,1)S(1)}, u32[]{:S(2)}, u32[]{:S(2)}) collective-permute-start(bf16[128,1536]{1,0:T(8,128)(2,1)S(1)} %get-tuple-element.16), channel_id=1, source_target_pairs={{0,1},{1,0},{2,3},{3,2},{4,5},{5,4},{6,7},{7,6},{8,9},{9,8},{10,11... | collective-permute-start | bytes 1179656 | tf_op jit(solution)/shard_map/ppermute | solution.py:345
  22.0 16.1 %collective-permute-start.2 = (bf16[128,1408]{1,0:T(8,128)(2,1)S(1)}, bf16[128,1408]{1,0:T(8,128)(2,1)S(1)}, u32[]{:S(2)}, u32[]{:S(2)}) collective-permute-start(bf16[128,1408]{1,0:T(8,128)(2,1)S(1)} %get-tuple-element.17), channel_id=1, source_target_pairs={{0,1},{1,0},{2,3},{3,2},{4,5},{5,4},{6,7},{7,6},{8,9},{9,8},{10,11... | collective-permute-start | bytes 1081352 | tf_op jit(solution)/shard_map/ppermute | solution.py:346

commit v11 on v10

--- a/solution.py
+++ b/solution.py
@@ -226,7 +226,7 @@
         inv = lax.rsqrt(jnp.maximum(total, 0.0) * (1.0 / width) + EPS)
         invs.append(inv)
         pre = pre * inv
-        sig = 1.0 / (1.0 + jnp.exp(-pre))
+        sig = 0.5 + 0.5 * jnp.tanh(0.5 * pre)
         act = (pre * sig).astype(BF16)
         pre_kept[s] = pre
         slope_kept[s] = sig * (1.0 + pre * (1.0 - sig))

time: 74.8 us -> 74.7 us (level)
  no operation moved by 1% of the time
where the time goes in v11:
time: 74.7 us; the launch traced here: 74.5 us
  blocking collectives  44.4 us (59%)
  starting transfers between devices  20 us (27%)
  Pallas kernels  9.22 us (12%)
  between operations  0.76 us (1%)
    ppermute x1, starting transfers between devices, local(): crossed = lax.ppermute(part, 'z_hi', [(0, 1), (1, 0)])  15.7 us
    all_to_all x1, blocking collectives, local(): got = lax.all_to_all(middle(got, shared_basis), 'z_far', 0, 0, tiled=True)  15.7 us
    all_to_all x1, blocking collectives, local(): got = lax.all_to_all(slots, ('z_near', 'x'), 0, 0, tiled=True)  15 us
    all_gather x1, blocking collectives, local(): every = lax.all_gather(join(part, crossed), ('y', 'core'), tiled=False)  13.7 us
    pallas_call x1, Pallas kernels, chain(): pl.pallas_call(chain_kernel, in_specs=[vmem] * 9, out_specs=[hbm, vmem],...  4.7 us
    pallas_call x1, Pallas kernels, project(): pl.pallas_call(functools.partial(project_kernel, sizes), in_specs=[pl.Blo...  2.67 us
    ppermute x1, starting transfers between devices, local(): share = lax.ppermute(share, 'core', [(0, 1), (1, 0)])  2.41 us
    ppermute x1, starting transfers between devices, local(): share_wide = lax.ppermute(share_wide, 'core', [(0, 1), (1, 0)])  1.92 us
  transfers between devices with their start and end apart: 3, of which 0 were waited for; matrix products, arithmetic and copies ran while one was open for 0% of the time, Pallas kernels for 1%

profile of v11, /device:TPU:8, one launch (start us, length us, event | category | flops | bytes accessed | tf_op | source)
XLA Modules:
  0.0 74.5 jit_solution(4931776777794517809)
XLA Ops:
  0.6 0.0 copy-start
  0.6 0.0 copy-start.1
  0.7 0.0 copy-start.2
  0.7 0.0 copy-start.3
  0.7 2.7 %project.1.part.after = bf16[64,384]{1,0:T(8,128)(2,1)S(1)} custom-call(bf16[128,4096]{1,0:T(8,128)(2,1)} %emb.1, bf16[4096,256]{1,0:T(8,128)(2,1)} %basis.1, bf16[64,4096]{1,0:T(8,128)(2,1)} %bitcast.13, bf16[64,4096]{1,0:T(8,128)(2,1)} %bitcast.14, f32[1,4096]{1,0:T(1,128)} %gain.1), custom_call_target="tpu_custom_call" | custom-call | tf_op jit(solution)/shard_map/project/pallas_call | solution.py:71
  3.4 15.7 %collective-permute-start = (bf16[64,384]{1,0:T(8,128)(2,1)S(1)}, bf16[64,384]{1,0:T(8,128)(2,1)S(1)}, u32[]{:S(2)}, u32[]{:S(2)}) collective-permute-start(bf16[64,384]{1,0:T(8,128)(2,1)S(1)} %project.1.part.after), channel_id=1, source_target_pairs={{0,64},{64,0},{1,65},{65,1},{2,66},{66,2},{3,67},{67,3},{4,68},{68... | collective-permute-start | bytes 147464 | tf_op jit(solution)/shard_map/ppermute | solution.py:343
  19.1 0.0 copy-done
  19.1 0.0 copy-done.1
  19.1 0.0 copy-done.2
  19.1 0.0 copy-done.3
  19.1 0.9 %embed.1 = (f32[256,128]{1,0:T(8,128)S(1)}, f32[1,128]{1,0:T(1,128)S(1)}, bf16[256,128]{1,0:T(8,128)(2,1)S(1)}, bf16[128,2048]{1,0:T(8,128)(2,1)S(1)}, f32[1,204...) custom-call(bf16[128,4096]{1,0:T(8,128)(2,1)S(1)} %copy-done.1, ...), custom_call_target="tpu_custom_call" | custom-call | tf_op jit(solution)/shard_map/embed/pallas_call | solution.py:142
  20.1 1.9 %collective-permute-start.1 = (bf16[128,1536]{1,0:T(8,128)(2,1)S(1)}, bf16[128,1536]{1,0:T(8,128)(2,1)S(1)}, u32[]{:S(2)}, u32[]{:S(2)}) collective-permute-start(bf16[128,1536]{1,0:T(8,128)(2,1)S(1)} %get-tuple-element.16), channel_id=1, source_target_pairs={{0,1},{1,0},{2,3},{3,2},{4,5},{5,4},{6,7},{7,6},{8,9},{9,8},{10,11... | collective-permute-start | bytes 1179656 | tf_op jit(solution)/shard_map/ppermute | solution.py:345
  22.0 2.4 %collective-permute-start.2 = (bf16[128,1408]{1,0:T(8,128)(2,1)S(1)}, bf16[128,1408]{1,0:T(8,128)(2,1)S(1)}, u32[]{:S(2)}, u32[]{:S(2)}) collective-permute-start(bf16[128,1408]{1,0:T(8,128)(2,1)S(1)} %get-tuple-element.17), channel_id=1, source_target_pairs={{0,1},{1,0},{2,3},{3,2},{4,5},{5,4},{6,7},{7,6},{8,9},{9,8},{10,11... | collective-permute-start | bytes 1081352 | tf_op jit(solution)/shard_map/ppermute | solution.py:346
  24.4 0.0 collective-permute-done.crossed
  24.4 13.7 %all-gather = bf16[16,64,384]{2,1,0:T(8,128)(2,1)S(1)} all-gather(bf16[2,64,384]{2,1,0:T(8,128)(2,1)S(1)} %join.1), channel_id=2, replica_groups=mesh['y'=4,'z_hi'=2,'z_far'=4,'z_near'=2,'x'=4,'core'=2] {'y','core'}, dimensions={0}, use_global_device_ids=true | all-gather | bytes 884736 | tf_op jit(solution)/shard_map/all_gather | solution.py:347
  38.1 0.0 collective-permute-done.2.share
  38.1 0.0 collective-permute-done.1.share_wide
  38.1 4.7 %chain.1 = (bf16[128,256]{1,0:T(8,128)(2,1)}, bf16[8,64,512]{2,1,0:T(8,128)(2,1)S(1)}) custom-call(bf16[4,2,2,64,384]{4,3,2,1,0:T(8,128)(2,1)S(1)} %bitcast.12, f32[1,128]{1,0:T(1,128)S(1)} %get-tuple-element.11.norm, f32[256,128]{1,0:T(8,128)S(1)} %get-tuple-element.12.emb_basis, bf16[256,128]{1,0:T(8,128)(2,1)S(1)} %get-tuple-element.13.cotangent, ...), custom_call_target="tpu_custom_call" | custom-call | tf_op jit(solution)/shard_map/chain/pallas_call | solution.py:277
  42.8 15.0 %all_to_all.10.got = bf16[8,64,512]{2,1,0:T(8,128)(2,1)S(1)} all-to-all(bf16[8,64,512]{2,1,0:T(8,128)(2,1)S(1)} %get-tuple-element.19), channel_id=1, replica_groups=mesh['y'=4,'z_hi'=2,'z_far'=4,'z_near'=2,'x'=4,'core'=2] {'z_near','x'}, dimensions={0} | all-to-all | bytes 1048576 | tf_op jit(solution)/shard_map/all_to_all | solution.py:350
  57.9 0.3 middle.1
  58.2 15.7 %all_to_all.11.got = bf16[4,64,128]{2,1,0:T(8,128)(2,1)S(1)} all-to-all(bf16[4,64,128]{2,1,0:T(8,128)(2,1)S(1)} %middle.1), channel_id=1, replica_groups=mesh['y'=4,'z_hi'=2,'z_far'=4,'z_near'=2,'x'=4,'core'=2] {'z_far'}, dimensions={0} | all-to-all | bytes 131072 | tf_op jit(solution)/shard_map/all_to_all | solution.py:351
  73.9 0.6 final.1
  (1 shorter events, 0.0 us)
Async XLA Ops:
  0.6 18.5 %copy-start = (bf16[4096,256]{1,0:T(8,128)(2,1)S(1)}, bf16[4096,256]{1,0:T(8,128)(2,1)}, u32[]{:S(2)}) copy-start(bf16[4096,256]{1,0:T(8,128)(2,1)} %basis.1) | copy-start | bytes 6291460
  0.6 18.5 %copy-start.1 = (bf16[128,4096]{1,0:T(8,128)(2,1)S(1)}, bf16[128,4096]{1,0:T(8,128)(2,1)}, u32[]{:S(2)}) copy-start(bf16[128,4096]{1,0:T(8,128)(2,1)} %emb.1) | copy-start | bytes 3145732
  0.7 18.5 %copy-start.2 = (f32[1,4096]{1,0:T(1,128)S(1)}, f32[1,4096]{1,0:T(1,128)}, u32[]{:S(2)}) copy-start(f32[1,4096]{1,0:T(1,128)} %gain.1) | copy-start | bytes 49156
  0.7 18.5 %copy-start.3 = (bf16[128,256]{1,0:T(8,128)(2,1)S(1)}, bf16[128,256]{1,0:T(8,128)(2,1)}, u32[]{:S(2)}) copy-start(bf16[128,256]{1,0:T(8,128)(2,1)} %cotangent.1) | copy-start | bytes 196612
  3.4 21.0 %collective-permute-start = (bf16[64,384]{1,0:T(8,128)(2,1)S(1)}, bf16[64,384]{1,0:T(8,128)(2,1)S(1)}, u32[]{:S(2)}, u32[]{:S(2)}) collective-permute-start(bf16[64,384]{1,0:T(8,128)(2,1)S(1)} %project.1.part.after), channel_id=1, source_target_pairs={{0,64},{64,0},{1,65},{65,1},{2,66},{66,2},{3,67},{67,3},{4,68},{68... | collective-permute-start | bytes 147464 | tf_op jit(solution)/shard_map/ppermute | solution.py:343
  20.1 18.1 %collective-permute-start.1 = (bf16[128,1536]{1,0:T(8,128)(2,1)S(1)}, bf16[128,1536]{1,0:T(8,128)(2,1)S(1)}, u32[]{:S(2)}, u32[]{:S(2)}) collective-permute-start(bf16[128,1536]{1,0:T(8,128)(2,1)S(1)} %get-tuple-element.16), channel_id=1, source_target_pairs={{0,1},{1,0},{2,3},{3,2},{4,5},{5,4},{6,7},{7,6},{8,9},{9,8},{10,11... | collective-permute-start | bytes 1179656 | tf_op jit(solution)/shard_map/ppermute | solution.py:345
  22.0 16.1 %collective-permute-start.2 = (bf16[128,1408]{1,0:T(8,128)(2,1)S(1)}, bf16[128,1408]{1,0:T(8,128)(2,1)S(1)}, u32[]{:S(2)}, u32[]{:S(2)}) collective-permute-start(bf16[128,1408]{1,0:T(8,128)(2,1)S(1)} %get-tuple-element.17), channel_id=1, source_target_pairs={{0,1},{1,0},{2,3},{3,2},{4,5},{5,4},{6,7},{7,6},{8,9},{9,8},{10,11... | collective-permute-start | bytes 1081352 | tf_op jit(solution)/shard_map/ppermute | solution.py:346
